TPU v7x, 256 devices: a whole 4x4x8 slice. The times are simulated.
256 devices in a mesh: ctx: 32 (over y, x, core), tp: 8 (over z).
Axes of the slice: x: 4, y: 4, z: 8, core: 2. Of those that a mesh axis runs over, the one named last changes fastest.
Arguments:
- value: bfloat16 [8192, 8192], P('ctx', 'tp'), may hold values from -6 to 6
- gate_q1: bfloat16 [8192, 8192], P('ctx', 'tp'), may hold values from -6 to 6
- gate_k1: bfloat16 [8192, 8192], P('ctx', 'tp'), may hold values from -6 to 6
- gate_q2: bfloat16 [8192, 8192], P('ctx', 'tp'), may hold values from -6 to 6
- gate_k2: bfloat16 [8192, 8192], P('ctx', 'tp'), may hold values from -6 to 6
- gate_q3: bfloat16 [8192, 8192], P('ctx', 'tp'), may hold values from -6 to 6
- gate_k3: bfloat16 [8192, 8192], P('ctx', 'tp'), may hold values from -6 to 6
- grad_out: bfloat16 [8192, 8192], P('ctx', 'tp'), may hold values from -6 to 6
- short_filter: bfloat16 [7, 8192], P(None, 'tp'), may hold values from -2 to 2
- medium_filter: bfloat16 [128, 512], replicated, may hold values from -0.5 to 0.5
- residues: float32 [16, 512], replicated, may hold values from -1.5 to 1.5
- rates: float32 [16, 512], replicated, may hold values from 3e-05 to 0.05
Outputs:
- mixed: bfloat16 [8192, 8192], P('ctx', 'tp')
- grad_value: bfloat16 [8192, 8192], P('ctx', 'tp')
- grad_q1: bfloat16 [8192, 8192], P('ctx', 'tp')
- grad_k1: bfloat16 [8192, 8192], P('ctx', 'tp')
- grad_q2: bfloat16 [8192, 8192], P('ctx', 'tp')
- grad_k2: bfloat16 [8192, 8192], P('ctx', 'tp')
- grad_q3: bfloat16 [8192, 8192], P('ctx', 'tp')
- grad_k3: bfloat16 [8192, 8192], P('ctx', 'tp')
- grad_short: float32 [7, 8192], P(None, 'tp')
- grad_medium: float32 [128, 512], replicated
All inputs are finite; a program needn't handle non-finite values.
Results may differ from a plain program's by a relative error of at most 0.02.
Values may be sent and summed in bfloat16 or wider, within the bound.
No kernel may reach another device: no remote copies, remote signals or barrier semaphores. Data moves between devices by JAX's collectives and lax.ppermute only.
A program may use at most 128 MiB of HBM per device.

v0:
```python
import math

import jax
import jax.numpy as jnp
from jax import lax
from jax.sharding import PartitionSpec as P


def carried_in(part, axis, combine, identity, reverse):
    count = lax.axis_size(axis)
    place = lax.axis_index(axis)
    ahead = count - 1 - place if reverse else place
    gathered = jax.tree.map(lambda a: lax.all_gather(a, axis), part)
    state = jax.tree.map(lambda a, e: jnp.zeros_like(a) + jnp.asarray(e, a.dtype), part, identity)

    def one(turn, state):
        source = count - 1 - turn if reverse else turn
        return combine(
            state, jax.tree.map(lambda a: lax.dynamic_index_in_dim(a, source, 0, False), gathered)
        )

    return lax.fori_loop(0, ahead, one, state)


def shifted(block, axis, distance):
    devices = range(lax.axis_size(axis))
    route = [(i - distance, i) for i in devices if i - distance in devices]
    return lax.ppermute(block, axis, route)


def causal_taps(extended, filt, count):
    taps = filt.shape[0]
    total = jnp.zeros((count, extended.shape[1]), jnp.float32)
    for lag in range(taps):
        start = taps - 1 - lag
        total = (
            total
            + extended[start : start + count].astype(jnp.float32)
            * filt[lag].astype(jnp.float32)[None, :]
        )
    return total


def adjoint_taps(extended, filt, count):
    taps = filt.shape[0]
    total = jnp.zeros((count, extended.shape[1]), jnp.float32)
    for lag in range(taps):
        total = (
            total
            + extended[lag : lag + count].astype(jnp.float32)
            * filt[lag].astype(jnp.float32)[None, :]
        )
    return total


def lag_sums(grads, extended, taps, count):
    terms = []
    for lag in range(taps):
        start = taps - 1 - lag
        terms.append(
            jnp.sum(
                grads.astype(jnp.float32) * extended[start : start + count].astype(jnp.float32),
                axis=0,
            )
        )
    return jnp.stack(terms)


def make_tables(count):
    size = 2 * count
    freq = jnp.arange(count + 1)
    times = jnp.arange(size)
    phase = (freq[:, None] * times[None, :] % size).astype(jnp.float32) * (2.0 * math.pi / size)
    cosine = jnp.cos(phase)
    sine = jnp.sin(phase)
    weights = jnp.where((freq == 0) | (freq == count), 1.0, 2.0).astype(jnp.float32)[:, None] / size
    return (cosine, sine, weights)


def spectra(tables, signal):
    cosine, sine, weights = tables
    length = signal.shape[0]
    highest = lax.Precision.HIGHEST
    real_part = jnp.dot(cosine[:, :length], signal, precision=highest)
    imag_part = -jnp.dot(sine[:, :length], signal, precision=highest)
    return (real_part, imag_part)


def inverse(tables, real_part, imag_part, start, rows):
    cosine, sine, weights = tables
    highest = lax.Precision.HIGHEST
    dims = (((0,), (0,)), ((), ()))
    first = lax.dot_general(
        cosine[:, start : start + rows], real_part * weights, dims, precision=highest
    )
    second = lax.dot_general(
        sine[:, start : start + rows], imag_part * weights, dims, precision=highest
    )
    return first - second


def times_spec(left, right):
    return (left[0] * right[0] - left[1] * right[1], left[0] * right[1] + left[1] * right[0])


def conj_times(left, right):
    return (left[0] * right[0] + left[1] * right[1], left[0] * right[1] - left[1] * right[0])


def widen(spec, copies):
    return (jnp.tile(spec[0], (1, copies)), jnp.tile(spec[1], (1, copies)))


def combine_states(earlier, later):
    return (earlier[0] * later[0], earlier[1] * later[0] + later[1])


def modal_conv(signal, tables, long_spec, residues, rates, reverse):
    highest = lax.Precision.HIGHEST
    f32 = jnp.float32
    if reverse:
        signal = signal[::-1]
    count, width = signal.shape
    modes, groups = rates.shape
    copies = width // groups
    weight_g = residues * jnp.sqrt(2.0 * rates)
    decay = jnp.tile(rates, (1, copies))
    steps_n = jnp.arange(count).astype(f32)
    signal = signal.astype(f32)
    product = times_spec(spectra(tables, signal), long_spec)
    local = inverse(tables, product[0], product[1], 0, count).reshape(count, copies, groups)
    shaped = signal.reshape(count, copies, groups)
    ending = jnp.exp(-rates[:, None, :] * (float(count - 1) - steps_n)[None, :, None])
    carry = jnp.einsum("msg,skg->mkg", ending, shaped, precision=highest).reshape(modes, width)
    whole_decay = jnp.exp(-decay * count)
    incoming = carried_in(
        (whole_decay, carry),
        "ctx",
        combine_states,
        (jnp.ones_like(carry), jnp.zeros_like(carry)),
        reverse,
    )[1]
    reach = jnp.exp(-rates[None] * (steps_n + 1.0)[:, None, None]) * weight_g[None]
    far = jnp.einsum(
        "tmg,mkg->tkg", reach, incoming.reshape(modes, copies, groups), precision=highest
    )
    result = (local + far).reshape(count, width)
    if reverse:
        result = result[::-1]
    return result


def on_device(
    value,
    gate_q1,
    gate_k1,
    gate_q2,
    gate_k2,
    gate_q3,
    gate_k3,
    grad_out,
    short_filter,
    medium_filter,
    residues,
    rates,
):
    f32 = jnp.float32
    bf = jnp.bfloat16
    count, width = value.shape
    short_taps = short_filter.shape[0]
    medium_taps = medium_filter.shape[0]
    modes, groups = rates.shape
    copies = width // groups
    tables = make_tables(count)
    medium_spec = widen(spectra(tables, medium_filter.astype(f32)), copies)
    weight_g = residues * jnp.sqrt(2.0 * rates)
    steps_n = jnp.arange(count).astype(f32)
    filt_local = jnp.zeros((count, groups), f32)
    for mode in range(modes):
        filt_local = filt_local + weight_g[mode][None, :] * jnp.exp(
            -rates[mode][None, :] * steps_n[:, None]
        )
    long_spec = widen(spectra(tables, filt_local), copies)

    def mul(left, right):
        return left.astype(f32) * right.astype(f32)

    u1 = mul(gate_k1, value).astype(bf)
    rim_one = shifted(u1[count - (short_taps - 1) :], "ctx", 1)
    ext_one = jnp.concatenate([rim_one, u1], axis=0)
    z1 = causal_taps(ext_one, short_filter, count)
    x1 = mul(gate_q1, z1).astype(bf)
    u2 = mul(gate_k2, x1).astype(bf)
    rim_two = shifted(u2[count - (medium_taps - 1) :], "ctx", 1)
    ext_two = jnp.concatenate([rim_two, u2], axis=0)
    ext_spec = spectra(tables, ext_two.astype(f32))
    forward_spec = times_spec(ext_spec, medium_spec)
    z2 = inverse(tables, forward_spec[0], forward_spec[1], medium_taps - 1, count)
    x2 = mul(gate_q2, z2).astype(bf)
    u3 = mul(gate_k3, x2).astype(bf)
    z3 = modal_conv(u3, tables, long_spec, residues, rates, False)
    mixed = mul(gate_q3, z3).astype(bf)
    grad_q3 = mul(grad_out, z3).astype(bf)
    dz3 = mul(grad_out, gate_q3)
    du3 = modal_conv(dz3, tables, long_spec, residues, rates, True)
    grad_k3 = mul(du3, x2).astype(bf)
    dx2 = mul(du3, gate_k3).astype(bf)
    grad_q2 = mul(dx2, z2).astype(bf)
    dz2 = mul(dx2, gate_q2).astype(bf)
    rim_back_two = shifted(dz2[: medium_taps - 1], "ctx", -1)
    back_spec = conj_times(
        medium_spec, spectra(tables, jnp.concatenate([dz2, rim_back_two], axis=0).astype(f32))
    )
    du2 = inverse(tables, back_spec[0], back_spec[1], 0, count)
    grad_k2 = mul(du2, x1).astype(bf)
    dx1 = mul(du2, gate_k2).astype(bf)
    grad_q1 = mul(dx1, z1).astype(bf)
    dz1 = mul(dx1, gate_q1).astype(bf)
    rim_back_one = shifted(dz1[: short_taps - 1], "ctx", -1)
    du1 = adjoint_taps(jnp.concatenate([dz1, rim_back_one], axis=0), short_filter, count)
    grad_k1 = mul(du1, value).astype(bf)
    grad_value = mul(du1, gate_k1).astype(bf)
    short_terms = lag_sums(dz1, ext_one, short_taps, count)
    cross = conj_times(spectra(tables, dz2.astype(f32)), ext_spec)
    half = cross[0].shape[0]
    cross_real = jnp.sum(cross[0].reshape(half, copies, groups), axis=1)
    cross_imag = jnp.sum(cross[1].reshape(half, copies, groups), axis=1)
    medium_terms = inverse(tables, cross_real, cross_imag, 0, medium_taps)[::-1]
    grad_short = lax.psum(short_terms, "ctx")
    grad_medium = lax.psum(medium_terms, ("ctx", "tp"))
    return (
        mixed,
        grad_value,
        grad_q1,
        grad_k1,
        grad_q2,
        grad_k2,
        grad_q3,
        grad_k3,
        grad_short,
        grad_medium,
    )


def solution(mesh):
    in_specs = (
        P("ctx", "tp"),
        P("ctx", "tp"),
        P("ctx", "tp"),
        P("ctx", "tp"),
        P("ctx", "tp"),
        P("ctx", "tp"),
        P("ctx", "tp"),
        P("ctx", "tp"),
        P(None, "tp"),
        P(),
        P(),
        P(),
    )
    out_specs = (
        P("ctx", "tp"),
        P("ctx", "tp"),
        P("ctx", "tp"),
        P("ctx", "tp"),
        P("ctx", "tp"),
        P("ctx", "tp"),
        P("ctx", "tp"),
        P("ctx", "tp"),
        P(None, "tp"),
        P(),
    )
    return jax.shard_map(
        on_device, mesh=mesh, in_specs=in_specs, out_specs=out_specs, check_vma=False
    )
```

profile of v0, /device:TPU:1, one launch (start us, length us, event | category | flops | bytes accessed | tf_op | source)
XLA Modules:
  0.0 647.6 jit_solution(10763751259414295482)
XLA Ops:
  7.3 1.3 copy.82
  10.3 1.4 rev.9
  12.9 8.0 %fusion.15 = f32[16,2,512]{0,1,2:T(2,128)S(1)} fusion(f32[256]{0:T(256)S(1)} %fusion.157, f32[16,512]{0,1:T(8,128)S(1)} %copy.84, f32[256,2,512]{0,2,1:T(8,128)S(1)} %bitcast.120), kind=kOutput, calls=%fused_computation.73 | convolution fusion | flops 52428800 | bytes 1147904 | tf_op jit(solution)/shard_map/msg,skg->mkg/dot_general | solution.py:134
  23.6 4.7 collective-permute-start
  29.2 2.0 fusion.130
  31.3 2.1 fusion.146
  34.3 2.0 fusion.129
  36.3 2.1 convolution_negate_fusion.3
  39.3 1.0 copy-done.5
  40.3 1.1 convolution_negate_fusion.1
  41.4 1.5 fusion.143
  42.9 2.1 fusion.29
  45.0 3.1 convolution_subtract_fusion.1
  48.1 2.6 copy.94
  50.7 2.5 copy.99
  54.4 1.2 copy.104
  56.7 1.2 copy.105
  57.9 17.1 %all-gather.8.cloned.1.call-done = f32[32,16,1024]{2,1,0:T(8,128)} async-done(((f32[1,16,1024]{2,1,0:T(8,128)}), f32[32,16,1024]{2,1,0:T(8,128)}) %all-gather.8.cloned.1.call-update) | async-done | bytes 2097168 | tf_op jit(solution)/shard_map/all_gather | solution.py:13
  75.0 51.3 %all-gather.4.cloned.1.call-done = f32[32,16,1024]{2,1,0:T(8,128)} async-done(((f32[1,16,1024]{2,1,0:T(8,128)}), f32[32,16,1024]{2,1,0:T(8,128)}) %all-gather.4.cloned.1.call-update) | async-done | bytes 2097168 | tf_op jit(solution)/shard_map/all_gather | solution.py:13
  126.3 27.9 %while.27 = (s32[]{:T(128)}, f32[16,1024]{1,0:T(8,128)S(1)}, s32[]{:T(128)}, f32[32,16,1024]{2,1,0:T(8,128)}, f32[32,16,1024]{2,1,0:T(8,128)}, /*index=5*/s32[]{:T(128)}, s32[]{:T(128)}, s32[]{:T(128)}, s32[]{:T(128)}) while((s32[]{:T(128)}, f32[16,1024]{1,0:T(8,128)S(1)}, s32[]{:T(128)}, f32[32,16,1024]{2,1,0:T(8,128)}, ...), condition=%wide.region_3.4_spmd, body=%wide.region_2.3_spmd.sunk | while | flops 32774 | bytes 262287 | solution.py:22
  154.3 1.0 copy.97
  155.3 8.0 %fusion = f32[512,2,256]{2,1,0:T(2,128)} fusion(f32[16,2,512]{0,1,2:T(2,128)} %copy.97, f32[16,512]{0,1:T(8,128)} %copy.88, f32[256]{0:T(256)S(1)} %fusion.156, f32[16,512]{0,1:T(8,128)} %copy-done.23), kind=kOutput, calls=%fused_computation.5 | convolution fusion | flops 54525952 | bytes 1180672 | tf_op jit(solution)/shard_map/tmg,mkg->tkg/dot_general | solution.py:144
  163.3 2.3 copy.98
  165.6 2.7 bitcast_add_fusion.2
  168.3 2.6 copy.100
  170.8 2.5 copy.101
  173.4 8.9 %rev.10 = f32[256,1024]{1,0:T(8,128)} reverse(f32[256,1024]{1,0:T(8,128)} %copy.101), dimensions={0} | reverse | bytes 2097152 | tf_op jit(solution)/shard_map/rev | solution.py:149
  182.3 1.8 fusion.71
  184.1 3.3 collective-permute-start.2
  187.9 3.8 collective-permute-done.2
  191.8 1.0 fusion.118
  192.8 1.0 convolution_negate_fusion
  194.3 2.1 fusion.20
  196.4 3.8 fusion.67
  200.3 2.1 fusion.87
  202.5 2.1 collective-permute-start.1
  205.2 2.5 collective-permute-done.1
  207.7 1.0 fusion.119
  208.7 2.7 multiply_subtract_fusion
  211.4 2.2 fusion.47
  213.6 3.7 fusion.69
  217.3 2.2 reshape.122
  219.5 3.5 copy.85
  223.0 6.7 %fusion.14 = f32[16,2,512]{0,1,2:T(2,128)} fusion(bf16[256,2,512]{0,1,2:T(2,128)(2,1)} %copy.85, f32[256]{0:T(256)S(1)} %fusion.157, f32[16,512]{0,1:T(8,128)} %copy-done.23), kind=kOutput, calls=%fused_computation.72 | convolution fusion | flops 52428800 | bytes 623616 | tf_op jit(solution)/shard_map/msg,skg->mkg/dot_general | solution.py:134
  229.7 1.2 copy.86
  232.4 1.9 collective-permute-start.3
  234.4 118.9 %psum.14 = f32[7,1024]{1,0:T(8,128)} all-reduce(f32[7,1024]{1,0:T(8,128)S(1)} %stack.31), channel_id=1, replica_groups=mesh['ctx'=32,'tp'=8] {'ctx'}, use_global_device_ids=true, to_apply=%region_11.12 | all-reduce | flops 7168 | bytes 57344 | tf_op jit(solution)/shard_map/psum | solution.py:229
  353.3 5.2 fusion.59
  359.5 3.1 reshape.129
  362.6 3.1 reshape.130
  365.7 3.3 reduce_sum.88
  369.0 3.3 reduce_sum.89
  372.3 1.9 fusion.95
  374.1 1.5 convolution_subtract_fusion.4
  375.6 3.2 rev.11
  378.9 1.7 fusion.148
  381.2 2.1 fusion.38
  383.3 3.2 convolution_subtract_fusion.2
  386.5 1.6 copy.83
  389.8 7.0 %fusion.1 = f32[512,2,256]{2,1,0:T(2,128)S(1)} fusion(f32[16,2,512]{0,1,2:T(2,128)S(1)} %copy.89, f32[16,512]{0,1:T(8,128)S(1)} %copy-done.25, f32[256]{0:T(256)S(1)} %fusion.156, f32[16,512]{0,1:T(8,128)S(1)} %copy-done.24), kind=kOutput, calls=%fused_computation.6 | convolution fusion | flops 54525952 | bytes 1180672 | tf_op jit(solution)/shard_map/tmg,mkg->tkg/dot_general | solution.py:144
  399.2 1.0 copy.102
  400.2 1.0 copy.103
  401.2 237.6 %all-reduce.2.cloned.1.call-done = f32[128,512]{1,0:T(8,128)} async-done(((f32[128,512]{1,0:T(8,128)}), f32[128,512]{1,0:T(8,128)}) %all-reduce.2.cloned.1.call-update) | async-done | bytes 262160 | tf_op jit(solution)/shard_map/psum | solution.py:230
  638.9 1.7 copy.129
  (149 shorter events, 47.7 us)
Async XLA Ops:
  7.2 46.1 %copy-start = (bf16[128,512]{1,0:T(8,128)(2,1)S(1)}, bf16[128,512]{1,0:T(8,128)(2,1)}, u32[]{:S(2)}) copy-start(bf16[128,512]{1,0:T(8,128)(2,1)} %param.25) | copy-start | bytes 393220
  7.2 1.4 copy-start.22
  7.2 67.8 %all-gather.8.cloned.1.call-start = ((), (), s32[]{:S(2)}) async-start(), calls=%async_computation.2 | async-start | bytes 2162688 | tf_op jit(solution)/shard_map/all_gather | solution.py:13
  8.6 0.8 copy-start.8
  9.4 0.8 copy-start.10
  10.3 1.5 copy-start.26
  10.3 1.5 copy-start.28
  11.8 9.1 %copy-start.4 = (f32[256,1024]{0,1:T(8,128)}, f32[256,1024]{0,1:T(8,128)S(1)}, u32[]{:S(2)}) copy-start(f32[256,1024]{0,1:T(8,128)S(1)} %rev.9) | copy-start | bytes 3145732
  12.0 0.9 copy-start.23
  20.9 1.8 copy-start.17
  20.9 1.8 copy-start.18
  21.8 104.5 %all-gather.4.cloned.1.call-start = ((), (), s32[]{:S(2)}) async-start(), calls=%async_computation | async-start | bytes 2162688 | tf_op jit(solution)/shard_map/all_gather | solution.py:13
  22.6 365.8 %all-gather.6.cloned.1.call-start = ((), (), s32[]{:S(2)}) async-start(), calls=%async_computation.1 | async-start | bytes 2162688 | tf_op jit(solution)/shard_map/all_gather | solution.py:13
  22.8 0.8 copy-start.12
  23.6 172.8 %collective-permute-start = (bf16[6,1024]{1,0:T(8,128)(2,1)S(1)}, bf16[6,1024]{1,0:T(8,128)(2,1)S(1)}, u32[]{:S(2)}, u32[]{:S(2)}) collective-permute-start(bf16[6,1024]{1,0:T(8,128)(2,1)S(1)} %slice.316), channel_id=1, source_target_pairs={{0,8},{8,16},{16,24},{24,32},{32,40},{40,48},{48,56},{56,64},{64,7... | collective-permute-start | bytes 36872 | tf_op jit(solution)/shard_map/ppermute | solution.py:28
  39.1 1.2 copy-start.5
  56.7 1.2 copy-start.27
  184.1 7.7 %collective-permute-start.2 = (bf16[127,1024]{1,0:T(8,128)(2,1)S(1)}, bf16[127,1024]{1,0:T(8,128)(2,1)S(1)}, u32[]{:S(2)}, u32[]{:S(2)}) collective-permute-start(bf16[127,1024]{1,0:T(8,128)(2,1)S(1)} %slice.349), channel_id=1, source_target_pairs={{8,0},{16,8},{24,16},{32,24},{40,32},{48,40},{56,48},{64,56},{72,6... | collective-permute-start | bytes 780296 | tf_op jit(solution)/shard_map/ppermute | solution.py:28
  192.8 1.2 copy-start.2
  192.8 1.6 copy-start.3
  194.3 2.1 copy-start.13
  194.3 2.1 copy-start.20
  196.4 3.8 copy-start.21
  202.5 5.2 collective-permute-start.1
  211.4 2.2 copy-start.6
  211.4 2.2 copy-start.15
  211.4 2.2 copy-start.16
  231.6 407.2 %all-reduce.2.cloned.1.call-start = ((), (), s32[]{:S(2)}) async-start(), calls=%async_computation.3 | async-start | bytes 524288 | tf_op jit(solution)/shard_map/psum | solution.py:230
  232.4 120.9 %collective-permute-start.3 = (bf16[6,1024]{1,0:T(8,128)(2,1)S(1)}, bf16[6,1024]{1,0:T(8,128)(2,1)S(1)}, u32[]{:S(2)}, u32[]{:S(2)}) collective-permute-start(bf16[6,1024]{1,0:T(8,128)(2,1)S(1)} %slice.350), channel_id=1, source_target_pairs={{8,0},{16,8},{24,16},{32,24},{40,32},{48,40},{56,48},{64,56},{72,6... | collective-permute-start | bytes 36872 | tf_op jit(solution)/shard_map/ppermute | solution.py:28
  353.3 5.2 copy-start.19
  372.2 1.9 copy-start.14
  378.9 1.7 copy-start.7
  388.4 1.3 copy-start.24
  388.4 1.3 copy-start.25
  397.8 1.0 copy-start.9
  397.8 1.2 copy-start.11
  399.2 241.3 %copy-start.1 = (bf16[128,512]{1,0:T(8,128)(2,1)S(1)}, bf16[128,512]{1,0:T(8,128)(2,1)}, u32[]{:S(2)}) copy-start(bf16[128,512]{1,0:T(8,128)(2,1)} %param.25) | copy-start | bytes 393220
Sparse Core Ops, SparseCore 0:
  21.9 53.0 all-gather.7
  78.1 48.1 all-gather.3
  231.8 47.3 all-gather.5
  388.5 250.3 all-reduce.1
where the time goes:
time: 658 us; the launch traced here: 648 us
  waiting for transfers between devices  312 us (47%)
  blocking collectives  119 us (18%)
  matrix products  72 us (11%)
  local copies, waits for them, and re-layouts  64.2 us (10%)
  other arithmetic  52.2 us (8%)
  between operations  15.1 us (2%)
  starting transfers between devices  12.2 us (2%)
    psum x1, waiting for transfers between devices, on_device(): grad_medium = lax.psum(medium_terms, ('ctx', 'tp'))  238 us
    psum x1, blocking collectives, on_device(): grad_short = lax.psum(short_terms, 'ctx')  119 us
    all_gather x3, waiting for transfers between devices, carried_in(): gathered = jax.tree.map(lambda a: lax.all_gather(a, axis), part)  68.4 us
    add x31, other arithmetic, combine_states(): return (earlier[0] * later[0], earlier[1] * later[0] + later[1])  28.1 us
    dot_general x5, matrix products, inverse(): lax.dot_general(sine[:, start:start + rows], imag_part * weights, dims, p...  15.3 us
    unnamed x71, local copies, waits for them, and re-layouts  15 us
    dot_general x2, matrix products, modal_conv(): jnp.einsum('tmg,mkg->tkg', reach, incoming.reshape(modes, copies, groups)...  15 us
    dot_general x2, matrix products, modal_conv(): jnp.einsum('msg,skg->mkg', ending, shaped, precision=highest)  14.7 us
  transfers between devices with their start and end apart: 8, of which 5 were waited for; matrix products, arithmetic and copies ran while one was open for 21% of the time, Pallas kernels for 0%

commit v1 on v0

v1 whole, which is shorter than its diff:
```python
import functools

import jax
import jax.numpy as jnp
import numpy as np
from jax import lax
from jax.experimental import pallas as pl
from jax.experimental.pallas import tpu as pltpu
from jax.sharding import PartitionSpec as P

F32 = jnp.float32
BF = jnp.bfloat16
LANES = 128
VMEM_LIMIT = 40 * 1024 * 1024


def dft_tables(count):
    size = 2 * count
    freq = np.arange(count)[:, None].astype(np.int64)

    def waves(times):
        phase = (freq * times[None, :]) % size * (2.0 * np.pi / size)
        cosine, sine = np.cos(phase), -np.sin(phase)
        sine[0] = np.where(times % 2 == 0, 1.0, -1.0)
        return np.concatenate([cosine, sine], axis=0)

    forward = waves(np.arange(size))
    scale = np.full((size, 1), 2.0 / size)
    scale[0] = scale[count] = 1.0 / size
    backward = (forward * scale).T
    return forward, backward


def dot(a, b):
    return jnp.dot(a, b, preferred_element_type=F32)


def spec_mul(spec, filt):
    half = spec.shape[0] // 2
    re, im = spec[:half], spec[half:]
    a, b, c = filt
    return jnp.concatenate([(re * a - im * b).astype(BF), (re * b + im * c).astype(BF)], axis=0)


def spec_conj(spec, filt):
    half = spec.shape[0] // 2
    re, im = spec[:half], spec[half:]
    a, b, c = filt
    return jnp.concatenate([(re * a + im * b).astype(BF), (im * c - re * b).astype(BF)], axis=0)


def row_index(shape):
    return lax.broadcasted_iota(jnp.int32, shape, 0)


def end_states(signal_ref, rates_ref, out_ref, reverse):
    count, width = signal_ref.shape
    modes = rates_ref.shape[0]
    tiles = count // 8
    for group in range(width // LANES):
        lanes = slice(group * LANES, (group + 1) * LANES)
        rates = rates_ref[:, lanes]
        step = jnp.exp(-8.0 * rates)
        steps = [jnp.broadcast_to(step[m : m + 1], (8, LANES)) for m in range(modes)]

        def body(j, sums, lanes=lanes, steps=steps):
            tile = tiles - 1 - j if reverse else j
            u = signal_ref[pl.ds(pl.multiple_of(tile * 8, 8), 8), lanes]
            return tuple(s * a + u for s, a in zip(sums, steps))

        zero = jnp.zeros((8, LANES), F32)
        sums = lax.fori_loop(0, tiles, body, (zero,) * modes, unroll=4)
        sub = row_index((8, LANES)).astype(F32)
        ages = sub if reverse else 7.0 - sub
        rows = [
            jnp.sum(s * jnp.exp(-rates[m : m + 1] * ages), axis=0, keepdims=True)
            for m, s in enumerate(sums)
        ]
        out_ref[:, lanes] = jnp.concatenate(rows, axis=0)


def far_field(states, rates_ref, weights_ref, out_ref, reverse, first, lanes):
    count = out_ref.shape[0]
    modes = rates_ref.shape[0]
    tiles = count // 8
    rates = rates_ref[:, lanes]
    weights = weights_ref[:, lanes] * jnp.sqrt(2.0 * rates)
    if states is not None:
        weights = weights * states
    step = jnp.exp(-8.0 * rates)
    steps = [jnp.broadcast_to(step[m : m + 1], (8, LANES)) for m in range(modes)]
    sub = row_index((8, LANES)).astype(F32)
    ages = (7.0 - sub if reverse else sub) + float(first)
    terms = tuple(weights[m : m + 1] * jnp.exp(-rates[m : m + 1] * ages) for m in range(modes))

    def body(j, terms):
        tile = tiles - 1 - j if reverse else j
        level = list(terms)
        while len(level) > 1:
            level = [level[i] + level[i + 1] for i in range(0, len(level), 2)]
        out_ref[pl.ds(pl.multiple_of(tile * 8, 8), 8), lanes] = level[0]
        return tuple(s * a for s, a in zip(terms, steps))

    lax.fori_loop(0, tiles, body, terms, unroll=4)


def add_far(state_ref, rates_ref, weights_ref, out_ref, reverse):
    for group in range(out_ref.shape[1] // LANES):
        lanes = slice(group * LANES, (group + 1) * LANES)
        far_field(state_ref[:, lanes], rates_ref, weights_ref, out_ref, reverse, 1, lanes)


def mul(a, b):
    return a.astype(F32) * b.astype(F32)


def back_carry_kernel(grad_ref, gate_ref, rates_ref, out_ref, signal):
    signal[...] = mul(grad_ref[...], gate_ref[...])
    end_states(signal, rates_ref, out_ref, True)


def short_causal(ext, filt_ref, rows, start):
    total = None
    for lag in range(filt_ref.shape[0]):
        term = ext[pl.ds(start - lag, rows), :] * filt_ref[lag : lag + 1, :].astype(F32)
        total = term if total is None else total + term
    return total


def fore_rim_kernel(value_ref, k1_ref, q1_ref, k2_ref, filt_ref, out_ref, ext):
    count = value_ref.shape[0]
    rim = q1_ref.shape[0]
    u1 = mul(k1_ref[...], value_ref[...]).astype(BF)
    ext[...] = u1.astype(F32)
    z1 = short_causal(ext, filt_ref, rim, count - rim)
    x1 = mul(q1_ref[...], z1).astype(BF)
    out_ref[0:rim, :] = mul(k2_ref[...], x1).astype(BF)
    out_ref[rim : rim + 16, :] = u1[count - 16 :]


def filters_kernel(table_ref, medium_ref, residues_ref, rates_ref, ma, mb, mc, la, lb, lc, local):
    highest = lax.Precision.HIGHEST
    count = local.shape[0]
    taps = medium_ref.shape[0]
    for group in range(local.shape[1] // LANES):
        lanes = slice(group * LANES, (group + 1) * LANES)
        far_field(None, rates_ref, residues_ref, local, False, 0, lanes)
    table = table_ref[...]
    for filt, (a, b, c) in (
        (medium_ref[...].astype(F32), (ma, mb, mc)),
        (local[...], (la, lb, lc)),
    ):
        spec = jnp.dot(
            table[:, : filt.shape[0]], filt, precision=highest, preferred_element_type=F32
        )
        re, im = spec[:count], spec[count:]
        edge = row_index(re.shape) == 0
        a[...] = re
        b[...] = jnp.where(edge, 0.0, im)
        c[...] = jnp.where(edge, im, re)


def fore_kernel(
    value_ref, k1_ref, q1_ref, k2_ref, q2_ref, k3_ref, rim_ref, filt_ref, rates_ref,
    fwd_ref, inv_ref, ma, mb, mc,
    z1_ref, x1_ref, u2_ref, z2_ref, x2_ref, u3_ref, carry_ref, ext,
):
    count = value_ref.shape[0]
    rim = rim_ref.shape[0] - 16
    u1 = mul(k1_ref[...], value_ref[...]).astype(BF)
    ext[0:16, :] = rim_ref[rim : rim + 16, :].astype(F32)
    ext[16:, :] = u1.astype(F32)
    z1 = short_causal(ext, filt_ref, count, 16)
    z1_ref[...] = z1.astype(BF)
    x1 = mul(q1_ref[...], z1).astype(BF)
    x1_ref[...] = x1
    u2 = mul(k2_ref[...], x1).astype(BF)
    u2_ref[...] = u2
    spec = dot(fwd_ref[:, :count], u2) + dot(fwd_ref[:, 2 * count - rim :], rim_ref[0:rim, :])
    z2 = dot(inv_ref[...], spec_mul(spec, (ma[...], mb[...], mc[...])))
    z2_ref[...] = z2.astype(BF)
    x2 = mul(q2_ref[...], z2).astype(BF)
    x2_ref[...] = x2
    u3 = mul(k3_ref[...], x2).astype(BF)
    u3_ref[...] = u3
    ext[0:count, :] = u3.astype(F32)
    end_states(ext.at[0:count, :], rates_ref, carry_ref, False)


def back_local_kernel(grad_ref, gate_ref, fwd_ref, inv_ref, la, lb, lc, out_ref):
    count = grad_ref.shape[0]
    spec = dot(fwd_ref[:, :count], mul(grad_ref[...], gate_ref[...]).astype(BF))
    out_ref[...] = dot(inv_ref[...], spec_conj(spec, (la[...], lb[...], lc[...])))


def back_long_kernel(
    near_ref, state_ref, rates_ref, residues_ref, x2_ref, z2_ref, k3_ref, q2_ref, k2_ref, q1_ref,
    fwd_ref, inv_ref, ma, mb, mc,
    gk3_ref, gq2_ref, dz2_ref, du2_ref, rim_ref, far,
):
    count = near_ref.shape[0]
    rim = rim_ref.shape[0] - 16
    add_far(state_ref, rates_ref, residues_ref, far, True)
    du3 = near_ref[...] + far[...]
    gk3_ref[...] = mul(du3, x2_ref[...]).astype(BF)
    dx2 = mul(du3, k3_ref[...]).astype(BF)
    gq2_ref[...] = mul(dx2, z2_ref[...]).astype(BF)
    dz2 = mul(dx2, q2_ref[...]).astype(BF)
    dz2_ref[...] = dz2
    spec = dot(fwd_ref[:, :count], dz2)
    du2 = dot(inv_ref[...], spec_conj(spec, (ma[...], mb[...], mc[...])))
    du2_ref[...] = du2
    rim_ref[0:rim, :] = dz2[0:rim]
    dx1 = mul(du2[0:16], k2_ref[0:16, :]).astype(BF)
    rim_ref[rim : rim + 16, :] = mul(dx1, q1_ref[0:16, :]).astype(BF)


def medium_terms_kernel(dz2_ref, u2_ref, rim_ref, fwd_ref, lag_ref, out_ref, total):
    count = dz2_ref.shape[0]
    rim = rim_ref.shape[0]
    step = pl.program_id(0)
    ext = dot(fwd_ref[:, :count], u2_ref[...]) + dot(fwd_ref[:, 2 * count - rim :], rim_ref[...])
    grad = dot(fwd_ref[:, :count], dz2_ref[...])
    er, ei, dr, di = ext[:count], ext[count:], grad[:count], grad[count:]
    edge = row_index(er.shape) == 0
    high = di * ei
    re = dr * er + jnp.where(edge, 0.0, high)
    im = jnp.where(edge, high, dr * ei - di * er)
    cross = jnp.concatenate([re, im], axis=0)

    @pl.when(step % 2 == 0)
    def _():
        total[...] = cross

    @pl.when(step % 2 == 1)
    def _():
        out_ref[...] = dot(lag_ref[...], (total[...] + cross).astype(BF))


def back_short_kernel(
    du2_ref, rim_ref, x1_ref, z1_ref, k2_ref, q1_ref, k1_ref, value_ref, fore_ref, filt_ref,
    terms_ref, fwd_ref, inv_ref, ma, mb, mc,
    gk2_ref, gq1_ref, gk1_ref, gv_ref, send_ref, ext, signal,
):
    count = du2_ref.shape[0]
    rim = rim_ref.shape[0] - 16
    taps = filt_ref.shape[0]
    step = pl.program_id(0)
    spec = dot(fwd_ref[:, count : count + rim], rim_ref[0:rim, :])
    du2 = du2_ref[...] + dot(inv_ref[...], spec_conj(spec, (ma[...], mb[...], mc[...])))
    gk2_ref[...] = mul(du2, x1_ref[...]).astype(BF)
    dx1 = mul(du2, k2_ref[...]).astype(BF)
    gq1_ref[...] = mul(dx1, z1_ref[...]).astype(BF)
    dz1 = mul(dx1, q1_ref[...]).astype(BF).astype(F32)
    ext[0:count, :] = dz1
    ext[count:, :] = rim_ref[rim : rim + 16, :].astype(F32)
    signal[0:16, :] = fore_ref[...].astype(F32)
    signal[16:, :] = mul(k1_ref[...], value_ref[...]).astype(BF).astype(F32)
    du1 = None
    for lag in range(taps):
        term = ext[pl.ds(lag, count), :] * filt_ref[lag : lag + 1, :].astype(F32)
        du1 = term if du1 is None else du1 + term
    gk1_ref[...] = mul(du1, value_ref[...]).astype(BF)
    gv_ref[...] = mul(du1, k1_ref[...]).astype(BF)

    pieces, width = send_ref.shape[0], du2_ref.shape[1]

    @pl.when(step == 0)
    def _():
        send_ref[...] = jnp.zeros_like(send_ref)
        share = terms_ref.shape[0] // pieces
        half = terms_ref.shape[1] // 2
        for piece in range(pieces):
            rows = terms_ref[piece * share : (piece + 1) * share, :]
            send_ref[piece, 0:share, 0:half] = rows[:, :half]
            send_ref[piece, share : 2 * share, 0:half] = rows[:, half:]

    block = (step % 2) * 2 + step // 2
    for lag in range(taps):
        row = jnp.sum(dz1 * signal[pl.ds(16 - lag, count), :], axis=0, keepdims=True)
        spot = lag * 4 + block
        send_ref[spot, 0:1, width : width + LANES] = row[:, :LANES]
        send_ref[spot, 1:2, width : width + LANES] = row[:, LANES:]


def fore_long_kernel(
    u3_ref, state_ref, rates_ref, residues_ref, q3_ref, grad_ref, fwd_ref, inv_ref, la, lb, lc,
    mixed_ref, gq3_ref, far,
):
    count = u3_ref.shape[0]
    add_far(state_ref, rates_ref, residues_ref, far, False)
    spec = dot(fwd_ref[:, :count], u3_ref[...])
    z3 = far[...] + dot(inv_ref[...], spec_mul(spec, (la[...], lb[...], lc[...])))
    mixed_ref[...] = mul(q3_ref[...], z3).astype(BF)
    gq3_ref[...] = mul(grad_ref[...], z3).astype(BF)


def swapped(block, distance):
    size = lax.axis_size("ctx")
    return lax.ppermute(block, "ctx", [(i, i ^ distance) for i in range(size)])


def shifted(block, distance):
    size = lax.axis_size("ctx")
    route = [(i, i + distance) for i in range(size) if 0 <= i + distance < size]
    return lax.ppermute(block, "ctx", route)


def scan_states(carry, rates, count, reverse):
    size = lax.axis_size("ctx")
    place = lax.axis_index("ctx")
    if reverse:
        place = size - 1 - place
    drop = rates * float(-count)

    def power(n):
        return jnp.exp(drop * n.astype(F32))

    total, prefix = carry, jnp.zeros_like(carry)
    group = 1
    for fan in (2, 4, 4):
        mine = (place // group) % fan
        offset = place % group
        others = [(d, swapped(total, d * group)) for d in range(1, fan)]
        if group * fan < size:
            new_total = total * power(group * (fan - 1 - mine))
        for d, other in others:
            theirs = mine ^ d
            before = theirs < mine
            gap = jnp.where(before, offset + group * (mine - 1 - theirs), 0)
            prefix = prefix + jnp.where(before, power(gap), 0.0) * other
            if group * fan < size:
                new_total = new_total + power(group * (fan - 1 - theirs)) * other
        if group * fan < size:
            total = new_total
        group *= fan
    return prefix


def on_device(
    value, gate_q1, gate_k1, gate_q2, gate_k2, gate_q3, gate_k3, grad_out,
    short_filter, medium_filter, residues, rates,
):
    count, width = value.shape
    modes, groups = rates.shape
    copies = width // groups
    taps, medium_taps = short_filter.shape[0], medium_filter.shape[0]
    cb = groups // 2
    steps = copies * 2
    rim = medium_taps
    forward, backward = dft_tables(count)
    fwd32 = jnp.asarray(forward[:, :count], F32)
    fwd = jnp.asarray(forward, BF)
    inv = jnp.asarray(backward[:count], BF)
    lag = jnp.asarray(backward[(-np.arange(medium_taps)) % (2 * count)], BF)

    def chan(i):
        return (i % copies) * 2 + i // copies

    def data(rows, at=0):
        return pl.BlockSpec((rows, cb), lambda i: (at, chan(i)))

    def filt(rows):
        return pl.BlockSpec((rows, cb), lambda i: (0, i // copies))

    def whole(shape):
        return pl.BlockSpec(shape, lambda i: (0,) * len(shape))

    def shape(rows, dtype=BF, cols=width):
        return jax.ShapeDtypeStruct((rows, cols), dtype)

    def call(kernel, name, in_specs, out_specs, out_shape, scratch=()):
        return pl.pallas_call(
            kernel,
            name=name,
            grid=(steps,),
            in_specs=in_specs,
            out_specs=out_specs,
            out_shape=out_shape,
            scratch_shapes=list(scratch),
            compiler_params=pltpu.CompilerParams(vmem_limit_bytes=VMEM_LIMIT),
        )

    table_specs = [whole(fwd.shape), whole(inv.shape)]
    spec3 = [filt(count)] * 3
    wide_rates = jnp.tile(rates, (1, copies))

    back_carry = call(
        back_carry_kernel, "back_carry", [data(count)] * 2 + [filt(modes)], data(modes),
        shape(modes, F32), [pltpu.VMEM((count, cb), F32)],
    )(grad_out, gate_q3, rates)
    back_state = scan_states(back_carry, wide_rates, count, True)

    rim_send = call(
        fore_rim_kernel, "fore_rim",
        [data(count)] * 2 + [data(rim, 1)] * 2 + [data(taps)],
        data(rim + 16), shape(rim + 16), [pltpu.VMEM((count, cb), F32)],
    )(value, gate_k1, gate_q1, gate_k2, short_filter)
    rim_fore = shifted(rim_send, 1)

    spectra = pl.pallas_call(
        filters_kernel,
        name="filters",
        out_shape=[shape(count, F32, groups)] * 6,
        scratch_shapes=[pltpu.VMEM((count, groups), F32)],
        compiler_params=pltpu.CompilerParams(vmem_limit_bytes=VMEM_LIMIT),
    )(fwd32, medium_filter, residues, rates)
    med, lng = spectra[:3], spectra[3:]

    du3_near = call(
        back_local_kernel, "back_local", [data(count)] * 2 + table_specs + spec3, data(count),
        shape(count, F32),
    )(grad_out, gate_q3, fwd, inv, *lng)

    z1, x1, u2, z2, x2, u3, fore_carry = call(
        fore_kernel, "fore",
        [data(count)] * 6 + [data(rim + 16), data(taps), filt(modes)] + table_specs + spec3,
        [data(count)] * 6 + [data(modes)],
        [shape(count)] * 6 + [shape(modes, F32)],
        [pltpu.VMEM((count + 16, cb), F32)],
    )(value, gate_k1, gate_q1, gate_k2, gate_q2, gate_k3, rim_fore, short_filter, rates, fwd, inv, *med)
    fore_state = scan_states(fore_carry, wide_rates, count, False)

    grad_k3, grad_q2, dz2, du2_near, rim_back_send = call(
        back_long_kernel, "back_long",
        [data(count), data(modes), filt(modes), filt(modes)]
        + [data(count)] * 4 + [data(16)] * 2 + table_specs + spec3,
        [data(count)] * 4 + [data(rim + 16)],
        [shape(count)] * 3 + [shape(count, F32), shape(rim + 16)],
        [pltpu.VMEM((count, cb), F32)],
    )(du3_near, back_state, rates, residues, x2, z2, gate_k3, gate_q2, gate_k2, gate_q1, fwd, inv, *med)
    rim_back = shifted(rim_back_send, -1)

    terms = call(
        medium_terms_kernel, "medium_terms",
        [data(count)] * 2 + [data(rim)] + [whole(fwd.shape), whole(lag.shape)],
        filt(medium_taps), shape(medium_taps, F32, groups), [pltpu.VMEM((2 * count, cb), F32)],
    )(dz2, u2, rim_fore, fwd, lag)

    mixed, grad_q3 = call(
        fore_long_kernel, "fore_long",
        [data(count), data(modes), filt(modes), filt(modes)] + [data(count)] * 2 + table_specs + spec3,
        [data(count)] * 2, [shape(count)] * 2, [pltpu.VMEM((count, cb), F32)],
    )(u3, fore_state, rates, residues, gate_q3, grad_out, fwd, inv, *lng)

    ctx, tp = lax.axis_size("ctx"), lax.axis_size("tp")
    packet = (ctx, 8, cb + LANES)
    grad_k2, grad_q1, grad_k1, grad_value, send = call(
        back_short_kernel, "back_short",
        [data(count), data(rim + 16)] + [data(count)] * 6 + [data(16, rim // 16), data(taps)]
        + [whole((medium_taps, groups))] + table_specs + spec3,
        [data(count)] * 4 + [whole(packet)],
        [shape(count)] * 4 + [jax.ShapeDtypeStruct(packet, F32)],
        [pltpu.VMEM((count + 16, cb), F32)] * 2,
    )(du2_near, rim_back, x1, z1, gate_k2, gate_q1, gate_k1, value, rim_fore, short_filter, terms,
      fwd, inv, *med)

    got = lax.all_to_all(send, "ctx", 0, 0)
    part = jnp.sum(got, axis=0)
    spread = jnp.broadcast_to(part[None, :, :cb], (tp, 8, cb))
    medium = jnp.sum(lax.all_to_all(spread, "tp", 0, 0), axis=0)
    piece = jnp.concatenate([medium, part[:, cb:]], axis=1)
    full = lax.all_to_all(jnp.broadcast_to(piece[None], packet), "ctx", 0, 0)
    share = medium_taps // ctx
    grad_medium = (
        full[:, :, :cb].reshape(ctx, 2, share, cb).transpose(0, 2, 1, 3).reshape(medium_taps, groups)
    )
    grad_short = full[:, 0:2, cb:].reshape(8, width)[:taps]
    return (
        mixed, grad_value, grad_q1, grad_k1, grad_q2, grad_k2, grad_q3, grad_k3, grad_short, grad_medium,
    )


def solution(mesh):
    data = P("ctx", "tp")
    return jax.shard_map(
        on_device,
        mesh=mesh,
        in_specs=(data,) * 8 + (P(None, "tp"), P(), P(), P()),
        out_specs=(data,) * 8 + (P(None, "tp"), P()),
        check_vma=False,
    )
```

time: 658 us -> 116 us (0.18); the launches traced: 648 us -> 114 us
  waiting for transfers between devices: 312 us -> 12.6 us
  blocking collectives: 119 us -> 0 us
  matrix products: 72 us -> 0 us
  other arithmetic: 52.2 us -> 2.07 us
  local copies, waits for them, and re-layouts: 64.2 us -> 15.3 us
  Pallas kernels: 0 us -> 37.5 us
  starting transfers between devices: 12.2 us -> 44.9 us
  between operations: 15.1 us -> 1.87 us
    psum x1 -> x0, waiting for transfers between devices: 238 us -> none  [on_device(): grad_medium = lax.psum(medium_terms, ('ctx', 'tp'))]
    psum x1 -> x0, blocking collectives: 119 us -> none  [on_device(): grad_short = lax.psum(short_terms, 'ctx')]
    dot_general x28 -> x0, matrix products: 72 us -> none  [the longest x5 15.3 us: inverse(): lax.dot_general(sine[:, start:start + rows], imag_part * weights, dims, p...]
    all_gather x3 -> x0, waiting for transfers between devices: 68.4 us -> none  [carried_in(): gathered = jax.tree.map(lambda a: lax.all_gather(a, axis), part)]
    pallas_call x0 -> x9, Pallas kernels: none -> 37.5 us  [the longest x1 7.09 us: on_device(): call(fore_kernel, 'fore', [data(count)] * 6 + [data(rim + 16), data(taps)...]
    add x34 -> x6, other arithmetic: 31 us -> 1.18 us  [the longest x2 1.09 us: scan_states(): prefix = prefix + jnp.where(before, power(gap), 0.0) * other]
    all_to_all x0 -> x3, starting transfers between devices: none -> 22.3 us  [the longest x1 8.79 us: on_device(): got = lax.all_to_all(send, 'ctx', 0, 0)]
    reshape x11 -> x0, local copies, waits for them, and re-layouts: 18.7 us -> none  [the longest x2 5.68 us: modal_conv(): shaped = signal.reshape(count, copies, groups)]
  transfers between devices with their start and end apart: 8 -> 19, of which waited for: 5 -> 5; matrix products, arithmetic and copies ran while one was open for 21% -> 4% of each run, Pallas kernels for 0% -> 14%
where the time goes in v1:
time: 116 us; the launch traced here: 114 us
  starting transfers between devices  44.9 us (39%)
  Pallas kernels  37.5 us (32%)
  local copies, waits for them, and re-layouts  15.3 us (13%)
  waiting for transfers between devices  12.6 us (11%)
  other arithmetic  2.07 us (2%)
  between operations  1.87 us (2%)
    ppermute x14, starting transfers between devices, swapped(): return lax.ppermute(block, 'ctx', [(i, i ^ distance) for i in range(size)])  17 us
    unnamed x122, local copies, waits for them, and re-layouts  12.4 us
    all_to_all x1, starting transfers between devices, on_device(): got = lax.all_to_all(send, 'ctx', 0, 0)  8.79 us
    all_to_all x1, starting transfers between devices, on_device(): medium = jnp.sum(lax.all_to_all(spread, 'tp', 0, 0), axis=0)  8.2 us
    pallas_call x1, Pallas kernels, on_device(): call(fore_kernel, 'fore', [data(count)] * 6 + [data(rim + 16), data(taps)...  7.09 us
    pallas_call x1, Pallas kernels, on_device(): call(back_short_kernel, 'back_short', [data(count), data(rim + 16)] + [da...  6.58 us
    ppermute x2, starting transfers between devices, shifted(): return lax.ppermute(block, 'ctx', route)  5.66 us
    pallas_call x1, Pallas kernels, on_device(): call(back_long_kernel, 'back_long', [data(count), data(modes), filt(modes...  5.62 us
  transfers between devices with their start and end apart: 19, of which 5 were waited for; matrix products, arithmetic and copies ran while one was open for 4% of the time, Pallas kernels for 14%

profile of v1, /device:TPU:1, one launch (start us, length us, event | category | flops | bytes accessed | tf_op | source)
XLA Modules:
  0.0 114.2 jit_solution(14300938910295105001)
XLA Ops:
  0.7 1.0 copy-done.6
  1.7 1.0 copy-done.8
  2.7 0.8 copy-done.11
  3.5 2.1 %back_carry.1 = f32[16,1024]{1,0:T(8,128)S(1)} custom-call(bf16[256,1024]{1,0:T(8,128)(2,1)S(1)} %copy-done.8, bf16[256,1024]{1,0:T(8,128)(2,1)S(1)} %copy-done.6, f32[16,512]{1,0:T(8,128)S(1)} %copy-done.11), custom_call_target="tpu_custom_call" | custom-call | tf_op jit(solution)/shard_map/back_carry/pallas_call | solution.py:388
  5.6 3.3 %collective-permute-start.8 = (f32[16,1024]{1,0:T(8,128)S(1)}, f32[16,1024]{1,0:T(8,128)S(1)}, u32[]{:S(2)}, u32[]{:S(2)}) collective-permute-start(f32[16,1024]{1,0:T(8,128)S(1)} %back_carry.1), channel_id=1, source_target_pairs={{0,8},{8,0},{16,24},{24,16},{32,40},{40,32},{48,56},{56,48},{64,72... | collective-permute-start | bytes 196616 | tf_op jit(solution)/shard_map/ppermute | solution.py:300
  9.0 0.8 copy-done.12
  9.7 0.1 exponential_select_fusion.6
  10.0 0.8 collective-permute-start.11
  10.8 0.5 collective-permute-start.10
  11.3 2.0 %collective-permute-start.9 = (f32[16,1024]{1,0:T(8,128)S(1)}, f32[16,1024]{1,0:T(8,128)S(1)}, u32[]{:S(2)}, u32[]{:S(2)}) collective-permute-start(f32[16,1024]{1,0:T(8,128)S(1)} %multiply_add_fusion.2), channel_id=1, source_target_pairs={{0,16},{8,24},{16,0},{24,8},{32,48},{40,56},{48,32},{56,40},{64,80... | collective-permute-start | bytes 196616 | tf_op jit(solution)/shard_map/ppermute | solution.py:300
  13.3 2.1 %fore_rim.1 = bf16[144,1024]{1,0:T(8,128)(2,1)} custom-call(bf16[256,1024]{1,0:T(8,128)(2,1)S(1)} %copy-done.4, bf16[256,1024]{1,0:T(8,128)(2,1)S(1)} %copy-done.5, bf16[256,1024]{1,0:T(8,128)(2,1)S(1)} %copy-done.1, bf16[256,1024]{1,0:T(8,128)(2,1)S(1)} %copy-done.2, bf16[7,1024]{1,0:T(8,128)(2,1)S(1)} %copy-done.26), custom_call_target="tpu_custom_call" | custom-call | tf_op jit(solution)/shard_map/fore_rim/pallas_call | solution.py:394
  15.4 2.6 %collective-permute-start = (bf16[144,1024]{1,0:T(8,128)(2,1)}, bf16[144,1024]{1,0:T(8,128)(2,1)}, u32[]{:S(2)}, u32[]{:S(2)}) collective-permute-start(bf16[144,1024]{1,0:T(8,128)(2,1)} %fore_rim.1), channel_id=1, source_target_pairs={{0,8},{8,16},{16,24},{24,32},{32,40},{40,48},{48,56},{56,64},{64,7... | collective-permute-start | bytes 884744 | tf_op jit(solution)/shard_map/ppermute | solution.py:306
  18.5 0.5 copy-done.29
  19.1 0.0 copy-done.31
  19.1 0.0 copy-done.33
  19.1 2.5 %collective-permute-start.14 = (f32[16,1024]{1,0:T(8,128)S(1)}, f32[16,1024]{1,0:T(8,128)S(1)}, u32[]{:S(2)}, u32[]{:S(2)}) collective-permute-start(f32[16,1024]{1,0:T(8,128)S(1)} %multiply_add_fusion.1), channel_id=1, source_target_pairs={{0,192},{8,200},{16,208},{24,216},{32,224},{40,232},{48,240},{56,2... | collective-permute-start | bytes 196616 | tf_op jit(solution)/shard_map/ppermute | solution.py:300
  21.6 0.3 collective-permute-start.13
  21.9 0.4 collective-permute-start.12
  22.4 0.7 exponential_select_fusion
  23.5 0.0 copy-start
  23.6 0.6 copy-done.21
  24.2 2.6 %filters.1 = (f32[256,512]{1,0:T(8,128)S(1)}, f32[256,512]{1,0:T(8,128)S(1)}, f32[256,512]{1,0:T(8,128)S(1)}, f32[256,512]{1,0:T(8,128)S(1)}, f32[256,512]{1,0:T(8,128)S(1)}, /*index=5*/f32[256,512]{1,0:T(8,128)S(1)}) custom-call(f32[512,256]{1,0:T(8,128)S(1)} %copy-done.21, bf16[128,512]{1,0:T(8,128)(2,1)S(1)} %copy-done.28, f32[16,512]{1,0:T(8,128)S(1)} %copy-done.25, ...), custom_call_target="tpu_custom_call" | custom-call | tf_op jit(solution)/shard_map/filters/pallas_call | solution.py:401
  27.0 2.8 %back_local.1.near_ref = f32[256,1024]{1,0:T(8,128)S(1)} custom-call(bf16[256,1024]{1,0:T(8,128)(2,1)S(1)} %copy-done.9, bf16[256,1024]{1,0:T(8,128)(2,1)S(1)} %copy-done.7, bf16[512,512]{1,0:T(8,128)(2,1)S(1)} %copy-done, bf16[256,512]{1,0:T(8,128)(2,1)S(1)} %copy-done.3, f32[256,512]{1,0:T(8,128)S(1)} %get-tuple-element.40.la, ...), custom_call_target="tpu_custom_call" | custom-call | tf_op jit(solution)/shard_map/back_local/pallas_call | solution.py:410
  29.8 0.8 copy-done.15
  30.6 0.1 multiply_add_fusion.state_ref
  30.7 0.9 copy-done.13
  31.6 7.1 %fore.1 = (bf16[256,1024]{1,0:T(8,128)(2,1)S(1)}, bf16[256,1024]{1,0:T(8,128)(2,1)S(1)}, bf16[256,1024]{1,0:T(8,128)(2,1)S(1)}, bf16[256,1024]{1,0:T(8,128)(2,1)...) custom-call(bf16[256,1024]{1,0:T(8,128)(2,1)S(1)} %copy-done.4, ...), custom_call_target="tpu_custom_call" | custom-call | tf_op jit(solution)/shard_map/fore/pallas_call | solution.py:415
  38.7 0.0 copy-start.27
  38.7 5.6 %back_long.1 = (bf16[256,1024]{1,0:T(8,128)(2,1)}, bf16[256,1024]{1,0:T(8,128)(2,1)}, bf16[256,1024]{1,0:T(8,128)(2,1)S(1)}, f32[256,1024]{1,0:T(8,128)S(1)}, bf16[144,1024]{1,0:T(8,128)(2,1)S(1)}) custom-call(f32[256,1024]{1,0:T(8,128)S(1)} %back_local.1.near_ref, f32[16,1024]{1,0:T(8,128)S(1)} %multiply_add_fusion.state_ref, f32[16,512]{1,0:T(8,128)S(1)} %copy-done.12, ...), custom_call_target="tpu_custom_call" | custom-call | tf_op jit(solution)/shard_map/back_long/pallas_call | solution.py:424
  44.3 3.0 %collective-permute-start.15 = (bf16[144,1024]{1,0:T(8,128)(2,1)S(1)}, bf16[144,1024]{1,0:T(8,128)(2,1)S(1)}, u32[]{:S(2)}, u32[]{:S(2)}) collective-permute-start(bf16[144,1024]{1,0:T(8,128)(2,1)S(1)} %get-tuple-element.47), channel_id=1, source_target_pairs={{8,0},{16,8},{24,16},{32,24},{40,32},{48,40},{56,48},{64,56},{72,6... | collective-permute-start | bytes 884744 | tf_op jit(solution)/shard_map/ppermute | solution.py:306
  47.4 3.4 %medium_terms.1.terms_ref = f32[128,512]{1,0:T(8,128)S(1)} custom-call(bf16[256,1024]{1,0:T(8,128)(2,1)S(1)} %get-tuple-element.50.dz2_ref, bf16[256,1024]{1,0:T(8,128)(2,1)S(1)} %get-tuple-element.51.u2_ref, bf16[144,1024]{1,0:T(8,128)(2,1)} %collective-permute-done.rim_ref.fore_ref, bf16[512,512]{1,0:T(8,128)(2,1)S(1)} %copy-done, ...), custom_call_target="tpu_custom_call" | custom-call | tf_op jit(solution)/shard_map/medium_terms/pallas_call | solution.py:434
  50.8 1.6 %collective-permute-done.15.rim_ref = bf16[144,1024]{1,0:T(8,128)(2,1)S(1)} collective-permute-done((bf16[144,1024]{1,0:T(8,128)(2,1)S(1)}, bf16[144,1024]{1,0:T(8,128)(2,1)S(1)}, u32[]{:S(2)}, u32[]{:S(2)}) %collective-permute-start.15) | collective-permute-done | bytes 294944 | tf_op jit(solution)/shard_map/ppermute | solution.py:306
  52.4 6.6 %back_short.1 = (bf16[256,1024]{1,0:T(8,128)(2,1)}, bf16[256,1024]{1,0:T(8,128)(2,1)}, bf16[256,1024]{1,0:T(8,128)(2,1)}, bf16[256,1024]{1,0:T(8,128)(2,1)}, f32[32,8,384]{2,1,0:T(8,128)S(1)}) custom-call(f32[256,1024]{1,0:T(8,128)S(1)} %get-tuple-element.46.du2_ref, bf16[144,1024]{1,0:T(8,128)(2,1)S(1)} %collective-permute-done.15.rim_ref, ...), custom_call_target="tpu_custom_call" | custom-call | tf_op jit(solution)/shard_map/back_short/pallas_call | solution.py:448
  59.0 0.7 copy-done.24
  59.7 8.8 %all-to-all-start = ((f32[32,8,384]{2,1,0:T(8,128)}), f32[32,8,384]{2,1,0:T(8,128)S(1)}, u32[]{:S(2)}, u32[]{:S(2)}) async-start(f32[32,8,384]{2,1,0:T(8,128)} %copy-done.24), calls=%async_computation | async-start | bytes 786432 | tf_op jit(solution)/shard_map/all_to_all | solution.py:458
  68.5 0.3 collective-permute-start.1
  68.9 0.7 copy-done.44
  69.7 0.2 collective-permute-done.1
  69.9 2.7 %collective-permute-start.4 = (f32[16,1024]{1,0:T(8,128)S(1)}, f32[16,1024]{1,0:T(8,128)S(1)}, u32[]{:S(2)}, u32[]{:S(2)}) collective-permute-start(f32[16,1024]{1,0:T(8,128)S(1)} %multiply_add_fusion.5), channel_id=1, source_target_pairs={{0,48},{8,56},{16,32},{24,40},{32,16},{40,24},{48,0},{56,8},{64,11... | collective-permute-start | bytes 196616 | tf_op jit(solution)/shard_map/ppermute | solution.py:300
  72.6 0.6 collective-permute-start.3
  73.1 0.1 collective-permute-start.2
  73.3 0.7 copy-done.42
  74.1 0.7 copy-done.41
  74.9 0.7 copy-done.40
  75.6 3.9 %all-to-all-done = f32[32,8,384]{2,1,0:T(8,128)S(1)} async-done(((f32[32,8,384]{2,1,0:T(8,128)}), f32[32,8,384]{2,1,0:T(8,128)S(1)}, u32[]{:S(2)}, u32[]{:S(2)}) %all-to-all-start) | async-done | bytes 393248 | tf_op jit(solution)/shard_map/all_to_all | solution.py:458
  79.6 0.6 broadcast_in_dim.30
  80.3 8.2 %all-to-all-start.1 = ((f32[8,8,256]{2,1,0:T(8,128)}), f32[8,8,256]{2,1,0:T(8,128)S(1)}, u32[]{:S(2)}, u32[]{:S(2)}) async-start(f32[8,8,256]{2,1,0:T(8,128)} %broadcast_in_dim.30), calls=%async_computation.1 | async-start | bytes 131072 | tf_op jit(solution)/shard_map/all_to_all | solution.py:461
  88.5 0.9 collective-permute-start.7
  89.4 0.4 collective-permute-start.6
  89.9 2.0 %collective-permute-start.5 = (f32[16,1024]{1,0:T(8,128)S(1)}, f32[16,1024]{1,0:T(8,128)}, u32[]{:S(2)}, u32[]{:S(2)}) collective-permute-start(f32[16,1024]{1,0:T(8,128)S(1)} %multiply_add_fusion.4), channel_id=1, source_target_pairs={{0,64},{8,72},{16,80},{24,88},{32,96},{40,104},{48,112},{56,120},{... | collective-permute-start | bytes 196616 | tf_op jit(solution)/shard_map/ppermute | solution.py:300
  91.9 4.4 %all-to-all-done.1 = f32[8,8,256]{2,1,0:T(8,128)S(1)} async-done(((f32[8,8,256]{2,1,0:T(8,128)}), f32[8,8,256]{2,1,0:T(8,128)S(1)}, u32[]{:S(2)}, u32[]{:S(2)}) %all-to-all-start.1) | async-done | bytes 65568 | tf_op jit(solution)/shard_map/all_to_all | solution.py:461
  96.3 0.8 broadcast_in_dim.31
  97.1 5.3 %all-to-all-start.2 = ((f32[32,8,384]{2,1,0:T(8,128)}), f32[32,8,384]{2,1,0:T(8,128)S(1)}, u32[]{:S(2)}, u32[]{:S(2)}) async-start(f32[32,8,384]{2,1,0:T(8,128)} %broadcast_in_dim.31), calls=%async_computation.2 | async-start | bytes 786432 | tf_op jit(solution)/shard_map/all_to_all | solution.py:463
  102.7 0.4 copy-done.37
  103.2 0.2 copy-done.36
  103.6 1.0 multiply_add_fusion.3.state_ref
  104.6 0.1 copy-done.16
  104.7 0.1 copy-done.10
  104.9 5.2 %fore_long.1 = (bf16[256,1024]{1,0:T(8,128)(2,1)}, bf16[256,1024]{1,0:T(8,128)(2,1)}) custom-call(bf16[256,1024]{1,0:T(8,128)(2,1)S(1)} %copy-done.23, f32[16,1024]{1,0:T(8,128)S(1)} %multiply_add_fusion.3.state_ref, f32[16,512]{1,0:T(8,128)S(1)} %copy-done.12, f32[16,512]{1,0:T(8,128)S(1)} %copy-done.25, bf16[256,1024]{1,0:T(8,128)(2,1)S(1)} %copy-done.7, ...), custom_call_target="tpu_custom_call" | custom-call | tf_op jit(solution)/shard_map/fore_long/pallas_call | solution.py:440
  110.0 2.5 %all-to-all-done.2 = f32[32,8,384]{2,1,0:T(8,128)S(1)} async-done(((f32[32,8,384]{2,1,0:T(8,128)}), f32[32,8,384]{2,1,0:T(8,128)S(1)}, u32[]{:S(2)}, u32[]{:S(2)}) %all-to-all-start.2) | async-done | bytes 393248 | tf_op jit(solution)/shard_map/all_to_all | solution.py:463
  112.6 0.1 copy.32
  112.7 0.2 copy.31
  112.9 0.7 copy.59
  113.6 0.6 slice.20
  (152 shorter events, 1.4 us)
Async XLA Ops:
  0.6 1.0 copy-start.6
  1.7 1.0 copy-start.8
  2.7 0.8 copy-start.11
  3.5 9.8 %copy-start.4 = (bf16[256,1024]{1,0:T(8,128)(2,1)S(1)}, bf16[256,1024]{1,0:T(8,128)(2,1)}, u32[]{:S(2)}) copy-start(bf16[256,1024]{1,0:T(8,128)(2,1)} %value_ref.5) | copy-start | bytes 1572868
  3.5 9.8 %copy-start.5 = (bf16[256,1024]{1,0:T(8,128)(2,1)S(1)}, bf16[256,1024]{1,0:T(8,128)(2,1)}, u32[]{:S(2)}) copy-start(bf16[256,1024]{1,0:T(8,128)(2,1)} %k1_ref.5) | copy-start | bytes 1572868
  5.6 4.3 %collective-permute-start.8 = (f32[16,1024]{1,0:T(8,128)S(1)}, f32[16,1024]{1,0:T(8,128)S(1)}, u32[]{:S(2)}, u32[]{:S(2)}) collective-permute-start(f32[16,1024]{1,0:T(8,128)S(1)} %back_carry.1), channel_id=1, source_target_pairs={{0,8},{8,0},{16,24},{24,16},{32,40},{40,32},{48,56},{56,48},{64,72... | collective-permute-start | bytes 196616 | tf_op jit(solution)/shard_map/ppermute | solution.py:300
  9.0 0.8 copy-start.12
  9.7 3.6 %copy-start.1 = (bf16[256,1024]{1,0:T(8,128)(2,1)S(1)}, bf16[256,1024]{1,0:T(8,128)(2,1)}, u32[]{:S(2)}) copy-start(bf16[256,1024]{1,0:T(8,128)(2,1)} %q1_ref.7) | copy-start | bytes 1572868
  9.7 3.6 %copy-start.2 = (bf16[256,1024]{1,0:T(8,128)(2,1)S(1)}, bf16[256,1024]{1,0:T(8,128)(2,1)}, u32[]{:S(2)}) copy-start(bf16[256,1024]{1,0:T(8,128)(2,1)} %k2_ref.7) | copy-start | bytes 1572868
  9.9 3.4 %copy-start.26 = (bf16[7,1024]{1,0:T(8,128)(2,1)S(1)}, bf16[7,1024]{1,0:T(8,128)(2,1)}, u32[]{:S(2)}) copy-start(bf16[7,1024]{1,0:T(8,128)(2,1)} %filt_ref.5) | copy-start | bytes 43012
  10.0 8.5 %collective-permute-start.11 = (f32[16,1024]{1,0:T(8,128)S(1)}, f32[16,1024]{1,0:T(8,128)S(1)}, u32[]{:S(2)}, u32[]{:S(2)}) collective-permute-start(f32[16,1024]{1,0:T(8,128)S(1)} %multiply_add_fusion.2), channel_id=1, source_target_pairs={{0,48},{8,56},{16,32},{24,40},{32,16},{40,24},{48,0},{56,8},{64,11... | collective-permute-start | bytes 196616 | tf_op jit(solution)/shard_map/ppermute | solution.py:300
  10.8 7.7 %collective-permute-start.10 = (f32[16,1024]{1,0:T(8,128)S(1)}, f32[16,1024]{1,0:T(8,128)S(1)}, u32[]{:S(2)}, u32[]{:S(2)}) collective-permute-start(f32[16,1024]{1,0:T(8,128)S(1)} %multiply_add_fusion.2), channel_id=1, source_target_pairs={{0,32},{8,40},{16,48},{24,56},{32,0},{40,8},{48,16},{56,24},{64,96... | collective-permute-start | bytes 196616 | tf_op jit(solution)/shard_map/ppermute | solution.py:300
  11.3 7.2 %collective-permute-start.9 = (f32[16,1024]{1,0:T(8,128)S(1)}, f32[16,1024]{1,0:T(8,128)S(1)}, u32[]{:S(2)}, u32[]{:S(2)}) collective-permute-start(f32[16,1024]{1,0:T(8,128)S(1)} %multiply_add_fusion.2), channel_id=1, source_target_pairs={{0,16},{8,24},{16,0},{24,8},{32,48},{40,56},{48,32},{56,40},{64,80... | collective-permute-start | bytes 196616 | tf_op jit(solution)/shard_map/ppermute | solution.py:300
  15.4 15.3 %collective-permute-start = (bf16[144,1024]{1,0:T(8,128)(2,1)}, bf16[144,1024]{1,0:T(8,128)(2,1)}, u32[]{:S(2)}, u32[]{:S(2)}) collective-permute-start(bf16[144,1024]{1,0:T(8,128)(2,1)} %fore_rim.1), channel_id=1, source_target_pairs={{0,8},{8,16},{16,24},{24,32},{32,40},{40,48},{48,56},{56,64},{64,7... | collective-permute-start | bytes 884744 | tf_op jit(solution)/shard_map/ppermute | solution.py:306
  19.1 11.5 %collective-permute-start.14 = (f32[16,1024]{1,0:T(8,128)S(1)}, f32[16,1024]{1,0:T(8,128)S(1)}, u32[]{:S(2)}, u32[]{:S(2)}) collective-permute-start(f32[16,1024]{1,0:T(8,128)S(1)} %multiply_add_fusion.1), channel_id=1, source_target_pairs={{0,192},{8,200},{16,208},{24,216},{32,224},{40,232},{48,240},{56,2... | collective-permute-start | bytes 196616 | tf_op jit(solution)/shard_map/ppermute | solution.py:300
  21.6 9.0 %collective-permute-start.13 = (f32[16,1024]{1,0:T(8,128)S(1)}, f32[16,1024]{1,0:T(8,128)S(1)}, u32[]{:S(2)}, u32[]{:S(2)}) collective-permute-start(f32[16,1024]{1,0:T(8,128)S(1)} %multiply_add_fusion.1), channel_id=1, source_target_pairs={{0,128},{8,136},{16,144},{24,152},{32,160},{40,168},{48,176},{56,1... | collective-permute-start | bytes 196616 | tf_op jit(solution)/shard_map/ppermute | solution.py:300
  21.9 8.6 %collective-permute-start.12 = (f32[16,1024]{1,0:T(8,128)S(1)}, f32[16,1024]{1,0:T(8,128)S(1)}, u32[]{:S(2)}, u32[]{:S(2)}) collective-permute-start(f32[16,1024]{1,0:T(8,128)S(1)} %multiply_add_fusion.1), channel_id=1, source_target_pairs={{0,64},{8,72},{16,80},{24,88},{32,96},{40,104},{48,112},{56,120},{... | collective-permute-start | bytes 196616 | tf_op jit(solution)/shard_map/ppermute | solution.py:300
  22.4 1.2 %copy-start.25 = (f32[16,512]{1,0:T(8,128)S(1)}, f32[16,512]{1,0:T(8,128)}, u32[]{:S(2)}) copy-start(f32[16,512]{1,0:T(8,128)} %residues_ref.5) | copy-start | bytes 98308
  22.4 1.2 %copy-start.28 = (bf16[128,512]{1,0:T(8,128)(2,1)S(1)}, bf16[128,512]{1,0:T(8,128)(2,1)}, u32[]{:S(2)}) copy-start(bf16[128,512]{1,0:T(8,128)(2,1)} %medium_ref.1) | copy-start | bytes 393220
  23.1 1.1 copy-start.21
  23.2 3.6 %copy-start.9 = (bf16[256,1024]{1,0:T(8,128)(2,1)S(1)}, bf16[256,1024]{1,0:T(8,128)(2,1)}, u32[]{:S(2)}) copy-start(bf16[256,1024]{1,0:T(8,128)(2,1)} %grad_ref.5) | copy-start | bytes 1572868
  23.4 3.5 %copy-start.7 = (bf16[256,1024]{1,0:T(8,128)(2,1)S(1)}, bf16[256,1024]{1,0:T(8,128)(2,1)}, u32[]{:S(2)}) copy-start(bf16[256,1024]{1,0:T(8,128)(2,1)} %gate_ref.3) | copy-start | bytes 1572868
  23.5 3.4 %copy-start = (bf16[512,512]{1,0:T(8,128)(2,1)S(1)}, bf16[512,512]{1,0:T(8,128)(2,1)}, u32[]{:S(2)}) copy-start(bf16[512,512]{1,0:T(8,128)(2,1)} %constant.152.clone.fwd_ref) | copy-start | bytes 1572868
  24.2 2.7 %copy-start.3 = (bf16[256,512]{1,0:T(8,128)(2,1)S(1)}, bf16[256,512]{1,0:T(8,128)(2,1)}, u32[]{:S(2)}) copy-start(bf16[256,512]{1,0:T(8,128)(2,1)} %constant.153.clone.inv_ref) | copy-start | bytes 786436
  26.8 2.9 %copy-start.17 = (f32[256,512]{1,0:T(8,128)}, f32[256,512]{1,0:T(8,128)S(1)}, u32[]{:S(2)}) copy-start(f32[256,512]{1,0:T(8,128)S(1)} %get-tuple-element.41.lb) | copy-start | bytes 1572868
  26.9 2.9 %copy-start.19 = (f32[256,512]{1,0:T(8,128)}, f32[256,512]{1,0:T(8,128)S(1)}, u32[]{:S(2)}) copy-start(f32[256,512]{1,0:T(8,128)S(1)} %get-tuple-element.42.lc) | copy-start | bytes 1572868
  26.9 3.7 %copy-start.30 = (f32[16,1024]{1,0:T(8,128)S(1)}, f32[16,1024]{1,0:T(8,128)}, u32[]{:S(2)}) copy-start(f32[16,1024]{1,0:T(8,128)} %copy-done.29) | copy-start | bytes 196612
  26.9 3.7 %copy-start.32 = (f32[16,1024]{1,0:T(8,128)S(1)}, f32[16,1024]{1,0:T(8,128)}, u32[]{:S(2)}) copy-start(f32[16,1024]{1,0:T(8,128)} %copy-done.31) | copy-start | bytes 196612
  26.9 3.7 %copy-start.34 = (f32[16,1024]{1,0:T(8,128)S(1)}, f32[16,1024]{1,0:T(8,128)}, u32[]{:S(2)}) copy-start(f32[16,1024]{1,0:T(8,128)} %copy-done.33) | copy-start | bytes 196612
  26.9 3.8 %copy-start.14 = (bf16[256,1024]{1,0:T(8,128)(2,1)S(1)}, bf16[256,1024]{1,0:T(8,128)(2,1)}, u32[]{:S(2)}) copy-start(bf16[256,1024]{1,0:T(8,128)(2,1)} %k3_ref.3) | copy-start | bytes 1572868
  29.8 0.8 copy-start.15
  30.6 1.0 copy-start.13
  38.7 5.6 %copy-start.22 = (bf16[256,1024]{1,0:T(8,128)(2,1)}, bf16[256,1024]{1,0:T(8,128)(2,1)S(1)}, u32[]{:S(2)}) copy-start(bf16[256,1024]{1,0:T(8,128)(2,1)S(1)} %get-tuple-element.38.u3_ref) | copy-start | bytes 1572868
  38.7 8.7 %copy-start.27 = (bf16[128,512]{1,0:T(8,128)(2,1)S(1)}, bf16[128,512]{1,0:T(8,128)(2,1)}, u32[]{:S(2)}) copy-start(bf16[128,512]{1,0:T(8,128)(2,1)} %constant.154.clone.lag_ref) | copy-start | bytes 393220
  44.3 8.0 %collective-permute-start.15 = (bf16[144,1024]{1,0:T(8,128)(2,1)S(1)}, bf16[144,1024]{1,0:T(8,128)(2,1)S(1)}, u32[]{:S(2)}, u32[]{:S(2)}) collective-permute-start(bf16[144,1024]{1,0:T(8,128)(2,1)S(1)} %get-tuple-element.47), channel_id=1, source_target_pairs={{8,0},{16,8},{24,16},{32,24},{40,32},{48,40},{56,48},{64,56},{72,6... | collective-permute-start | bytes 884744 | tf_op jit(solution)/shard_map/ppermute | solution.py:306
  59.0 0.8 copy-start.24
  59.7 9.1 %copy-start.45 = (f32[16,512]{1,0:T(8,128)S(1)}, f32[16,512]{1,0:T(8,128)}, u32[]{:S(2)}) copy-start(f32[16,512]{1,0:T(8,128)} %get-tuple-element.82) | copy-start | bytes 98308
  59.7 19.9 %all-to-all-start = ((f32[32,8,384]{2,1,0:T(8,128)}), f32[32,8,384]{2,1,0:T(8,128)S(1)}, u32[]{:S(2)}, u32[]{:S(2)}) async-start(f32[32,8,384]{2,1,0:T(8,128)} %copy-done.24), calls=%async_computation | async-start | bytes 786432 | tf_op jit(solution)/shard_map/all_to_all | solution.py:458
  68.5 1.3 %collective-permute-start.1 = (f32[16,1024]{1,0:T(8,128)S(1)}, f32[16,1024]{1,0:T(8,128)S(1)}, u32[]{:S(2)}, u32[]{:S(2)}) collective-permute-start(f32[16,1024]{1,0:T(8,128)S(1)} %get-tuple-element.39), channel_id=1, source_target_pairs={{0,8},{8,0},{16,24},{24,16},{32,40},{40,32},{48,56},{56,48},{64,72... | collective-permute-start | bytes 196616 | tf_op jit(solution)/shard_map/ppermute | solution.py:300
  68.9 0.8 copy-start.44
  69.8 3.4 %copy-start.43 = (f32[16,512]{1,0:T(8,128)S(1)}, f32[16,512]{1,0:T(8,128)}, u32[]{:S(2)}) copy-start(f32[16,512]{1,0:T(8,128)} %get-tuple-element.75) | copy-start | bytes 98308
  69.9 18.6 %collective-permute-start.4 = (f32[16,1024]{1,0:T(8,128)S(1)}, f32[16,1024]{1,0:T(8,128)S(1)}, u32[]{:S(2)}, u32[]{:S(2)}) collective-permute-start(f32[16,1024]{1,0:T(8,128)S(1)} %multiply_add_fusion.5), channel_id=1, source_target_pairs={{0,48},{8,56},{16,32},{24,40},{32,16},{40,24},{48,0},{56,8},{64,11... | collective-permute-start | bytes 196616 | tf_op jit(solution)/shard_map/ppermute | solution.py:300
  72.6 15.9 %collective-permute-start.3 = (f32[16,1024]{1,0:T(8,128)S(1)}, f32[16,1024]{1,0:T(8,128)S(1)}, u32[]{:S(2)}, u32[]{:S(2)}) collective-permute-start(f32[16,1024]{1,0:T(8,128)S(1)} %multiply_add_fusion.5), channel_id=1, source_target_pairs={{0,32},{8,40},{16,48},{24,56},{32,0},{40,8},{48,16},{56,24},{64,96... | collective-permute-start | bytes 196616 | tf_op jit(solution)/shard_map/ppermute | solution.py:300
  73.1 15.3 %collective-permute-start.2 = (f32[16,1024]{1,0:T(8,128)S(1)}, f32[16,1024]{1,0:T(8,128)S(1)}, u32[]{:S(2)}, u32[]{:S(2)}) collective-permute-start(f32[16,1024]{1,0:T(8,128)S(1)} %multiply_add_fusion.5), channel_id=1, source_target_pairs={{0,16},{8,24},{16,0},{24,8},{32,48},{40,56},{48,32},{56,40},{64,80... | collective-permute-start | bytes 196616 | tf_op jit(solution)/shard_map/ppermute | solution.py:300
  73.3 0.8 copy-start.42
  74.1 0.8 copy-start.41
  74.8 0.8 copy-start.40
  79.6 12.3 %copy-start.46 = (f32[8,384]{1,0:T(8,128)}, f32[8,384]{1,0:T(8,128)S(1)}, u32[]{:S(2)}) copy-start(f32[8,384]{1,0:T(8,128)S(1)} %reduce_sum.18) | copy-start | bytes 36868
  80.3 16.0 %all-to-all-start.1 = ((f32[8,8,256]{2,1,0:T(8,128)}), f32[8,8,256]{2,1,0:T(8,128)S(1)}, u32[]{:S(2)}, u32[]{:S(2)}) async-start(f32[8,8,256]{2,1,0:T(8,128)} %broadcast_in_dim.30), calls=%async_computation.1 | async-start | bytes 131072 | tf_op jit(solution)/shard_map/all_to_all | solution.py:461
  88.5 15.0 %collective-permute-start.7 = (f32[16,1024]{1,0:T(8,128)S(1)}, f32[16,1024]{1,0:T(8,128)}, u32[]{:S(2)}, u32[]{:S(2)}) collective-permute-start(f32[16,1024]{1,0:T(8,128)S(1)} %multiply_add_fusion.4), channel_id=1, source_target_pairs={{0,192},{8,200},{16,208},{24,216},{32,224},{40,232},{48,240},{56,2... | collective-permute-start | bytes 196616 | tf_op jit(solution)/shard_map/ppermute | solution.py:300
  89.4 14.1 %collective-permute-start.6 = (f32[16,1024]{1,0:T(8,128)S(1)}, f32[16,1024]{1,0:T(8,128)}, u32[]{:S(2)}, u32[]{:S(2)}) collective-permute-start(f32[16,1024]{1,0:T(8,128)S(1)} %multiply_add_fusion.4), channel_id=1, source_target_pairs={{0,128},{8,136},{16,144},{24,152},{32,160},{40,168},{48,176},{56,1... | collective-permute-start | bytes 196616 | tf_op jit(solution)/shard_map/ppermute | solution.py:300
  89.9 13.7 %collective-permute-start.5 = (f32[16,1024]{1,0:T(8,128)S(1)}, f32[16,1024]{1,0:T(8,128)}, u32[]{:S(2)}, u32[]{:S(2)}) collective-permute-start(f32[16,1024]{1,0:T(8,128)S(1)} %multiply_add_fusion.4), channel_id=1, source_target_pairs={{0,64},{8,72},{16,80},{24,88},{32,96},{40,104},{48,112},{56,120},{... | collective-permute-start | bytes 196616 | tf_op jit(solution)/shard_map/ppermute | solution.py:300
  91.9 4.4 %slice-start = ((f32[8,384]{1,0:T(8,128)}), f32[8,128]{1,0:T(8,128)S(1)}, s32[]{:S(2)}) async-start(f32[8,384]{1,0:T(8,128)} %copy-done.46), calls=%async_computation.3 | async-start | bytes 8192 | tf_op jit(solution)/shard_map/slice | solution.py:462
  97.1 5.5 %copy-start.39 = (f32[16,512]{1,0:T(8,128)S(1)}, f32[16,512]{1,0:T(8,128)}, u32[]{:S(2)}) copy-start(f32[16,512]{1,0:T(8,128)} %get-tuple-element.73) | copy-start | bytes 98308
  97.1 5.5 %copy-start.38 = (f32[16,512]{1,0:T(8,128)S(1)}, f32[16,512]{1,0:T(8,128)}, u32[]{:S(2)}) copy-start(f32[16,512]{1,0:T(8,128)} %get-tuple-element.74) | copy-start | bytes 98308
  97.1 15.5 %all-to-all-start.2 = ((f32[32,8,384]{2,1,0:T(8,128)}), f32[32,8,384]{2,1,0:T(8,128)S(1)}, u32[]{:S(2)}, u32[]{:S(2)}) async-start(f32[32,8,384]{2,1,0:T(8,128)} %broadcast_in_dim.31), calls=%async_computation.2 | async-start | bytes 786432 | tf_op jit(solution)/shard_map/all_to_all | solution.py:463
  102.4 0.8 copy-start.37
  102.4 2.2 %copy-start.23 = (bf16[256,1024]{1,0:T(8,128)(2,1)S(1)}, bf16[256,1024]{1,0:T(8,128)(2,1)}, u32[]{:S(2)}) copy-start(bf16[256,1024]{1,0:T(8,128)(2,1)} %copy-done.22) | copy-start | bytes 1572868
  102.5 2.1 %copy-start.20 = (f32[256,512]{1,0:T(8,128)S(1)}, f32[256,512]{1,0:T(8,128)}, u32[]{:S(2)}) copy-start(f32[256,512]{1,0:T(8,128)} %copy-done.19) | copy-start | bytes 1572868
  102.6 0.8 copy-start.36
  102.7 0.8 copy-start.35
  103.2 1.5 %copy-start.18 = (f32[256,512]{1,0:T(8,128)S(1)}, f32[256,512]{1,0:T(8,128)}, u32[]{:S(2)}) copy-start(f32[256,512]{1,0:T(8,128)} %copy-done.17) | copy-start | bytes 1572868
  103.5 1.2 %copy-start.16 = (f32[256,512]{1,0:T(8,128)S(1)}, f32[256,512]{1,0:T(8,128)}, u32[]{:S(2)}) copy-start(f32[256,512]{1,0:T(8,128)} %copy-done.15) | copy-start | bytes 1572868
  103.5 1.3 %copy-start.10 = (bf16[256,1024]{1,0:T(8,128)(2,1)S(1)}, bf16[256,1024]{1,0:T(8,128)(2,1)}, u32[]{:S(2)}) copy-start(bf16[256,1024]{1,0:T(8,128)(2,1)} %grad_ref.5) | copy-start | bytes 1572868
  (3 other events, 1.9 us)

commit v2 on v1

v2 whole, which is shorter than its diff:
```python
import jax
import jax.numpy as jnp
import numpy as np
from jax import lax
from jax.experimental import pallas as pl
from jax.experimental.pallas import tpu as pltpu
from jax.sharding import PartitionSpec as P

F32 = jnp.float32
BF = jnp.bfloat16
LANES = 128
VMEM_LIMIT = 28 * 1024 * 1024
BLOCK = 256
UNROLL = 4


def dft_tables(count):
    size = 2 * count
    freq = np.arange(count)[:, None].astype(np.int64)

    def waves(times):
        phase = (freq * times[None, :]) % size * (2.0 * np.pi / size)
        cosine, sine = np.cos(phase), -np.sin(phase)
        sine[0] = np.where(times % 2 == 0, 1.0, -1.0)
        return np.concatenate([cosine, sine], axis=0)

    forward = waves(np.arange(size))
    scale = np.full((size, 1), 2.0 / size)
    scale[0] = scale[count] = 1.0 / size
    backward = (forward * scale).T
    return forward, backward


def dot(a, b):
    return jnp.dot(a, b, preferred_element_type=F32)


def spec_mul(spec, filt):
    half = spec.shape[0] // 2
    re, im = spec[:half], spec[half:]
    a, b, c = filt
    return jnp.concatenate([(re * a - im * b).astype(BF), (re * b + im * c).astype(BF)], axis=0)


def spec_conj(spec, filt):
    half = spec.shape[0] // 2
    re, im = spec[:half], spec[half:]
    a, b, c = filt
    return jnp.concatenate([(re * a + im * b).astype(BF), (im * c - re * b).astype(BF)], axis=0)


def row_index(shape):
    return lax.broadcasted_iota(jnp.int32, shape, 0)


def end_states(signal_ref, rates_ref, lanes, own, reverse):
    tiles = signal_ref.shape[0] // 8
    modes = rates_ref.shape[0]
    rates = rates_ref[:, own]
    step = jnp.exp(-8.0 * rates)
    steps = [jnp.broadcast_to(step[m : m + 1], (8, LANES)) for m in range(modes)]

    def body(j, sums):
        tile = tiles - 1 - j if reverse else j
        u = signal_ref[pl.ds(pl.multiple_of(tile * 8, 8), 8), lanes]
        return tuple(s * a + u for s, a in zip(sums, steps))

    zero = jnp.zeros((8, LANES), F32)
    sums = lax.fori_loop(0, tiles, body, (zero,) * modes, unroll=UNROLL)
    sub = row_index((8, LANES)).astype(F32)
    ages = sub if reverse else 7.0 - sub
    rows = [
        jnp.sum(s * jnp.exp(-rates[m : m + 1] * ages), axis=0, keepdims=True)
        for m, s in enumerate(sums)
    ]
    return jnp.concatenate(rows, axis=0)


def far_field(states, rates, weights, out_ref, reverse, first, lanes):
    tiles = out_ref.shape[0] // 8
    modes = rates.shape[0]
    weights = weights * jnp.sqrt(2.0 * rates)
    if states is not None:
        weights = weights * states
    step = jnp.exp(-8.0 * rates)
    steps = [jnp.broadcast_to(step[m : m + 1], (8, LANES)) for m in range(modes)]
    sub = row_index((8, LANES)).astype(F32)
    ages = (7.0 - sub if reverse else sub) + float(first)
    terms = tuple(weights[m : m + 1] * jnp.exp(-rates[m : m + 1] * ages) for m in range(modes))

    def body(j, terms):
        tile = tiles - 1 - j if reverse else j
        level = list(terms)
        while len(level) > 1:
            level = [level[i] + level[i + 1] for i in range(0, len(level), 2)]
        out_ref[pl.ds(pl.multiple_of(tile * 8, 8), 8), lanes] = level[0]
        return tuple(s * a for s, a in zip(terms, steps))

    lax.fori_loop(0, tiles, body, terms, unroll=UNROLL)


def parts(width, groups, size=BLOCK):
    for start in range(0, width, size):
        own = start % groups
        yield slice(start, start + size), slice(own, own + size)


def mul(a, b):
    return a.astype(F32) * b.astype(F32)


def short_causal(ext, filt, rows, start, lanes):
    total = None
    for lag in range(filt.shape[0]):
        term = ext[pl.ds(start - lag, rows), lanes] * filt[lag : lag + 1, lanes].astype(F32)
        total = term if total is None else total + term
    return total


def fore_rim_kernel(flow, place_ref, value_ref, k1_ref, q1_ref, k2_ref, filt_ref, out_ref, ext):
    del place_ref
    count, width = value_ref.shape
    rim = out_ref.shape[0] - 16
    top = count - rim - 16
    for block, (lanes, _) in enumerate(parts(width, width)):
        flow.ready(block)
        u1 = mul(k1_ref[top:, lanes], value_ref[top:, lanes]).astype(BF)
        ext[:, lanes] = u1.astype(F32)
        z1 = short_causal(ext, filt_ref, rim, 16, lanes)
        x1 = mul(q1_ref[count - rim :, lanes], z1).astype(BF)
        out_ref[0:rim, lanes] = mul(k2_ref[count - rim :, lanes], x1).astype(BF)
        out_ref[rim : rim + 16, lanes] = u1[rim:]


def spectrum(table, filt, out):
    count = out.shape[1]
    spec = jnp.dot(
        table[:, : filt.shape[0]], filt, precision=lax.Precision.HIGHEST, preferred_element_type=F32
    )
    re, im = spec[:count], spec[count:]
    edge = row_index(re.shape) == 0
    out[0] = re
    out[1] = jnp.where(edge, 0.0, im)
    out[2] = jnp.where(edge, im, re)


def medium_filter_kernel(flow, table_ref, medium_ref, *refs):
    out_ref = refs[-1]
    flow.ready(0)
    spectrum(table_ref, medium_ref[...].astype(F32), out_ref)
    for piece in range(1, 4):
        flow.ready(piece)


def long_filter_kernel(table_ref, residues_ref, rates_ref, out_ref, local):
    for lanes, _ in parts(local.shape[1], local.shape[1], LANES):
        far_field(None, rates_ref[:, lanes], residues_ref[:, lanes], local, False, 0, lanes)
    spectrum(table_ref, local[...], out_ref)


def filt_of(ref, own):
    return ref[0, :, own], ref[1, :, own], ref[2, :, own]


def back_carry_kernel(grad_ref, gate_ref, rates_ref, carry_ref, signal):
    count, width = grad_ref.shape
    groups = rates_ref.shape[1]
    for lanes, own in parts(width, groups):
        signal[:, lanes] = mul(grad_ref[:, lanes], gate_ref[:, lanes])
        for side in range(0, BLOCK, LANES):
            at = slice(lanes.start + side, lanes.start + side + LANES)
            mine = slice(own.start + side, own.start + side + LANES)
            carry_ref[:, at] = end_states(signal, rates_ref, at, mine, True)


def back_near_kernel(grad_ref, gate_ref, fwd_ref, inv_ref, long_ref, near_ref):
    count, width = grad_ref.shape
    for lanes, own in parts(width, long_ref.shape[2]):
        spec = dot(fwd_ref[:, :count], mul(grad_ref[:, lanes], gate_ref[:, lanes]).astype(BF))
        near_ref[:, lanes] = dot(inv_ref[...], spec_conj(spec, filt_of(long_ref, own)))


def fore_kernel(
    value_ref, k1_ref, q1_ref, k2_ref, q2_ref, k3_ref, rim_ref, filt_ref, rates_ref, back_ref,
    fwd_ref, inv_ref, med_ref,
    z1_ref, x1_ref, u2_ref, z2_ref, x2_ref, u3_ref, carry_ref, send_ref, ext, signal,
):
    count, width = value_ref.shape
    modes, groups = rates_ref.shape
    rim = rim_ref.shape[0] - 16
    for lanes, own in parts(width, groups):
        u1 = mul(k1_ref[:, lanes], value_ref[:, lanes]).astype(BF)
        ext[0:16, lanes] = rim_ref[rim : rim + 16, lanes].astype(F32)
        ext[16:, lanes] = u1.astype(F32)
        z1 = short_causal(ext, filt_ref, count, 16, lanes)
        z1_ref[:, lanes] = z1.astype(BF)
        x1 = mul(q1_ref[:, lanes], z1).astype(BF)
        x1_ref[:, lanes] = x1
        u2 = mul(k2_ref[:, lanes], x1).astype(BF)
        u2_ref[:, lanes] = u2
        spec = dot(fwd_ref[:, :count], u2)
        spec = spec + dot(fwd_ref[:, 2 * count - rim :], rim_ref[0:rim, lanes])
        z2 = dot(inv_ref[...], spec_mul(spec, filt_of(med_ref, own)))
        z2_ref[:, lanes] = z2.astype(BF)
        x2 = mul(q2_ref[:, lanes], z2).astype(BF)
        x2_ref[:, lanes] = x2
        u3 = mul(k3_ref[:, lanes], x2).astype(BF)
        u3_ref[:, lanes] = u3
        signal[:, lanes] = u3.astype(F32)
    carry_ref[0:modes, :] = back_ref[...]
    for lanes, own in parts(width, groups, LANES):
        carry_ref[modes:, lanes] = end_states(signal, rates_ref, lanes, own, False)
    send_ref[...] = carry_ref[...].astype(BF)


def back_long_kernel(
    flow, near_ref, state_ref, rates_ref, residues_ref, x2_ref, z2_ref, k3_ref, q2_ref, k2_ref, q1_ref,
    fwd_ref, inv_ref, med_ref,
    gk3_ref, gq2_ref, dz2_ref, du2_ref, rim_ref, far,
):
    count, width = near_ref.shape
    modes, groups = rates_ref.shape
    rim = rim_ref.shape[0] - 16
    for lanes, own in parts(width, groups, LANES):
        far_field(
            state_ref[0:modes, lanes], rates_ref[:, own], residues_ref[:, own], far, True, 1, lanes
        )
    for block, (lanes, own) in enumerate(parts(width, groups)):
        du3 = near_ref[:, lanes] + far[:, lanes]
        gk3_ref[:, lanes] = mul(du3, x2_ref[:, lanes]).astype(BF)
        dx2 = mul(du3, k3_ref[:, lanes]).astype(BF)
        gq2_ref[:, lanes] = mul(dx2, z2_ref[:, lanes]).astype(BF)
        dz2 = mul(dx2, q2_ref[:, lanes]).astype(BF)
        dz2_ref[:, lanes] = dz2
        spec = dot(fwd_ref[:, :count], dz2)
        du2 = dot(inv_ref[...], spec_conj(spec, filt_of(med_ref, own)))
        du2_ref[:, lanes] = du2
        rim_ref[0:rim, lanes] = dz2[0:rim]
        dx1 = mul(du2[0:16], k2_ref[0:16, lanes]).astype(BF)
        rim_ref[rim : rim + 16, lanes] = mul(dx1, q1_ref[0:16, lanes]).astype(BF)
        flow.flush(block)


def medium_terms_kernel(dz2_ref, u2_ref, rim_ref, fwd_ref, lag_ref, out_ref, total):
    count, width = dz2_ref.shape
    groups = out_ref.shape[1]
    rim = rim_ref.shape[0] - 16
    for lanes, own in parts(width, groups):
        ext = dot(fwd_ref[:, :count], u2_ref[:, lanes])
        ext = ext + dot(fwd_ref[:, 2 * count - rim :], rim_ref[0:rim, lanes])
        grad = dot(fwd_ref[:, :count], dz2_ref[:, lanes])
        er, ei, dr, di = ext[:count], ext[count:], grad[:count], grad[count:]
        edge = row_index(er.shape) == 0
        high = di * ei
        re = dr * er + jnp.where(edge, 0.0, high)
        im = jnp.where(edge, high, dr * ei - di * er)
        if lanes == own:
            total[:count, own] = re
            total[count:, own] = im
        else:
            total[:count, own] += re
            total[count:, own] += im
    out_ref[...] = dot(lag_ref[...], total[...].astype(BF))


def back_short_kernel(
    flow, du2_ref, rim_ref, x1_ref, z1_ref, k2_ref, q1_ref, k1_ref, value_ref, fore_ref, filt_ref,
    terms_ref, fwd_ref, inv_ref, med_ref,
    gk2_ref, gq1_ref, gk1_ref, gv_ref, send_ref, ext, signal, packet,
):
    count, width = du2_ref.shape
    groups = terms_ref.shape[1]
    rim = rim_ref.shape[0] - 16
    taps = filt_ref.shape[0]
    pieces = send_ref.shape[0]
    share = terms_ref.shape[0] // pieces
    half = groups // 2
    packet[...] = jnp.zeros_like(packet)
    for piece in range(pieces):
        rows = terms_ref[piece * share : (piece + 1) * share, :]
        packet[piece, 0:share, 0:half] = rows[:, :half]
        packet[piece, share : 2 * share, 0:half] = rows[:, half:]
    for block, (lanes, own) in enumerate(parts(width, groups)):
        spec = dot(fwd_ref[:, count : count + rim], rim_ref[0:rim, lanes])
        du2 = du2_ref[:, lanes] + dot(inv_ref[...], spec_conj(spec, filt_of(med_ref, own)))
        gk2_ref[:, lanes] = mul(du2, x1_ref[:, lanes]).astype(BF)
        dx1 = mul(du2, k2_ref[:, lanes]).astype(BF)
        gq1_ref[:, lanes] = mul(dx1, z1_ref[:, lanes]).astype(BF)
        dz1 = mul(dx1, q1_ref[:, lanes]).astype(BF).astype(F32)
        ext[0:count, lanes] = dz1
        ext[count:, lanes] = rim_ref[rim : rim + 16, lanes].astype(F32)
        signal[0:16, lanes] = fore_ref[rim : rim + 16, lanes].astype(F32)
        signal[16:, lanes] = mul(k1_ref[:, lanes], value_ref[:, lanes]).astype(BF).astype(F32)
        du1 = None
        for lag in range(taps):
            term = ext[pl.ds(lag, count), lanes] * filt_ref[lag : lag + 1, lanes].astype(F32)
            du1 = term if du1 is None else du1 + term
        gk1_ref[:, lanes] = mul(du1, value_ref[:, lanes]).astype(BF)
        gv_ref[:, lanes] = mul(du1, k1_ref[:, lanes]).astype(BF)
        flow.flush(block)
        for lag in range(taps):
            row = jnp.sum(dz1 * signal[pl.ds(16 - lag, count), lanes], axis=0, keepdims=True)
            spot = lag * (width // BLOCK) + block
            packet[spot, 0:1, half : half + LANES] = row[:, :LANES]
            packet[spot, 1:2, half : half + LANES] = row[:, LANES:]
    send_ref[...] = packet[...].astype(send_ref.dtype)


def fore_near_kernel(u3_ref, fwd_ref, inv_ref, long_ref, near_ref):
    count, width = u3_ref.shape
    for lanes, own in parts(width, long_ref.shape[2]):
        spec = dot(fwd_ref[:, :count], u3_ref[:, lanes])
        near_ref[:, lanes] = dot(inv_ref[...], spec_mul(spec, filt_of(long_ref, own)))


def fore_long_kernel(
    flow, near_ref, state_ref, rates_ref, residues_ref, q3_ref, grad_ref, mixed_ref, gq3_ref, far
):
    width = near_ref.shape[1]
    modes, groups = rates_ref.shape
    for block, (lanes, own) in enumerate(parts(width, groups)):
        for side in range(0, BLOCK, LANES):
            at = slice(lanes.start + side, lanes.start + side + LANES)
            mine = slice(own.start + side, own.start + side + LANES)
            far_field(
                state_ref[modes:, at], rates_ref[:, mine], residues_ref[:, mine], far, False, 1, at
            )
        z3 = far[:, lanes] + near_ref[:, lanes]
        mixed_ref[:, lanes] = mul(q3_ref[:, lanes], z3).astype(BF)
        gq3_ref[:, lanes] = mul(grad_ref[:, lanes], z3).astype(BF)
        flow.flush(block)


def scan_kernel(count, group, fan, size, refs):
    place_ref, rates_ref, total_ref = refs[:3]
    others = refs[3 : 2 + fan]
    rest = refs[2 + fan :]
    prefix_ref = None if group == 1 else rest[0]
    outs = rest if group == 1 else rest[1:]
    modes, groups = rates_ref.shape
    width = total_ref.shape[1]
    place = place_ref[0]
    last = group * fan >= size
    for side in range(2):
        rows = slice(side * modes, (side + 1) * modes)
        at = size - 1 - place if side == 0 else place
        mine = (at // group) % fan
        offset = at % group
        drop = rates_ref[...] * float(-count)

        def power(n, keep=None):
            value = jnp.exp(drop * n.astype(F32))
            return value if keep is None else jnp.where(keep, value, 0.0)

        for copy in range(width // groups):
            lanes = slice(copy * groups, (copy + 1) * groups)
            prefix = jnp.zeros((modes, groups), F32) if group == 1 else prefix_ref[rows, lanes]
            total = None
            if not last:
                total = total_ref[rows, lanes] * power(group * (fan - 1 - mine))
            for d, other in enumerate(others, 1):
                theirs = mine ^ d
                before = theirs < mine
                block = other[rows, lanes].astype(F32)
                gap = jnp.where(before, offset + group * (mine - 1 - theirs), 0)
                prefix = prefix + power(gap, before) * block
                if not last:
                    total = total + power(group * (fan - 1 - theirs)) * block
            outs[0][rows, lanes] = prefix
            if not last:
                outs[1][rows, lanes] = total
                outs[2][rows, lanes] = total.astype(BF)


def first_sum_kernel(got_ref, spread_ref, part_ref):
    part = jnp.sum(got_ref[...].astype(F32), axis=0)
    part_ref[...] = part
    half = spread_ref.shape[2]
    spread_ref[...] = jnp.broadcast_to(part[None, :, :half], spread_ref.shape).astype(
        spread_ref.dtype
    )


def second_sum_kernel(got_ref, part_ref, piece_ref):
    medium = jnp.sum(got_ref[...].astype(F32), axis=0)
    half = medium.shape[1]
    piece = jnp.concatenate([medium, part_ref[:, half:]], axis=1)
    piece_ref[...] = jnp.broadcast_to(piece[None], piece_ref.shape).astype(piece_ref.dtype)


def collect_kernel(full_ref, short_ref, medium_ref):
    pieces = full_ref.shape[0]
    half = medium_ref.shape[1] // 2
    share = medium_ref.shape[0] // pieces
    for piece in range(pieces):
        rows = full_ref[piece].astype(F32)
        place = slice(piece * share, (piece + 1) * share)
        medium_ref[place, :half] = rows[0:share, :half]
        medium_ref[place, half:] = rows[share : 2 * share, :half]
    blocks = short_ref.shape[1] // BLOCK
    for lag in range(short_ref.shape[0]):
        for block in range(blocks):
            rows = full_ref[lag * blocks + block].astype(F32)
            for side in range(2):
                start = block * BLOCK + side * LANES
                short_ref[lag : lag + 1, start : start + LANES] = rows[side : side + 1, half:]


def swapped(block, distance):
    size = lax.axis_size("ctx")
    return lax.ppermute(block, "ctx", [(i, i ^ distance) for i in range(size)])


def shifted(block, distance):
    size = lax.axis_size("ctx")
    route = [(i, i + distance) for i in range(size) if 0 <= i + distance < size]
    return lax.ppermute(block, "ctx", route)


def exchanged(block, axis):
    return lax.all_to_all(block, axis, 0, 0)


def axes():
    return lax.axis_size("ctx"), lax.axis_size("tp"), lax.axis_index("ctx")


def shape(rows, cols, dtype=BF):
    return jax.ShapeDtypeStruct((rows, cols), dtype)


class Big:
    def __init__(self, array, block=BLOCK, kept=False):
        self.array, self.block, self.kept = array, block, kept

    def lanes(self):
        width = self.array.shape[-1]
        return [slice(k, k + self.block) for k in range(0, width, self.block)]


class Held:
    def __init__(self, array):
        self.array = array


class Moves:
    def __init__(self, sources, targets, arrays, sems):
        self.copies, count = {}, 0
        for piece in range(max([len(a.lanes()) for a in arrays], default=0)):
            for source, target, array in zip(sources, targets, arrays):
                if piece < len(array.lanes()):
                    at = (slice(None),) * (len(array.array.shape) - 1) + (array.lanes()[piece],)
                    copy = pltpu.make_async_copy(source.at[at], target.at[at], sems.at[count])
                    self.copies.setdefault(piece, []).append(copy)
                    count += 1

    def start(self, piece):
        for copy in self.copies.get(piece, []):
            copy.start()

    def wait(self, piece):
        for copy in self.copies.get(piece, []):
            copy.wait()


class Flow:
    def __init__(self, loads, stores):
        self.loads, self.stores = loads, stores
        for piece in loads.copies:
            loads.start(piece)

    def ready(self, piece):
        self.loads.wait(piece)

    def flush(self, piece):
        self.stores.start(piece)


def call(kernel, name, out_shape, *scratch, scalars=0):
    outs = out_shape if isinstance(out_shape, list) else [out_shape]

    def typed(o):
        if isinstance(o, Big):
            return pltpu.HBM(o.array.shape, o.array.dtype)
        return pltpu.VMEM(o.array.shape, o.array.dtype) if isinstance(o, Held) else o

    def placed(a):
        if isinstance(a, Big):
            return pltpu.with_memory_space_constraint(a.array, pltpu.HBM)
        if isinstance(a, Held):
            return pltpu.with_memory_space_constraint(a.array, pltpu.VMEM)
        return a

    def run(*args):
        big_in = [a for a in args if isinstance(a, Big)]
        kept = [a for a in big_in if a.kept]
        big_out = [o for o in outs if isinstance(o, Big)]

        def body(*refs):
            ins, rest = list(refs[: len(args)]), refs[len(args) :]
            results, rest = list(rest[: len(outs)]), rest[len(outs) :]
            held_kept, rest = iter(rest[: len(kept)]), rest[len(kept) :]
            fresh = len(big_in) - len(kept)
            held_new, rest = iter(rest[:fresh]), rest[fresh:]
            held_in = [next(held_kept) if a.kept else next(held_new) for a in big_in]
            held_out, rest = rest[: len(big_out)], rest[len(big_out) :]
            own, sems = rest[: len(scratch)], rest[len(scratch) :]
            if not big_in and not big_out:
                kernel(*ins, *results, *own)
                return
            at_in = [k for k, a in enumerate(args) if isinstance(a, Big)]
            at_out = [k for k, o in enumerate(outs) if isinstance(o, Big)]
            loads = Moves([ins[k] for k in at_in], held_in, big_in, sems[0])
            stores = Moves(held_out, [results[k] for k in at_out], big_out, sems[1])
            for k, ref in zip(at_in, held_in):
                ins[k] = ref
            for k, ref in zip(at_out, held_out):
                results[k] = ref
            kernel(Flow(loads, stores), *ins, *results, *own)
            for piece in stores.copies:
                stores.wait(piece)

        def place(a, k=None):
            if isinstance(a, Big):
                return pl.BlockSpec(memory_space=pltpu.HBM)
            return pl.BlockSpec(memory_space=pltpu.SMEM if k is not None and k < scalars else pltpu.VMEM)

        held = [pltpu.VMEM(a.array.shape, a.array.dtype) for a in big_in + big_out if not a.kept]
        sems = []
        if big_in or big_out:
            for group in (big_in, big_out):
                sems.append(pltpu.SemaphoreType.DMA((max(1, sum(len(a.lanes()) for a in group)),)))
        got = pl.pallas_call(
            body,
            name=name,
            in_specs=[place(a, k) for k, a in enumerate(args)],
            out_specs=[place(o) for o in outs] + [place(None)] * len(kept),
            out_shape=[typed(o) for o in outs] + [typed(Held(a.array)) for a in kept],
            scratch_shapes=held + [pltpu.VMEM(c, F32) for c in scratch] + sems,
            compiler_params=pltpu.CompilerParams(vmem_limit_bytes=VMEM_LIMIT),
        )(*[placed(a) for a in args])
        return got if isinstance(out_shape, list) or kept else got[0]

    return run


def after(array, other):
    return lax.optimization_barrier((array, other))[0]


def scan_states(total, send, rates, count, place, size, works):
    modes2, width = total.shape
    prefix = ()
    group = 1
    done = []
    for fan, work in zip((2, 4, 4), works):
        others = [swapped(send, d * group) for d in range(1, fan)]
        done.append(work(send, *done))
        total = after(total, done[-1])
        last = group * fan >= size
        outs = [shape(modes2, width, F32)]
        if not last:
            outs += [shape(modes2, width, F32), shape(modes2, width)]

        def kernel(*refs, group=group, fan=fan):
            scan_kernel(count, group, fan, size, refs)

        got = call(kernel, "scan%d" % group, outs, scalars=1)(place, rates, total, *others, *prefix)
        prefix = (got[0],)
        if not last:
            total, send = got[1], got[2]
        group *= fan
    return prefix[0], done


def on_device(
    value, gate_q1, gate_k1, gate_q2, gate_k2, gate_q3, gate_k3, grad_out,
    short_filter, medium_filter, residues, rates,
):
    count, width = value.shape
    modes, groups = rates.shape
    taps, rim = short_filter.shape[0], medium_filter.shape[0]
    ctx, tp, place = axes()
    place = jnp.reshape(place, (1,)).astype(jnp.int32)
    forward, backward = dft_tables(count)
    fwd32 = jnp.asarray(forward[:, :count], F32)
    fwd = jnp.asarray(forward, BF)
    inv = jnp.asarray(backward[:count], BF)
    lag = jnp.asarray(backward[(-np.arange(rim)) % (2 * count)], BF)
    value, gate_q1, gate_k1, gate_q2, gate_k2, gate_q3, gate_k3, grad_out = [
        Big(a, kept=True)
        for a in (value, gate_q1, gate_k1, gate_q2, gate_k2, gate_q3, gate_k3, grad_out)
    ]
    tables = [Big(t, t.shape[1], kept=True) for t in (fwd32, fwd, inv, lag)]
    full, ext_full = Big(shape(count, width)), (count + 16, width)
    kept, wide = Held(shape(count, width)), Held(shape(count, width, F32))
    filters = Held(jax.ShapeDtypeStruct((3, count, groups), F32))

    def hold(arrays):
        return [Held(a) for a in arrays]

    rim_send, *got = call(
        fore_rim_kernel, "fore_rim", shape(rim + 16, width), (rim + 16, width), scalars=1
    )(place, value, gate_k1, gate_q1, gate_k2, short_filter)
    value, gate_k1, gate_q1, gate_k2 = hold(got)
    rim_fore = shifted(rim_send, 1)
    got = call(medium_filter_kernel, "medium_filter", filters)(
        tables[0], medium_filter, *tables[1:], grad_out, gate_q3, gate_q2, gate_k3
    )
    med, fwd32, fwd, inv, lag, grad_out, gate_q3, gate_q2, gate_k3 = hold(got)
    back_carry = call(back_carry_kernel, "back_carry", shape(modes, width, F32), (count, width))(
        grad_out, gate_q3, rates
    )

    got = call(
        fore_kernel, "fore",
        [kept] * 6 + [shape(2 * modes, width, F32), shape(2 * modes, width)],
        ext_full, (count, width),
    )(value, gate_k1, gate_q1, gate_k2, gate_q2, gate_k3, rim_fore, short_filter, rates, back_carry,
      fwd, inv, med)
    z1, x1, u2, z2, x2, u3 = hold(got[:6])
    carry, send = got[6:]

    def long_filter(start):
        return call(long_filter_kernel, "long_filter", filters, (count, groups))(
            fwd32, residues, after(rates, start)
        )

    def back_near(start, lng):
        return call(back_near_kernel, "back_near", wide)(
            grad_out, gate_q3, fwd, inv, Held(after(lng, start))
        )

    def fore_near(start, lng, _):
        return call(fore_near_kernel, "fore_near", wide)(u3, fwd, inv, Held(after(lng, start)))

    states, (_, du3_near, z3_near) = scan_states(
        carry, send, rates, count, place, ctx, (long_filter, back_near, fore_near)
    )

    grad_k3, grad_q2, dz2, du2_near, rim_back_send = call(
        back_long_kernel, "back_long", [full] * 2 + [kept, wide, shape(rim + 16, width)], (count, width)
    )(Held(du3_near), states, rates, residues, x2, z2, gate_k3, gate_q2, gate_k2, gate_q1, fwd, inv, med)
    dz2, du2_near = Held(dz2), Held(du2_near)
    rim_back = shifted(rim_back_send, -1)

    terms = call(medium_terms_kernel, "medium_terms", shape(rim, groups, F32), (2 * count, groups))(
        dz2, u2, rim_fore, fwd, lag
    )
    mixed, grad_q3 = call(fore_long_kernel, "fore_long", [full] * 2, (count, width))(
        Held(z3_near), states, rates, residues, gate_q3, grad_out
    )
    terms = after(terms, mixed)

    packet = (ctx, 8, groups // 2 + LANES)
    grad_k2, grad_q1, grad_k1, grad_value, out = call(
        back_short_kernel, "back_short",
        [full] * 4 + [jax.ShapeDtypeStruct(packet, BF)], ext_full, ext_full, packet,
    )(du2_near, rim_back, x1, z1, gate_k2, gate_q1, gate_k1, value, rim_fore, short_filter, terms,
      fwd, inv, med)

    spread, part = call(
        first_sum_kernel, "first_sum",
        [jax.ShapeDtypeStruct((tp, 8, groups // 2), BF), shape(8, packet[2], F32)],
    )(exchanged(out, "ctx"))
    piece = call(second_sum_kernel, "second_sum", jax.ShapeDtypeStruct(packet, BF))(
        exchanged(spread, "tp"), part
    )
    grad_short, grad_medium = call(
        collect_kernel, "collect", [shape(taps, width, F32), shape(rim, groups, F32)]
    )(exchanged(piece, "ctx"))
    return (
        mixed, grad_value, grad_q1, grad_k1, grad_q2, grad_k2, grad_q3, grad_k3, grad_short, grad_medium,
    )


def solution(mesh):
    data = P("ctx", "tp")
    return jax.shard_map(
        on_device,
        mesh=mesh,
        in_specs=(data,) * 8 + (P(None, "tp"), P(), P(), P()),
        out_specs=(data,) * 8 + (P(None, "tp"), P()),
        check_vma=False,
    )
```

time: 116 us -> 97.2 us (0.84); the launches traced: 114 us -> 96.8 us
  blocking collectives: 0 us -> 42 us
  starting transfers between devices: 44.9 us -> 17.9 us
  local copies, waits for them, and re-layouts: 15.3 us -> 0.74 us
  Pallas kernels: 37.5 us -> 28.6 us
  waiting for transfers between devices: 12.6 us -> 6.76 us
  other arithmetic: 2.07 us -> 0 us
    all_to_all x0 -> x3, blocking collectives: none -> 42 us  [exchanged(): return lax.all_to_all(block, axis, 0, 0)]
    all_to_all x3 -> x0, starting transfers between devices: 22.3 us -> none  [the longest x1 8.79 us: on_device(): got = lax.all_to_all(send, 'ctx', 0, 0)]
    unnamed x122 -> x10, local copies, waits for them, and re-layouts: 12.4 us -> 0.74 us
    all_to_all x3 -> x0, waiting for transfers between devices: 10.8 us -> none  [the longest x1 4.39 us: on_device(): medium = jnp.sum(lax.all_to_all(spread, 'tp', 0, 0), axis=0)]
    pallas_call x9 -> x17, Pallas kernels: 37.5 us -> 28.6 us  [run(): pl.pallas_call(body, name=name, in_specs=[place(a, k) for k, a in enumera...]
    ppermute x14 -> x7, starting transfers between devices: 17 us -> 8.91 us  [swapped(): return lax.ppermute(block, 'ctx', [(i, i ^ distance) for i in range(size)])]
    ppermute x14 -> x7, waiting for transfers between devices: 0.21 us -> 5.98 us  [swapped(): return lax.ppermute(block, 'ctx', [(i, i ^ distance) for i in range(size)])]
    ppermute x2, starting transfers between devices: 5.66 us -> 8.97 us  [shifted(): return lax.ppermute(block, 'ctx', route)]
  transfers between devices with their start and end apart: 19 -> 9, of which waited for: 5 -> 4; matrix products, arithmetic and copies ran while one was open for 4% -> 0% of each run, Pallas kernels for 14% -> 13%
where the time goes in v2:
time: 97.2 us; the launch traced here: 96.8 us
  blocking collectives  42 us (43%)
  Pallas kernels  28.6 us (29%)
  starting transfers between devices  17.9 us (18%)
  waiting for transfers between devices  6.76 us (7%)
    all_to_all x3, blocking collectives, exchanged(): return lax.all_to_all(block, axis, 0, 0)  42 us
    pallas_call x17, Pallas kernels, run(): pl.pallas_call(body, name=name, in_specs=[place(a, k) for k, a in enumera...  28.6 us
    ppermute x2, starting transfers between devices, shifted(): return lax.ppermute(block, 'ctx', route)  8.97 us
    ppermute x7, starting transfers between devices, swapped(): return lax.ppermute(block, 'ctx', [(i, i ^ distance) for i in range(size)])  8.91 us
    ppermute x7, waiting for transfers between devices, swapped(): return lax.ppermute(block, 'ctx', [(i, i ^ distance) for i in range(size)])  5.98 us
  transfers between devices with their start and end apart: 9, of which 4 were waited for; matrix products, arithmetic and copies ran while one was open for 0% of the time, Pallas kernels for 13%

profile of v2, /device:TPU:1, one launch (start us, length us, event | category | flops | bytes accessed | tf_op | source)
XLA Modules:
  0.0 96.8 jit_solution(18361504652947694136)
XLA Ops:
  0.6 0.0 copy-start.2
  0.7 0.7 copy-done.2
  1.4 0.0 copy-start.4
  1.4 2.1 %fore_rim.1 = (bf16[144,1024]{1,0:T(8,128)(2,1)S(1)}, bf16[256,1024]{1,0:T(8,128)(2,1)S(1)}, bf16[256,1024]{1,0:T(8,128)(2,1)S(1)}, bf16[256,1024]{1,0:T(8,128)(2,1)S(1)}, bf16[256,1024]{1,0:T(8,128)(2,1)S(1)}) custom-call(s32[1]{0:T(128)} %bitcast.refs_0_, bf16[256,1024]{1,0:T(8,128)(2,1)} %refs_1_.6, bf16[256,1024]{1,0:T(8,128)(2,1)} %refs_2_.5, ...), custom_call_target="tpu_custom_call" | custom-call | tf_op jit(solution)/shard_map/fore_rim/pallas_call | solution.py:533
  3.5 0.0 copy-start
  3.5 0.0 copy-start.3
  3.5 4.5 %collective-permute-start = (bf16[144,1024]{1,0:T(8,128)(2,1)S(1)}, bf16[144,1024]{1,0:T(8,128)(2,1)S(1)}, u32[]{:S(2)}, u32[]{:S(2)}) collective-permute-start(bf16[144,1024]{1,0:T(8,128)(2,1)S(1)} %get-tuple-element.67), channel_id=1, source_target_pairs={{0,8},{8,16},{16,24},{24,32},{32,40},{40,48},{48,56},{56,64},{64,7... | collective-permute-start | bytes 884744 | tf_op jit(solution)/shard_map/ppermute | solution.py:417
  8.0 0.0 copy-done.4
  8.0 2.6 %medium_filter.1 = (f32[3,256,512]{2,1,0:T(8,128)S(1)}, f32[512,256]{1,0:T(8,128)S(1)}, bf16[512,512]{1,0:T(8,128)(2,1)S(1)}, bf16[256,512]{1,0:T(8,128)(2,1)S(1...) custom-call(f32[512,256]{1,0:T(8,128)} %constant.14.clone.refs_0_, ...), custom_call_target="tpu_custom_call" | custom-call | tf_op jit(solution)/shard_map/medium_filter/pallas_call | solution.py:533
  10.7 0.0 copy-done
  10.7 1.8 %back_carry.1.refs_9_ = f32[16,1024]{1,0:T(8,128)S(1)} custom-call(bf16[256,1024]{1,0:T(8,128)(2,1)S(1)} %get-tuple-element.68.refs_0_.refs_5_, bf16[256,1024]{1,0:T(8,128)(2,1)S(1)} %get-tuple-element.69.refs_1_.refs_4_, f32[16,512]{1,0:T(8,128)S(1)} %copy-done), custom_call_target="tpu_custom_call" | custom-call | tf_op jit(solution)/shard_map/back_carry/pallas_call | solution.py:533
  12.5 0.0 collective-permute-done.refs_6_.refs_2_.refs_8_
  12.5 0.0 copy-done.3
  12.5 0.0 copy-start.1
  12.6 5.0 %fore.1 = (bf16[256,1024]{1,0:T(8,128)(2,1)S(1)}, bf16[256,1024]{1,0:T(8,128)(2,1)S(1)}, bf16[256,1024]{1,0:T(8,128)(2,1)S(1)}, bf16[256,1024]{1,0:T(8,128)(2,1)...) custom-call(bf16[256,1024]{1,0:T(8,128)(2,1)S(1)} %get-tuple-element, ...), custom_call_target="tpu_custom_call" | custom-call | tf_op jit(solution)/shard_map/fore/pallas_call | solution.py:533
  17.6 0.1 collective-permute-start.1
  17.7 0.0 copy-done.1
  17.7 1.9 %long_filter.1.refs_4_.refs_3_ = f32[3,256,512]{2,1,0:T(8,128)S(1)} custom-call(f32[512,256]{1,0:T(8,128)S(1)} %get-tuple-element.74.refs_0_, f32[16,512]{1,0:T(8,128)S(1)} %copy-done.1, f32[16,512]{1,0:T(8,128)S(1)} %copy-done), custom_call_target="tpu_custom_call" | custom-call | tf_op jit(solution)/shard_map/long_filter/pallas_call | solution.py:533
  19.6 0.0 collective-permute-done.1.refs_3_
  19.6 0.1 scan1.1
  19.7 3.0 %collective-permute-start.4 = (bf16[32,1024]{1,0:T(8,128)(2,1)S(1)}, bf16[32,1024]{1,0:T(8,128)(2,1)S(1)}, u32[]{:S(2)}, u32[]{:S(2)}) collective-permute-start(bf16[32,1024]{1,0:T(8,128)(2,1)S(1)} %get-tuple-element.80), channel_id=1, source_target_pairs={{0,48},{8,56},{16,32},{24,40},{32,16},{40,24},{48,0},{56,8},{64,11... | collective-permute-start | bytes 196616 | tf_op jit(solution)/shard_map/ppermute | solution.py:411
  22.7 0.5 collective-permute-start.3
  23.2 0.2 collective-permute-start.2
  23.4 0.9 back_near.1.refs_0_
  24.3 0.9 collective-permute-done.4.refs_5_
  25.3 2.1 %collective-permute-done.3.refs_4_ = bf16[32,1024]{1,0:T(8,128)(2,1)S(1)} collective-permute-done((bf16[32,1024]{1,0:T(8,128)(2,1)S(1)}, bf16[32,1024]{1,0:T(8,128)(2,1)S(1)}, u32[]{:S(2)}, u32[]{:S(2)}) %collective-permute-start.3) | collective-permute-done | bytes 65568 | tf_op jit(solution)/shard_map/ppermute | solution.py:411
  27.3 0.0 collective-permute-done.2.refs_3_
  27.3 0.2 scan2.1
  27.5 4.4 %collective-permute-start.7 = (bf16[32,1024]{1,0:T(8,128)(2,1)S(1)}, bf16[32,1024]{1,0:T(8,128)(2,1)S(1)}, u32[]{:S(2)}, u32[]{:S(2)}) collective-permute-start(bf16[32,1024]{1,0:T(8,128)(2,1)S(1)} %get-tuple-element.84), channel_id=1, source_target_pairs={{0,192},{8,200},{16,208},{24,216},{32,224},{40,232},{48,240},{56,2... | collective-permute-start | bytes 196616 | tf_op jit(solution)/shard_map/ppermute | solution.py:411
  31.9 0.3 collective-permute-start.6
  32.3 0.3 collective-permute-start.5
  32.6 0.9 fore_near.1.refs_0_
  33.5 0.0 collective-permute-done.7.refs_5_
  33.6 3.0 %collective-permute-done.6.refs_4_ = bf16[32,1024]{1,0:T(8,128)(2,1)S(1)} collective-permute-done((bf16[32,1024]{1,0:T(8,128)(2,1)S(1)}, bf16[32,1024]{1,0:T(8,128)(2,1)S(1)}, u32[]{:S(2)}, u32[]{:S(2)}) %collective-permute-start.6) | collective-permute-done | bytes 65568 | tf_op jit(solution)/shard_map/ppermute | solution.py:411
  36.5 0.0 collective-permute-done.5.refs_3_
  36.5 0.1 scan8.1.refs_1_
  36.6 3.7 %back_long.1 = (bf16[256,1024]{1,0:T(8,128)(2,1)}, bf16[256,1024]{1,0:T(8,128)(2,1)}, bf16[256,1024]{1,0:T(8,128)(2,1)S(1)}, f32[256,1024]{1,0:T(8,128)S(1)}, bf16[144,1024]{1,0:T(8,128)(2,1)S(1)}) custom-call(f32[256,1024]{1,0:T(8,128)S(1)} %back_near.1.refs_0_, f32[32,1024]{1,0:T(8,128)S(1)} %scan8.1.refs_1_, f32[16,512]{1,0:T(8,128)S(1)} %copy-done, ...), custom_call_target="tpu_custom_call" | custom-call | tf_op jit(solution)/shard_map/back_long/pallas_call | solution.py:533
  40.3 4.5 %collective-permute-start.8 = (bf16[144,1024]{1,0:T(8,128)(2,1)S(1)}, bf16[144,1024]{1,0:T(8,128)(2,1)S(1)}, u32[]{:S(2)}, u32[]{:S(2)}) collective-permute-start(bf16[144,1024]{1,0:T(8,128)(2,1)S(1)} %get-tuple-element.93), channel_id=1, source_target_pairs={{8,0},{16,8},{24,16},{32,24},{40,32},{48,40},{56,48},{64,56},{72,6... | collective-permute-start | bytes 884744 | tf_op jit(solution)/shard_map/ppermute | solution.py:417
  44.8 2.7 %fore_long.1 = (bf16[256,1024]{1,0:T(8,128)(2,1)}, bf16[256,1024]{1,0:T(8,128)(2,1)}) custom-call(f32[256,1024]{1,0:T(8,128)S(1)} %fore_near.1.refs_0_, f32[32,1024]{1,0:T(8,128)S(1)} %scan8.1.refs_1_, f32[16,512]{1,0:T(8,128)S(1)} %copy-done, f32[16,512]{1,0:T(8,128)S(1)} %copy-done.1, bf16[256,1024]{1,0:T(8,128)(2,1)S(1)} %get-tuple-element.69.refs_1_.refs_4_, ...), custom_call_target="tpu_custom_call" | custom-call | tf_op jit(solution)/shard_map/fore_long/pallas_call | solution.py:533
  47.5 1.2 %medium_terms.1.refs_10_ = f32[128,512]{1,0:T(8,128)S(1)} custom-call(bf16[256,1024]{1,0:T(8,128)(2,1)S(1)} %get-tuple-element.96.refs_0_, bf16[256,1024]{1,0:T(8,128)(2,1)S(1)} %get-tuple-element.97.refs_1_, bf16[144,1024]{1,0:T(8,128)(2,1)S(1)} %collective-permute-done.refs_6_.refs_2_.refs_8_, ...), custom_call_target="tpu_custom_call" | custom-call | tf_op jit(solution)/shard_map/medium_terms/pallas_call | solution.py:533
  48.7 0.8 collective-permute-done.8.refs_1_
  49.5 4.5 %back_short.1 = (bf16[256,1024]{1,0:T(8,128)(2,1)}, bf16[256,1024]{1,0:T(8,128)(2,1)}, bf16[256,1024]{1,0:T(8,128)(2,1)}, bf16[256,1024]{1,0:T(8,128)(2,1)}, bf16[32,8,384]{2,1,0:T(8,128)(2,1)S(1)}) custom-call(f32[256,1024]{1,0:T(8,128)S(1)} %get-tuple-element.92.refs_0_, bf16[144,1024]{1,0:T(8,128)(2,1)S(1)} %collective-permute-done.8.refs_1_, ...), custom_call_target="tpu_custom_call" | custom-call | tf_op jit(solution)/shard_map/back_short/pallas_call | solution.py:533
  54.0 13.8 %all_to_all.15.refs_0_ = bf16[32,8,384]{2,1,0:T(8,128)(2,1)S(1)} all-to-all(bf16[32,8,384]{2,1,0:T(8,128)(2,1)S(1)} %get-tuple-element.107), channel_id=1, replica_groups=mesh['ctx'=32,'tp'=8] {'ctx'}, dimensions={0} | all-to-all | bytes 393216 | tf_op jit(solution)/shard_map/all_to_all | solution.py:421
  67.9 14.8 %all_to_all.16.refs_0_ = bf16[8,8,256]{2,1,0:T(8,128)(2,1)S(1)} all-to-all(bf16[8,8,256]{2,1,0:T(8,128)(2,1)S(1)} %get-tuple-element.108), channel_id=1, replica_groups=mesh['ctx'=32,'tp'=8] {'tp'}, dimensions={0} | all-to-all | bytes 65536 | tf_op jit(solution)/shard_map/all_to_all | solution.py:421
  82.8 13.3 %all_to_all.17.refs_0_ = bf16[32,8,384]{2,1,0:T(8,128)(2,1)S(1)} all-to-all(bf16[32,8,384]{2,1,0:T(8,128)(2,1)S(1)} %second_sum.1), channel_id=1, replica_groups=mesh['ctx'=32,'tp'=8] {'ctx'}, dimensions={0} | all-to-all | bytes 393216 | tf_op jit(solution)/shard_map/all_to_all | solution.py:421
  96.1 0.7 collect.1
  (2 shorter events, 0.1 us)
Async XLA Ops:
  0.6 0.7 copy-start.2
  1.4 6.7 %copy-start.4 = (bf16[128,512]{1,0:T(8,128)(2,1)S(1)}, bf16[128,512]{1,0:T(8,128)(2,1)}, u32[]{:S(2)}) copy-start(bf16[128,512]{1,0:T(8,128)(2,1)} %refs_1_.7) | copy-start | bytes 393220
  3.5 7.2 %copy-start = (f32[16,512]{1,0:T(8,128)S(1)}, f32[16,512]{1,0:T(8,128)}, u32[]{:S(2)}) copy-start(f32[16,512]{1,0:T(8,128)} %refs_2_.9) | copy-start | bytes 98308
  3.5 9.0 %copy-start.3 = (bf16[7,1024]{1,0:T(8,128)(2,1)S(1)}, bf16[7,1024]{1,0:T(8,128)(2,1)}, u32[]{:S(2)}) copy-start(bf16[7,1024]{1,0:T(8,128)(2,1)} %refs_9_.1) | copy-start | bytes 43012
  3.5 9.0 %collective-permute-start = (bf16[144,1024]{1,0:T(8,128)(2,1)S(1)}, bf16[144,1024]{1,0:T(8,128)(2,1)S(1)}, u32[]{:S(2)}, u32[]{:S(2)}) collective-permute-start(bf16[144,1024]{1,0:T(8,128)(2,1)S(1)} %get-tuple-element.67), channel_id=1, source_target_pairs={{0,8},{8,16},{16,24},{24,32},{32,40},{40,48},{48,56},{56,64},{64,7... | collective-permute-start | bytes 884744 | tf_op jit(solution)/shard_map/ppermute | solution.py:417
  12.5 5.2 %copy-start.1 = (f32[16,512]{1,0:T(8,128)S(1)}, f32[16,512]{1,0:T(8,128)}, u32[]{:S(2)}) copy-start(f32[16,512]{1,0:T(8,128)} %refs_3_.6) | copy-start | bytes 98308
  17.6 2.0 %collective-permute-start.1 = (bf16[32,1024]{1,0:T(8,128)(2,1)S(1)}, bf16[32,1024]{1,0:T(8,128)(2,1)S(1)}, u32[]{:S(2)}, u32[]{:S(2)}) collective-permute-start(bf16[32,1024]{1,0:T(8,128)(2,1)S(1)} %get-tuple-element.75), channel_id=1, source_target_pairs={{0,8},{8,0},{16,24},{24,16},{32,40},{40,32},{48,56},{56,48},{64,72... | collective-permute-start | bytes 196616 | tf_op jit(solution)/shard_map/ppermute | solution.py:411
  19.7 5.6 %collective-permute-start.4 = (bf16[32,1024]{1,0:T(8,128)(2,1)S(1)}, bf16[32,1024]{1,0:T(8,128)(2,1)S(1)}, u32[]{:S(2)}, u32[]{:S(2)}) collective-permute-start(bf16[32,1024]{1,0:T(8,128)(2,1)S(1)} %get-tuple-element.80), channel_id=1, source_target_pairs={{0,48},{8,56},{16,32},{24,40},{32,16},{40,24},{48,0},{56,8},{64,11... | collective-permute-start | bytes 196616 | tf_op jit(solution)/shard_map/ppermute | solution.py:411
  22.7 4.6 %collective-permute-start.3 = (bf16[32,1024]{1,0:T(8,128)(2,1)S(1)}, bf16[32,1024]{1,0:T(8,128)(2,1)S(1)}, u32[]{:S(2)}, u32[]{:S(2)}) collective-permute-start(bf16[32,1024]{1,0:T(8,128)(2,1)S(1)} %get-tuple-element.80), channel_id=1, source_target_pairs={{0,32},{8,40},{16,48},{24,56},{32,0},{40,8},{48,16},{56,24},{64,96... | collective-permute-start | bytes 196616 | tf_op jit(solution)/shard_map/ppermute | solution.py:411
  23.2 4.1 %collective-permute-start.2 = (bf16[32,1024]{1,0:T(8,128)(2,1)S(1)}, bf16[32,1024]{1,0:T(8,128)(2,1)S(1)}, u32[]{:S(2)}, u32[]{:S(2)}) collective-permute-start(bf16[32,1024]{1,0:T(8,128)(2,1)S(1)} %get-tuple-element.80), channel_id=1, source_target_pairs={{0,16},{8,24},{16,0},{24,8},{32,48},{40,56},{48,32},{56,40},{64,80... | collective-permute-start | bytes 196616 | tf_op jit(solution)/shard_map/ppermute | solution.py:411
  27.5 6.1 %collective-permute-start.7 = (bf16[32,1024]{1,0:T(8,128)(2,1)S(1)}, bf16[32,1024]{1,0:T(8,128)(2,1)S(1)}, u32[]{:S(2)}, u32[]{:S(2)}) collective-permute-start(bf16[32,1024]{1,0:T(8,128)(2,1)S(1)} %get-tuple-element.84), channel_id=1, source_target_pairs={{0,192},{8,200},{16,208},{24,216},{32,224},{40,232},{48,240},{56,2... | collective-permute-start | bytes 196616 | tf_op jit(solution)/shard_map/ppermute | solution.py:411
  31.9 4.6 %collective-permute-start.6 = (bf16[32,1024]{1,0:T(8,128)(2,1)S(1)}, bf16[32,1024]{1,0:T(8,128)(2,1)S(1)}, u32[]{:S(2)}, u32[]{:S(2)}) collective-permute-start(bf16[32,1024]{1,0:T(8,128)(2,1)S(1)} %get-tuple-element.84), channel_id=1, source_target_pairs={{0,128},{8,136},{16,144},{24,152},{32,160},{40,168},{48,176},{56,1... | collective-permute-start | bytes 196616 | tf_op jit(solution)/shard_map/ppermute | solution.py:411
  32.3 4.3 %collective-permute-start.5 = (bf16[32,1024]{1,0:T(8,128)(2,1)S(1)}, bf16[32,1024]{1,0:T(8,128)(2,1)S(1)}, u32[]{:S(2)}, u32[]{:S(2)}) collective-permute-start(bf16[32,1024]{1,0:T(8,128)(2,1)S(1)} %get-tuple-element.84), channel_id=1, source_target_pairs={{0,64},{8,72},{16,80},{24,88},{32,96},{40,104},{48,112},{56,120},{... | collective-permute-start | bytes 196616 | tf_op jit(solution)/shard_map/ppermute | solution.py:411
  40.3 9.2 %collective-permute-start.8 = (bf16[144,1024]{1,0:T(8,128)(2,1)S(1)}, bf16[144,1024]{1,0:T(8,128)(2,1)S(1)}, u32[]{:S(2)}, u32[]{:S(2)}) collective-permute-start(bf16[144,1024]{1,0:T(8,128)(2,1)S(1)} %get-tuple-element.93), channel_id=1, source_target_pairs={{8,0},{16,8},{24,16},{32,24},{40,32},{48,40},{56,48},{64,56},{72,6... | collective-permute-start | bytes 884744 | tf_op jit(solution)/shard_map/ppermute | solution.py:417

commit v3 on v2

--- a/solution.py
+++ b/solution.py
@@ -11,7 +11,9 @@
 LANES = 128
 VMEM_LIMIT = 28 * 1024 * 1024
 BLOCK = 256
-UNROLL = 4
+WIDE = 512
+UNROLL = 16
+LATE = 99
 
 
 def dft_tables(count):
@@ -117,7 +119,10 @@
     return total
 
 
-def fore_rim_kernel(flow, place_ref, value_ref, k1_ref, q1_ref, k2_ref, filt_ref, out_ref, ext):
+def fore_rim_kernel(
+    flow, place_ref, filt_ref, value_ref, k1_ref, q1_ref, k2_ref, out_ref, *refs
+):
+    ext = refs[-1]
     del place_ref
     count, width = value_ref.shape
     rim = out_ref.shape[0] - 16
@@ -188,7 +193,7 @@
     count, width = value_ref.shape
     modes, groups = rates_ref.shape
     rim = rim_ref.shape[0] - 16
-    for lanes, own in parts(width, groups):
+    for lanes, own in parts(width, groups, WIDE):
         u1 = mul(k1_ref[:, lanes], value_ref[:, lanes]).astype(BF)
         ext[0:16, lanes] = rim_ref[rim : rim + 16, lanes].astype(F32)
         ext[16:, lanes] = u1.astype(F32)
@@ -214,9 +219,9 @@
 
 
 def back_long_kernel(
-    flow, near_ref, state_ref, rates_ref, residues_ref, x2_ref, z2_ref, k3_ref, q2_ref, k2_ref, q1_ref,
+    near_ref, state_ref, rates_ref, residues_ref, k3_ref, q2_ref, k2_ref, q1_ref,
     fwd_ref, inv_ref, med_ref,
-    gk3_ref, gq2_ref, dz2_ref, du2_ref, rim_ref, far,
+    du3_ref, dz2_ref, spec_ref, rim_ref, far,
 ):
     count, width = near_ref.shape
     modes, groups = rates_ref.shape
@@ -225,19 +230,29 @@
         far_field(
             state_ref[0:modes, lanes], rates_ref[:, own], residues_ref[:, own], far, True, 1, lanes
         )
-    for block, (lanes, own) in enumerate(parts(width, groups)):
+    for lanes, own in parts(width, groups, WIDE):
         du3 = near_ref[:, lanes] + far[:, lanes]
+        du3_ref[:, lanes] = du3
+        dx2 = mul(du3, k3_ref[:, lanes]).astype(BF)
+        dz2 = mul(dx2, q2_ref[:, lanes]).astype(BF)
+        dz2_ref[:, lanes] = dz2
+        spec = spec_conj(dot(fwd_ref[:, :count], dz2), filt_of(med_ref, own))
+        spec_ref[:, lanes] = spec
+        rim_ref[0:rim, lanes] = dz2[0:rim]
+        dx1 = mul(dot(inv_ref[0:16, :], spec), k2_ref[0:16, lanes]).astype(BF)
+        rim_ref[rim : rim + 16, lanes] = mul(dx1, q1_ref[0:16, lanes]).astype(BF)
+
+
+def back_rest_kernel(
+    flow, du3_ref, spec_ref, x2_ref, z2_ref, k3_ref, inv_ref, gk3_ref, gq2_ref, du2_ref
+):
+    width = du3_ref.shape[1]
+    for block, (lanes, _) in enumerate(parts(width, width)):
+        du2_ref[:, lanes] = dot(inv_ref[...], spec_ref[:, lanes])
+        du3 = du3_ref[:, lanes]
         gk3_ref[:, lanes] = mul(du3, x2_ref[:, lanes]).astype(BF)
         dx2 = mul(du3, k3_ref[:, lanes]).astype(BF)
         gq2_ref[:, lanes] = mul(dx2, z2_ref[:, lanes]).astype(BF)
-        dz2 = mul(dx2, q2_ref[:, lanes]).astype(BF)
-        dz2_ref[:, lanes] = dz2
-        spec = dot(fwd_ref[:, :count], dz2)
-        du2 = dot(inv_ref[...], spec_conj(spec, filt_of(med_ref, own)))
-        du2_ref[:, lanes] = du2
-        rim_ref[0:rim, lanes] = dz2[0:rim]
-        dx1 = mul(du2[0:16], k2_ref[0:16, lanes]).astype(BF)
-        rim_ref[rim : rim + 16, lanes] = mul(dx1, q1_ref[0:16, lanes]).astype(BF)
         flow.flush(block)
 
 
@@ -430,8 +445,19 @@
 
 
 class Big:
-    def __init__(self, array, block=BLOCK, kept=False):
-        self.array, self.block, self.kept = array, block, kept
+    def __init__(self, array, block=BLOCK, kept=False, head=0):
+        self.array, self.block, self.kept, self.head = array, block, kept, head
+
+    def count(self):
+        return len(self.lanes()) * (2 if self.head else 1)
+
+    def boxes(self, piece):
+        lead = (slice(None),) * (len(self.array.shape) - 1)
+        lanes = (self.lanes()[piece],)
+        if not self.head:
+            return [(piece, lead + lanes)]
+        top = (slice(0, self.head),) + lanes
+        return [(piece, (slice(self.head, self.array.shape[0]),) + lanes), (LATE, top)]
 
     def lanes(self):
         width = self.array.shape[-1]
@@ -449,10 +475,10 @@
         for piece in range(max([len(a.lanes()) for a in arrays], default=0)):
             for source, target, array in zip(sources, targets, arrays):
                 if piece < len(array.lanes()):
-                    at = (slice(None),) * (len(array.array.shape) - 1) + (array.lanes()[piece],)
-                    copy = pltpu.make_async_copy(source.at[at], target.at[at], sems.at[count])
-                    self.copies.setdefault(piece, []).append(copy)
-                    count += 1
+                    for key, at in array.boxes(piece):
+                        copy = pltpu.make_async_copy(source.at[at], target.at[at], sems.at[count])
+                        self.copies.setdefault(key, []).append(copy)
+                        count += 1
 
     def start(self, piece):
         for copy in self.copies.get(piece, []):
@@ -466,7 +492,7 @@
 class Flow:
     def __init__(self, loads, stores):
         self.loads, self.stores = loads, stores
-        for piece in loads.copies:
+        for piece in sorted(loads.copies):
             loads.start(piece)
 
     def ready(self, piece):
@@ -517,6 +543,7 @@
             for k, ref in zip(at_out, held_out):
                 results[k] = ref
             kernel(Flow(loads, stores), *ins, *results, *own)
+            loads.wait(LATE)
             for piece in stores.copies:
                 stores.wait(piece)
 
@@ -529,7 +556,7 @@
         sems = []
         if big_in or big_out:
             for group in (big_in, big_out):
-                sems.append(pltpu.SemaphoreType.DMA((max(1, sum(len(a.lanes()) for a in group)),)))
+                sems.append(pltpu.SemaphoreType.DMA((max(1, sum(a.count() for a in group)),)))
         got = pl.pallas_call(
             body,
             name=name,
@@ -554,9 +581,10 @@
     group = 1
     done = []
     for fan, work in zip((2, 4, 4), works):
-        others = [swapped(send, d * group) for d in range(1, fan)]
-        done.append(work(send, *done))
-        total = after(total, done[-1])
+        others = {d: swapped(send, d * group) for d in (1, 3, 2)[: fan - 1]}
+        others = [others[d] for d in range(1, fan)]
+        done.append(work and work(send, *done))
+        total = after(total, done[-1]) if work else total
         last = group * fan >= size
         outs = [shape(modes2, width, F32)]
         if not last:
@@ -587,9 +615,12 @@
     fwd = jnp.asarray(forward, BF)
     inv = jnp.asarray(backward[:count], BF)
     lag = jnp.asarray(backward[(-np.arange(rim)) % (2 * count)], BF)
-    value, gate_q1, gate_k1, gate_q2, gate_k2, gate_q3, gate_k3, grad_out = [
-        Big(a, kept=True)
-        for a in (value, gate_q1, gate_k1, gate_q2, gate_k2, gate_q3, gate_k3, grad_out)
+    head = count - rim - 16
+    value, gate_q1, gate_k1, gate_k2 = [
+        Big(a, kept=True, head=head) for a in (value, gate_q1, gate_k1, gate_k2)
+    ]
+    gate_q2, gate_q3, gate_k3, grad_out = [
+        Big(a, kept=True) for a in (gate_q2, gate_q3, gate_k3, grad_out)
     ]
     tables = [Big(t, t.shape[1], kept=True) for t in (fwd32, fwd, inv, lag)]
     full, ext_full = Big(shape(count, width)), (count + 16, width)
@@ -601,8 +632,8 @@
 
     rim_send, *got = call(
         fore_rim_kernel, "fore_rim", shape(rim + 16, width), (rim + 16, width), scalars=1
-    )(place, value, gate_k1, gate_q1, gate_k2, short_filter)
-    value, gate_k1, gate_q1, gate_k2 = hold(got)
+    )(place, Big(short_filter, width, kept=True), value, gate_k1, gate_q1, gate_k2)
+    short_filter, value, gate_k1, gate_q1, gate_k2 = hold(got)
     rim_fore = shifted(rim_send, 1)
     got = call(medium_filter_kernel, "medium_filter", filters)(
         tables[0], medium_filter, *tables[1:], grad_out, gate_q3, gate_q2, gate_k3
@@ -621,28 +652,33 @@
     z1, x1, u2, z2, x2, u3 = hold(got[:6])
     carry, send = got[6:]
 
-    def long_filter(start):
-        return call(long_filter_kernel, "long_filter", filters, (count, groups))(
+    def long_side(start, _):
+        lng = call(long_filter_kernel, "long_filter", filters, (count, groups))(
             fwd32, residues, after(rates, start)
         )
-
-    def back_near(start, lng):
-        return call(back_near_kernel, "back_near", wide)(
-            grad_out, gate_q3, fwd, inv, Held(after(lng, start))
+        return lng, call(back_near_kernel, "back_near", wide)(
+            grad_out, gate_q3, fwd, inv, Held(lng)
         )
 
-    def fore_near(start, lng, _):
-        return call(fore_near_kernel, "fore_near", wide)(u3, fwd, inv, Held(after(lng, start)))
-
-    states, (_, du3_near, z3_near) = scan_states(
-        carry, send, rates, count, place, ctx, (long_filter, back_near, fore_near)
-    )
-
-    grad_k3, grad_q2, dz2, du2_near, rim_back_send = call(
-        back_long_kernel, "back_long", [full] * 2 + [kept, wide, shape(rim + 16, width)], (count, width)
-    )(Held(du3_near), states, rates, residues, x2, z2, gate_k3, gate_q2, gate_k2, gate_q1, fwd, inv, med)
-    dz2, du2_near = Held(dz2), Held(du2_near)
+    def fore_near(start, _, sides):
+        return call(fore_near_kernel, "fore_near", wide)(
+            u3, fwd, inv, Held(after(sides[0], start))
+        )
+
+    states, (_, (lng, du3_near), z3_near) = scan_states(
+        carry, send, rates, count, place, ctx, (None, long_side, fore_near)
+    )
+
+    du3, dz2, spec, rim_back_send = call(
+        back_long_kernel, "back_long",
+        [wide, kept, Held(shape(2 * count, width)), shape(rim + 16, width)], (count, width),
+    )(Held(du3_near), states, rates, residues, gate_k3, gate_q2, gate_k2, gate_q1, fwd, inv, med)
+    dz2 = Held(dz2)
     rim_back = shifted(rim_back_send, -1)
+    grad_k3, grad_q2, du2_near = call(back_rest_kernel, "back_rest", [full] * 2 + [wide])(
+        Held(du3), Held(spec), x2, z2, gate_k3, inv
+    )
+    du2_near = Held(du2_near)
 
     terms = call(medium_terms_kernel, "medium_terms", shape(rim, groups, F32), (2 * count, groups))(
         dz2, u2, rim_fore, fwd, lag

time: 97.2 us -> 93.5 us (0.962)
  waiting for transfers between devices: 6.76 us -> 5.44 us
    pallas_call x17 -> x18, Pallas kernels: 28.6 us -> 27.7 us  [run(): pl.pallas_call(body, name=name, in_specs=[place(a, k) for k, a in enumera...]
  transfers between devices with their start and end apart: 9 -> 9, of which waited for: 4 -> 3; matrix products, arithmetic and copies ran while one was open for 0% -> 0% of each run, Pallas kernels for 13% -> 14%
where the time goes in v3:
time: 93.5 us; the launch traced here: 93.2 us
  blocking collectives  41.4 us (44%)
  Pallas kernels  27.7 us (30%)
  starting transfers between devices  17.9 us (19%)
  waiting for transfers between devices  5.44 us (6%)
    all_to_all x3, blocking collectives, exchanged(): return lax.all_to_all(block, axis, 0, 0)  41.4 us
    pallas_call x18, Pallas kernels, run(): pl.pallas_call(body, name=name, in_specs=[place(a, k) for k, a in enumera...  27.7 us
    ppermute x2, starting transfers between devices, shifted(): return lax.ppermute(block, 'ctx', route)  9.35 us
    ppermute x7, starting transfers between devices, swapped(): return lax.ppermute(block, 'ctx', [(i, i ^ distance) for i in range(size)])  8.51 us
    ppermute x7, waiting for transfers between devices, swapped(): return lax.ppermute(block, 'ctx', [(i, i ^ distance) for i in range(size)])  5.44 us
  transfers between devices with their start and end apart: 9, of which 3 were waited for; matrix products, arithmetic and copies ran while one was open for 0% of the time, Pallas kernels for 14%

profile of v3, /device:TPU:1, one launch (start us, length us, event | category | flops | bytes accessed | tf_op | source)
XLA Modules:
  0.0 93.2 jit_solution(3327705867990557393)
XLA Ops:
  0.6 0.0 copy-start.2
  0.7 2.2 %fore_rim.1 = (bf16[144,1024]{1,0:T(8,128)(2,1)S(1)}, bf16[7,1024]{1,0:T(8,128)(2,1)S(1)}, bf16[256,1024]{1,0:T(8,128)(2,1)S(1)}, bf16[256,1024]{1,0:T(8,128)(2,...) custom-call(s32[1]{0:T(128)} %bitcast.refs_0_, bf16[7,1024]{1,0:T(8,128)(2,1)} %refs_1_.6, ...), custom_call_target="tpu_custom_call" | custom-call | tf_op jit(solution)/shard_map/fore_rim/pallas_call | solution.py:560
  2.9 0.0 copy-start
  2.9 4.5 %collective-permute-start = (bf16[144,1024]{1,0:T(8,128)(2,1)S(1)}, bf16[144,1024]{1,0:T(8,128)(2,1)S(1)}, u32[]{:S(2)}, u32[]{:S(2)}) collective-permute-start(bf16[144,1024]{1,0:T(8,128)(2,1)S(1)} %get-tuple-element.68), channel_id=1, source_target_pairs={{0,8},{8,16},{16,24},{24,32},{32,40},{40,48},{48,56},{56,64},{64,7... | collective-permute-start | bytes 884744 | tf_op jit(solution)/shard_map/ppermute | solution.py:432
  7.4 0.0 copy-done.2
  7.4 2.7 %medium_filter.1 = (f32[3,256,512]{2,1,0:T(8,128)S(1)}, f32[512,256]{1,0:T(8,128)S(1)}, bf16[512,512]{1,0:T(8,128)(2,1)S(1)}, bf16[256,512]{1,0:T(8,128)(2,1)S(1...) custom-call(f32[512,256]{1,0:T(8,128)} %constant.14.clone.refs_0_, ...), custom_call_target="tpu_custom_call" | custom-call | tf_op jit(solution)/shard_map/medium_filter/pallas_call | solution.py:560
  10.1 0.0 copy-done
  10.1 1.5 %back_carry.1.refs_9_ = f32[16,1024]{1,0:T(8,128)S(1)} custom-call(bf16[256,1024]{1,0:T(8,128)(2,1)S(1)} %get-tuple-element.70.refs_0_.refs_5_, bf16[256,1024]{1,0:T(8,128)(2,1)S(1)} %get-tuple-element.71.refs_1_.refs_4_, f32[16,512]{1,0:T(8,128)S(1)} %copy-done), custom_call_target="tpu_custom_call" | custom-call | tf_op jit(solution)/shard_map/back_carry/pallas_call | solution.py:560
  11.6 0.0 collective-permute-done.refs_6_.refs_2_.refs_8_
  11.6 0.0 copy-start.1
  11.6 4.2 %fore.1 = (bf16[256,1024]{1,0:T(8,128)(2,1)S(1)}, bf16[256,1024]{1,0:T(8,128)(2,1)S(1)}, bf16[256,1024]{1,0:T(8,128)(2,1)S(1)}, bf16[256,1024]{1,0:T(8,128)(2,1)...) custom-call(bf16[256,1024]{1,0:T(8,128)(2,1)S(1)} %get-tuple-element, ...), custom_call_target="tpu_custom_call" | custom-call | tf_op jit(solution)/shard_map/fore/pallas_call | solution.py:560
  15.9 0.1 collective-permute-start.1
  16.0 1.2 %collective-permute-done.1.refs_3_ = bf16[32,1024]{1,0:T(8,128)(2,1)S(1)} collective-permute-done((bf16[32,1024]{1,0:T(8,128)(2,1)S(1)}, bf16[32,1024]{1,0:T(8,128)(2,1)S(1)}, u32[]{:S(2)}, u32[]{:S(2)}) %collective-permute-start.1) | collective-permute-done | bytes 65568 | tf_op jit(solution)/shard_map/ppermute | solution.py:426
  17.2 0.1 scan1.1
  17.3 3.0 %collective-permute-start.4 = (bf16[32,1024]{1,0:T(8,128)(2,1)S(1)}, bf16[32,1024]{1,0:T(8,128)(2,1)S(1)}, u32[]{:S(2)}, u32[]{:S(2)}) collective-permute-start(bf16[32,1024]{1,0:T(8,128)(2,1)S(1)} %get-tuple-element.79), channel_id=1, source_target_pairs={{0,48},{8,56},{16,32},{24,40},{32,16},{40,24},{48,0},{56,8},{64,11... | collective-permute-start | bytes 196616 | tf_op jit(solution)/shard_map/ppermute | solution.py:426
  20.3 0.5 collective-permute-start.3
  20.8 0.2 collective-permute-start.2
  21.0 0.0 copy-done.1
  21.0 1.7 %long_filter.1.refs_4_.refs_3_ = f32[3,256,512]{2,1,0:T(8,128)S(1)} custom-call(f32[512,256]{1,0:T(8,128)S(1)} %get-tuple-element.76.refs_0_, f32[16,512]{1,0:T(8,128)S(1)} %copy-done.1, f32[16,512]{1,0:T(8,128)S(1)} %copy-done), custom_call_target="tpu_custom_call" | custom-call | tf_op jit(solution)/shard_map/long_filter/pallas_call | solution.py:560
  22.7 1.0 %back_near.1.refs_0_ = f32[256,1024]{1,0:T(8,128)S(1)} custom-call(bf16[256,1024]{1,0:T(8,128)(2,1)S(1)} %get-tuple-element.70.refs_0_.refs_5_, bf16[256,1024]{1,0:T(8,128)(2,1)S(1)} %get-tuple-element.71.refs_1_.refs_4_, bf16[512,512]{1,0:T(8,128)(2,1)S(1)} %get-tuple-element.72.refs_10_.refs_2_.refs_1_.refs_8_.refs_3_.refs_11_, ...), custom_call_target="tpu_custom_call" | custom-call | tf_op jit(solution)/shard_map/back_near/pallas_call | solution.py:560
  23.7 0.0 collective-permute-done.4.refs_5_
  23.7 1.2 %collective-permute-done.3.refs_4_ = bf16[32,1024]{1,0:T(8,128)(2,1)S(1)} collective-permute-done((bf16[32,1024]{1,0:T(8,128)(2,1)S(1)}, bf16[32,1024]{1,0:T(8,128)(2,1)S(1)}, u32[]{:S(2)}, u32[]{:S(2)}) %collective-permute-start.3) | collective-permute-done | bytes 65568 | tf_op jit(solution)/shard_map/ppermute | solution.py:426
  24.9 0.0 collective-permute-done.2.refs_3_
  24.9 0.2 scan2.1
  25.1 4.0 %collective-permute-start.7 = (bf16[32,1024]{1,0:T(8,128)(2,1)S(1)}, bf16[32,1024]{1,0:T(8,128)(2,1)S(1)}, u32[]{:S(2)}, u32[]{:S(2)}) collective-permute-start(bf16[32,1024]{1,0:T(8,128)(2,1)S(1)} %get-tuple-element.84), channel_id=1, source_target_pairs={{0,192},{8,200},{16,208},{24,216},{32,224},{40,232},{48,240},{56,2... | collective-permute-start | bytes 196616 | tf_op jit(solution)/shard_map/ppermute | solution.py:426
  29.1 0.3 collective-permute-start.6
  29.5 0.3 collective-permute-start.5
  29.8 1.0 %fore_near.1.refs_0_ = f32[256,1024]{1,0:T(8,128)S(1)} custom-call(bf16[256,1024]{1,0:T(8,128)(2,1)S(1)} %get-tuple-element.75.refs_0_, bf16[512,512]{1,0:T(8,128)(2,1)S(1)} %get-tuple-element.72.refs_10_.refs_2_.refs_1_.refs_8_.refs_3_.refs_11_, bf16[256,512]{1,0:T(8,128)(2,1)S(1)} %get-tuple-element.73.refs_11_.refs_3_.refs_2_.refs_9_.refs_5_.refs_12_, ...), custom_call_target="tpu_custom_call" | custom-call | tf_op jit(solution)/shard_map/fore_near/pallas_call | solution.py:560
  30.7 0.0 collective-permute-done.7.refs_5_
  30.8 3.0 %collective-permute-done.6.refs_4_ = bf16[32,1024]{1,0:T(8,128)(2,1)S(1)} collective-permute-done((bf16[32,1024]{1,0:T(8,128)(2,1)S(1)}, bf16[32,1024]{1,0:T(8,128)(2,1)S(1)}, u32[]{:S(2)}, u32[]{:S(2)}) %collective-permute-start.6) | collective-permute-done | bytes 65568 | tf_op jit(solution)/shard_map/ppermute | solution.py:426
  33.7 0.0 collective-permute-done.5.refs_3_
  33.7 0.1 scan8.1.refs_1_
  33.8 2.5 %back_long.1 = (f32[256,1024]{1,0:T(8,128)S(1)}, bf16[256,1024]{1,0:T(8,128)(2,1)S(1)}, bf16[512,1024]{1,0:T(8,128)(2,1)S(1)}, bf16[144,1024]{1,0:T(8,128)(2,1)S(1)}) custom-call(f32[256,1024]{1,0:T(8,128)S(1)} %back_near.1.refs_0_, f32[32,1024]{1,0:T(8,128)S(1)} %scan8.1.refs_1_, f32[16,512]{1,0:T(8,128)S(1)} %copy-done, f32[16,512]{1,0:T(8,128)S(1)} %copy-done.1, ...), custom_call_target="tpu_custom_call" | custom-call | tf_op jit(solution)/shard_map/back_long/pallas_call | solution.py:560
  36.4 4.8 %collective-permute-start.8 = (bf16[144,1024]{1,0:T(8,128)(2,1)S(1)}, bf16[144,1024]{1,0:T(8,128)(2,1)S(1)}, u32[]{:S(2)}, u32[]{:S(2)}) collective-permute-start(bf16[144,1024]{1,0:T(8,128)(2,1)S(1)} %get-tuple-element.95), channel_id=1, source_target_pairs={{8,0},{16,8},{24,16},{32,24},{40,32},{48,40},{56,48},{64,56},{72,6... | collective-permute-start | bytes 884744 | tf_op jit(solution)/shard_map/ppermute | solution.py:432
  41.2 2.4 %fore_long.1 = (bf16[256,1024]{1,0:T(8,128)(2,1)}, bf16[256,1024]{1,0:T(8,128)(2,1)}) custom-call(f32[256,1024]{1,0:T(8,128)S(1)} %fore_near.1.refs_0_, f32[32,1024]{1,0:T(8,128)S(1)} %scan8.1.refs_1_, f32[16,512]{1,0:T(8,128)S(1)} %copy-done, f32[16,512]{1,0:T(8,128)S(1)} %copy-done.1, bf16[256,1024]{1,0:T(8,128)(2,1)S(1)} %get-tuple-element.71.refs_1_.refs_4_, ...), custom_call_target="tpu_custom_call" | custom-call | tf_op jit(solution)/shard_map/fore_long/pallas_call | solution.py:560
  43.6 1.2 %medium_terms.1.refs_10_ = f32[128,512]{1,0:T(8,128)S(1)} custom-call(bf16[256,1024]{1,0:T(8,128)(2,1)S(1)} %get-tuple-element.98.refs_0_, bf16[256,1024]{1,0:T(8,128)(2,1)S(1)} %get-tuple-element.99.refs_1_, bf16[144,1024]{1,0:T(8,128)(2,1)S(1)} %collective-permute-done.refs_6_.refs_2_.refs_8_, ...), custom_call_target="tpu_custom_call" | custom-call | tf_op jit(solution)/shard_map/medium_terms/pallas_call | solution.py:560
  44.8 1.6 %back_rest.1 = (bf16[256,1024]{1,0:T(8,128)(2,1)}, bf16[256,1024]{1,0:T(8,128)(2,1)}, f32[256,1024]{1,0:T(8,128)S(1)}) custom-call(f32[256,1024]{1,0:T(8,128)S(1)} %get-tuple-element.90.refs_0_, bf16[512,1024]{1,0:T(8,128)(2,1)S(1)} %get-tuple-element.91.refs_1_, bf16[256,1024]{1,0:T(8,128)(2,1)S(1)} %get-tuple-element.92.refs_2_, ...), custom_call_target="tpu_custom_call" | custom-call | tf_op jit(solution)/shard_map/back_rest/pallas_call | solution.py:560
  46.5 0.0 collective-permute-done.8.refs_1_
  46.5 4.5 %back_short.1 = (bf16[256,1024]{1,0:T(8,128)(2,1)}, bf16[256,1024]{1,0:T(8,128)(2,1)}, bf16[256,1024]{1,0:T(8,128)(2,1)}, bf16[256,1024]{1,0:T(8,128)(2,1)}, bf16[32,8,384]{2,1,0:T(8,128)(2,1)S(1)}) custom-call(f32[256,1024]{1,0:T(8,128)S(1)} %get-tuple-element.94.refs_0_, bf16[144,1024]{1,0:T(8,128)(2,1)S(1)} %collective-permute-done.8.refs_1_, ...), custom_call_target="tpu_custom_call" | custom-call | tf_op jit(solution)/shard_map/back_short/pallas_call | solution.py:560
  51.0 13.2 %all_to_all.15.refs_0_ = bf16[32,8,384]{2,1,0:T(8,128)(2,1)S(1)} all-to-all(bf16[32,8,384]{2,1,0:T(8,128)(2,1)S(1)} %get-tuple-element.109), channel_id=1, replica_groups=mesh['ctx'=32,'tp'=8] {'ctx'}, dimensions={0} | all-to-all | bytes 393216 | tf_op jit(solution)/shard_map/all_to_all | solution.py:436
  64.3 14.9 %all_to_all.16.refs_0_ = bf16[8,8,256]{2,1,0:T(8,128)(2,1)S(1)} all-to-all(bf16[8,8,256]{2,1,0:T(8,128)(2,1)S(1)} %get-tuple-element.110), channel_id=1, replica_groups=mesh['ctx'=32,'tp'=8] {'tp'}, dimensions={0} | all-to-all | bytes 65536 | tf_op jit(solution)/shard_map/all_to_all | solution.py:436
  79.2 13.3 %all_to_all.17.refs_0_ = bf16[32,8,384]{2,1,0:T(8,128)(2,1)S(1)} all-to-all(bf16[32,8,384]{2,1,0:T(8,128)(2,1)S(1)} %second_sum.1), channel_id=1, replica_groups=mesh['ctx'=32,'tp'=8] {'ctx'}, dimensions={0} | all-to-all | bytes 393216 | tf_op jit(solution)/shard_map/all_to_all | solution.py:436
  92.5 0.7 collect.1
  (2 shorter events, 0.1 us)
Async XLA Ops:
  0.6 6.7 %copy-start.2 = (bf16[128,512]{1,0:T(8,128)(2,1)S(1)}, bf16[128,512]{1,0:T(8,128)(2,1)}, u32[]{:S(2)}) copy-start(bf16[128,512]{1,0:T(8,128)(2,1)} %refs_1_.7) | copy-start | bytes 393220
  2.9 7.2 %copy-start = (f32[16,512]{1,0:T(8,128)S(1)}, f32[16,512]{1,0:T(8,128)}, u32[]{:S(2)}) copy-start(f32[16,512]{1,0:T(8,128)} %refs_2_.9) | copy-start | bytes 98308
  2.9 8.7 %collective-permute-start = (bf16[144,1024]{1,0:T(8,128)(2,1)S(1)}, bf16[144,1024]{1,0:T(8,128)(2,1)S(1)}, u32[]{:S(2)}, u32[]{:S(2)}) collective-permute-start(bf16[144,1024]{1,0:T(8,128)(2,1)S(1)} %get-tuple-element.68), channel_id=1, source_target_pairs={{0,8},{8,16},{16,24},{24,32},{32,40},{40,48},{48,56},{56,64},{64,7... | collective-permute-start | bytes 884744 | tf_op jit(solution)/shard_map/ppermute | solution.py:432
  11.6 9.4 %copy-start.1 = (f32[16,512]{1,0:T(8,128)S(1)}, f32[16,512]{1,0:T(8,128)}, u32[]{:S(2)}) copy-start(f32[16,512]{1,0:T(8,128)} %refs_3_.6) | copy-start | bytes 98308
  15.9 1.3 %collective-permute-start.1 = (bf16[32,1024]{1,0:T(8,128)(2,1)S(1)}, bf16[32,1024]{1,0:T(8,128)(2,1)S(1)}, u32[]{:S(2)}, u32[]{:S(2)}) collective-permute-start(bf16[32,1024]{1,0:T(8,128)(2,1)S(1)} %get-tuple-element.78), channel_id=1, source_target_pairs={{0,8},{8,0},{16,24},{24,16},{32,40},{40,32},{48,56},{56,48},{64,72... | collective-permute-start | bytes 196616 | tf_op jit(solution)/shard_map/ppermute | solution.py:426
  17.3 6.4 %collective-permute-start.4 = (bf16[32,1024]{1,0:T(8,128)(2,1)S(1)}, bf16[32,1024]{1,0:T(8,128)(2,1)S(1)}, u32[]{:S(2)}, u32[]{:S(2)}) collective-permute-start(bf16[32,1024]{1,0:T(8,128)(2,1)S(1)} %get-tuple-element.79), channel_id=1, source_target_pairs={{0,48},{8,56},{16,32},{24,40},{32,16},{40,24},{48,0},{56,8},{64,11... | collective-permute-start | bytes 196616 | tf_op jit(solution)/shard_map/ppermute | solution.py:426
  20.3 4.6 %collective-permute-start.3 = (bf16[32,1024]{1,0:T(8,128)(2,1)S(1)}, bf16[32,1024]{1,0:T(8,128)(2,1)S(1)}, u32[]{:S(2)}, u32[]{:S(2)}) collective-permute-start(bf16[32,1024]{1,0:T(8,128)(2,1)S(1)} %get-tuple-element.79), channel_id=1, source_target_pairs={{0,32},{8,40},{16,48},{24,56},{32,0},{40,8},{48,16},{56,24},{64,96... | collective-permute-start | bytes 196616 | tf_op jit(solution)/shard_map/ppermute | solution.py:426
  20.8 4.1 %collective-permute-start.2 = (bf16[32,1024]{1,0:T(8,128)(2,1)S(1)}, bf16[32,1024]{1,0:T(8,128)(2,1)S(1)}, u32[]{:S(2)}, u32[]{:S(2)}) collective-permute-start(bf16[32,1024]{1,0:T(8,128)(2,1)S(1)} %get-tuple-element.79), channel_id=1, source_target_pairs={{0,16},{8,24},{16,0},{24,8},{32,48},{40,56},{48,32},{56,40},{64,80... | collective-permute-start | bytes 196616 | tf_op jit(solution)/shard_map/ppermute | solution.py:426
  25.1 5.7 %collective-permute-start.7 = (bf16[32,1024]{1,0:T(8,128)(2,1)S(1)}, bf16[32,1024]{1,0:T(8,128)(2,1)S(1)}, u32[]{:S(2)}, u32[]{:S(2)}) collective-permute-start(bf16[32,1024]{1,0:T(8,128)(2,1)S(1)} %get-tuple-element.84), channel_id=1, source_target_pairs={{0,192},{8,200},{16,208},{24,216},{32,224},{40,232},{48,240},{56,2... | collective-permute-start | bytes 196616 | tf_op jit(solution)/shard_map/ppermute | solution.py:426
  29.1 4.6 %collective-permute-start.6 = (bf16[32,1024]{1,0:T(8,128)(2,1)S(1)}, bf16[32,1024]{1,0:T(8,128)(2,1)S(1)}, u32[]{:S(2)}, u32[]{:S(2)}) collective-permute-start(bf16[32,1024]{1,0:T(8,128)(2,1)S(1)} %get-tuple-element.84), channel_id=1, source_target_pairs={{0,128},{8,136},{16,144},{24,152},{32,160},{40,168},{48,176},{56,1... | collective-permute-start | bytes 196616 | tf_op jit(solution)/shard_map/ppermute | solution.py:426
  29.5 4.3 %collective-permute-start.5 = (bf16[32,1024]{1,0:T(8,128)(2,1)S(1)}, bf16[32,1024]{1,0:T(8,128)(2,1)S(1)}, u32[]{:S(2)}, u32[]{:S(2)}) collective-permute-start(bf16[32,1024]{1,0:T(8,128)(2,1)S(1)} %get-tuple-element.84), channel_id=1, source_target_pairs={{0,64},{8,72},{16,80},{24,88},{32,96},{40,104},{48,112},{56,120},{... | collective-permute-start | bytes 196616 | tf_op jit(solution)/shard_map/ppermute | solution.py:426
  36.4 10.1 %collective-permute-start.8 = (bf16[144,1024]{1,0:T(8,128)(2,1)S(1)}, bf16[144,1024]{1,0:T(8,128)(2,1)S(1)}, u32[]{:S(2)}, u32[]{:S(2)}) collective-permute-start(bf16[144,1024]{1,0:T(8,128)(2,1)S(1)} %get-tuple-element.95), channel_id=1, source_target_pairs={{8,0},{16,8},{24,16},{32,24},{40,32},{48,40},{56,48},{64,56},{72,6... | collective-permute-start | bytes 884744 | tf_op jit(solution)/shard_map/ppermute | solution.py:432

commit v4 on v3

--- a/solution.py
+++ b/solution.py
@@ -185,23 +185,37 @@
         near_ref[:, lanes] = dot(inv_ref[...], spec_conj(spec, filt_of(long_ref, own)))
 
 
+def fore_start_kernel(value_ref, k1_ref, q1_ref, k2_ref, filt_ref, z1_ref, x1_ref, u2_ref, ext):
+    count, width = value_ref.shape
+    for lanes, _ in parts(width, width, WIDE):
+        ext[:, lanes] = mul(k1_ref[:, lanes], value_ref[:, lanes]).astype(BF).astype(F32)
+        z1 = short_causal(ext, filt_ref, count - 16, 16, lanes)
+        z1_ref[16:, lanes] = z1.astype(BF)
+        x1 = mul(q1_ref[16:, lanes], z1).astype(BF)
+        x1_ref[16:, lanes] = x1
+        u2_ref[16:, lanes] = mul(k2_ref[16:, lanes], x1).astype(BF)
+
+
 def fore_kernel(
     value_ref, k1_ref, q1_ref, k2_ref, q2_ref, k3_ref, rim_ref, filt_ref, rates_ref, back_ref,
-    fwd_ref, inv_ref, med_ref,
+    z1_in, x1_in, u2_in, fwd_ref, inv_ref, med_ref,
     z1_ref, x1_ref, u2_ref, z2_ref, x2_ref, u3_ref, carry_ref, send_ref, ext, signal,
 ):
     count, width = value_ref.shape
     modes, groups = rates_ref.shape
     rim = rim_ref.shape[0] - 16
     for lanes, own in parts(width, groups, WIDE):
-        u1 = mul(k1_ref[:, lanes], value_ref[:, lanes]).astype(BF)
+        u1 = mul(k1_ref[0:16, lanes], value_ref[0:16, lanes]).astype(BF)
         ext[0:16, lanes] = rim_ref[rim : rim + 16, lanes].astype(F32)
-        ext[16:, lanes] = u1.astype(F32)
-        z1 = short_causal(ext, filt_ref, count, 16, lanes)
-        z1_ref[:, lanes] = z1.astype(BF)
-        x1 = mul(q1_ref[:, lanes], z1).astype(BF)
-        x1_ref[:, lanes] = x1
-        u2 = mul(k2_ref[:, lanes], x1).astype(BF)
+        ext[16:32, lanes] = u1.astype(F32)
+        z1 = short_causal(ext, filt_ref, 16, 16, lanes)
+        z1_ref[0:16, lanes] = z1.astype(BF)
+        z1_ref[16:, lanes] = z1_in[16:, lanes]
+        x1 = mul(q1_ref[0:16, lanes], z1).astype(BF)
+        x1_ref[0:16, lanes] = x1
+        x1_ref[16:, lanes] = x1_in[16:, lanes]
+        u2 = mul(k2_ref[0:16, lanes], x1).astype(BF)
+        u2 = jnp.concatenate([u2, u2_in[16:, lanes]], axis=0)
         u2_ref[:, lanes] = u2
         spec = dot(fwd_ref[:, :count], u2)
         spec = spec + dot(fwd_ref[:, 2 * count - rim :], rim_ref[0:rim, lanes])
@@ -643,12 +657,15 @@
         grad_out, gate_q3, rates
     )
 
+    begun = call(fore_start_kernel, "fore_start", [kept] * 3, (count, width))(
+        value, gate_k1, gate_q1, gate_k2, short_filter
+    )
     got = call(
         fore_kernel, "fore",
         [kept] * 6 + [shape(2 * modes, width, F32), shape(2 * modes, width)],
-        ext_full, (count, width),
+        (32, width), (count, width),
     )(value, gate_k1, gate_q1, gate_k2, gate_q2, gate_k3, rim_fore, short_filter, rates, back_carry,
-      fwd, inv, med)
+      *hold(begun), fwd, inv, med)
     z1, x1, u2, z2, x2, u3 = hold(got[:6])
     carry, send = got[6:]
 

time: 93.5 us -> 93.2 us (level)
  starting transfers between devices: 17.9 us -> 16.3 us
    ppermute x7, starting transfers between devices: 8.51 us -> 6.99 us  [swapped(): return lax.ppermute(block, 'ctx', [(i, i ^ distance) for i in range(size)])]
    pallas_call x18 -> x19, Pallas kernels: 27.7 us -> 28.5 us  [run(): pl.pallas_call(body, name=name, in_specs=[place(a, k) for k, a in enumera...]
  transfers between devices with their start and end apart: 9 -> 9, of which waited for: 3 -> 4; matrix products, arithmetic and copies ran while one was open for 0% -> 0% of each run, Pallas kernels for 14% -> 16%
where the time goes in v4:
time: 93.2 us; the launch traced here: 92.9 us
  blocking collectives  41.9 us (45%)
  Pallas kernels  28.5 us (31%)
  starting transfers between devices  16.3 us (17%)
  waiting for transfers between devices  5.26 us (6%)
    all_to_all x3, blocking collectives, exchanged(): return lax.all_to_all(block, axis, 0, 0)  41.9 us
    pallas_call x19, Pallas kernels, run(): pl.pallas_call(body, name=name, in_specs=[place(a, k) for k, a in enumera...  28.5 us
    ppermute x2, starting transfers between devices, shifted(): return lax.ppermute(block, 'ctx', route)  9.33 us
    ppermute x7, starting transfers between devices, swapped(): return lax.ppermute(block, 'ctx', [(i, i ^ distance) for i in range(size)])  6.99 us
    ppermute x7, waiting for transfers between devices, swapped(): return lax.ppermute(block, 'ctx', [(i, i ^ distance) for i in range(size)])  5.25 us
  transfers between devices with their start and end apart: 9, of which 4 were waited for; matrix products, arithmetic and copies ran while one was open for 0% of the time, Pallas kernels for 16%

profile of v4, /device:TPU:1, one launch (start us, length us, event | category | flops | bytes accessed | tf_op | source)
XLA Modules:
  0.0 92.9 jit_solution(15238681373678013252)
XLA Ops:
  0.6 0.0 copy-start.2
  0.7 2.2 %fore_rim.1 = (bf16[144,1024]{1,0:T(8,128)(2,1)S(1)}, bf16[7,1024]{1,0:T(8,128)(2,1)S(1)}, bf16[256,1024]{1,0:T(8,128)(2,1)S(1)}, bf16[256,1024]{1,0:T(8,128)(2,...) custom-call(s32[1]{0:T(128)} %bitcast.refs_0_, bf16[7,1024]{1,0:T(8,128)(2,1)} %refs_1_.6, ...), custom_call_target="tpu_custom_call" | custom-call | tf_op jit(solution)/shard_map/fore_rim/pallas_call | solution.py:574
  2.9 0.0 copy-start
  2.9 4.5 %collective-permute-start = (bf16[144,1024]{1,0:T(8,128)(2,1)S(1)}, bf16[144,1024]{1,0:T(8,128)(2,1)S(1)}, u32[]{:S(2)}, u32[]{:S(2)}) collective-permute-start(bf16[144,1024]{1,0:T(8,128)(2,1)S(1)} %get-tuple-element.71), channel_id=1, source_target_pairs={{0,8},{8,16},{16,24},{24,32},{32,40},{40,48},{48,56},{56,64},{64,7... | collective-permute-start | bytes 884744 | tf_op jit(solution)/shard_map/ppermute | solution.py:446
  7.4 0.0 copy-done.2
  7.4 2.7 %medium_filter.1 = (f32[3,256,512]{2,1,0:T(8,128)S(1)}, f32[512,256]{1,0:T(8,128)S(1)}, bf16[512,512]{1,0:T(8,128)(2,1)S(1)}, bf16[256,512]{1,0:T(8,128)(2,1)S(1...) custom-call(f32[512,256]{1,0:T(8,128)} %constant.14.clone.refs_0_, ...), custom_call_target="tpu_custom_call" | custom-call | tf_op jit(solution)/shard_map/medium_filter/pallas_call | solution.py:574
  10.1 0.0 copy-done
  10.1 1.5 %back_carry.1.refs_9_ = f32[16,1024]{1,0:T(8,128)S(1)} custom-call(bf16[256,1024]{1,0:T(8,128)(2,1)S(1)} %get-tuple-element.73.refs_0_.refs_5_, bf16[256,1024]{1,0:T(8,128)(2,1)S(1)} %get-tuple-element.74.refs_1_.refs_4_, f32[16,512]{1,0:T(8,128)S(1)} %copy-done), custom_call_target="tpu_custom_call" | custom-call | tf_op jit(solution)/shard_map/back_carry/pallas_call | solution.py:574
  11.6 2.0 %fore_start.1 = (bf16[256,1024]{1,0:T(8,128)(2,1)S(1)}, bf16[256,1024]{1,0:T(8,128)(2,1)S(1)}, bf16[256,1024]{1,0:T(8,128)(2,1)S(1)}) custom-call(bf16[256,1024]{1,0:T(8,128)(2,1)S(1)} %get-tuple-element.65.refs_0_.refs_7_, bf16[256,1024]{1,0:T(8,128)(2,1)S(1)} %get-tuple-element.66.refs_1_.refs_6_, ...), custom_call_target="tpu_custom_call" | custom-call | tf_op jit(solution)/shard_map/fore_start/pallas_call | solution.py:574
  13.6 0.0 collective-permute-done.refs_6_.refs_2_.refs_8_
  13.6 0.0 copy-start.1
  13.6 3.0 %fore.1 = (bf16[256,1024]{1,0:T(8,128)(2,1)S(1)}, bf16[256,1024]{1,0:T(8,128)(2,1)S(1)}, bf16[256,1024]{1,0:T(8,128)(2,1)S(1)}, bf16[256,1024]{1,0:T(8,128)(2,1)...) custom-call(bf16[256,1024]{1,0:T(8,128)(2,1)S(1)} %get-tuple-element, ...), custom_call_target="tpu_custom_call" | custom-call | tf_op jit(solution)/shard_map/fore/pallas_call | solution.py:574
  16.7 0.1 collective-permute-start.1
  16.8 1.2 %collective-permute-done.1.refs_3_ = bf16[32,1024]{1,0:T(8,128)(2,1)S(1)} collective-permute-done((bf16[32,1024]{1,0:T(8,128)(2,1)S(1)}, bf16[32,1024]{1,0:T(8,128)(2,1)S(1)}, u32[]{:S(2)}, u32[]{:S(2)}) %collective-permute-start.1) | collective-permute-done | bytes 65568 | tf_op jit(solution)/shard_map/ppermute | solution.py:440
  18.0 0.1 scan1.1
  18.1 2.6 %collective-permute-start.4 = (bf16[32,1024]{1,0:T(8,128)(2,1)S(1)}, bf16[32,1024]{1,0:T(8,128)(2,1)S(1)}, u32[]{:S(2)}, u32[]{:S(2)}) collective-permute-start(bf16[32,1024]{1,0:T(8,128)(2,1)S(1)} %get-tuple-element.85), channel_id=1, source_target_pairs={{0,48},{8,56},{16,32},{24,40},{32,16},{40,24},{48,0},{56,8},{64,11... | collective-permute-start | bytes 196616 | tf_op jit(solution)/shard_map/ppermute | solution.py:440
  20.7 0.5 collective-permute-start.3
  21.2 0.2 collective-permute-start.2
  21.4 0.0 copy-done.1
  21.4 1.7 %long_filter.1.refs_4_.refs_3_ = f32[3,256,512]{2,1,0:T(8,128)S(1)} custom-call(f32[512,256]{1,0:T(8,128)S(1)} %get-tuple-element.82.refs_0_, f32[16,512]{1,0:T(8,128)S(1)} %copy-done.1, f32[16,512]{1,0:T(8,128)S(1)} %copy-done), custom_call_target="tpu_custom_call" | custom-call | tf_op jit(solution)/shard_map/long_filter/pallas_call | solution.py:574
  23.2 1.0 %back_near.1.refs_0_ = f32[256,1024]{1,0:T(8,128)S(1)} custom-call(bf16[256,1024]{1,0:T(8,128)(2,1)S(1)} %get-tuple-element.73.refs_0_.refs_5_, bf16[256,1024]{1,0:T(8,128)(2,1)S(1)} %get-tuple-element.74.refs_1_.refs_4_, bf16[512,512]{1,0:T(8,128)(2,1)S(1)} %get-tuple-element.78.refs_13_.refs_2_.refs_1_.refs_8_.refs_3_.refs_11_, ...), custom_call_target="tpu_custom_call" | custom-call | tf_op jit(solution)/shard_map/back_near/pallas_call | solution.py:574
  24.1 0.0 collective-permute-done.4.refs_5_
  24.1 1.1 %collective-permute-done.3.refs_4_ = bf16[32,1024]{1,0:T(8,128)(2,1)S(1)} collective-permute-done((bf16[32,1024]{1,0:T(8,128)(2,1)S(1)}, bf16[32,1024]{1,0:T(8,128)(2,1)S(1)}, u32[]{:S(2)}, u32[]{:S(2)}) %collective-permute-start.3) | collective-permute-done | bytes 65568 | tf_op jit(solution)/shard_map/ppermute | solution.py:440
  25.3 0.0 collective-permute-done.2.refs_3_
  25.3 0.2 scan2.1
  25.5 2.6 %collective-permute-start.7 = (bf16[32,1024]{1,0:T(8,128)(2,1)S(1)}, bf16[32,1024]{1,0:T(8,128)(2,1)S(1)}, u32[]{:S(2)}, u32[]{:S(2)}) collective-permute-start(bf16[32,1024]{1,0:T(8,128)(2,1)S(1)} %get-tuple-element.90), channel_id=1, source_target_pairs={{0,192},{8,200},{16,208},{24,216},{32,224},{40,232},{48,240},{56,2... | collective-permute-start | bytes 196616 | tf_op jit(solution)/shard_map/ppermute | solution.py:440
  28.1 0.7 collective-permute-start.6
  28.8 0.2 collective-permute-start.5
  29.0 0.9 %fore_near.1.refs_0_ = f32[256,1024]{1,0:T(8,128)S(1)} custom-call(bf16[256,1024]{1,0:T(8,128)(2,1)S(1)} %get-tuple-element.81.refs_0_, bf16[512,512]{1,0:T(8,128)(2,1)S(1)} %get-tuple-element.78.refs_13_.refs_2_.refs_1_.refs_8_.refs_3_.refs_11_, bf16[256,512]{1,0:T(8,128)(2,1)S(1)} %get-tuple-element.79.refs_14_.refs_3_.refs_2_.refs_9_.refs_5_.refs_12_, ...), custom_call_target="tpu_custom_call" | custom-call | tf_op jit(solution)/shard_map/fore_near/pallas_call | solution.py:574
  29.9 0.1 collective-permute-done.7.refs_5_
  30.1 2.8 %collective-permute-done.6.refs_4_ = bf16[32,1024]{1,0:T(8,128)(2,1)S(1)} collective-permute-done((bf16[32,1024]{1,0:T(8,128)(2,1)S(1)}, bf16[32,1024]{1,0:T(8,128)(2,1)S(1)}, u32[]{:S(2)}, u32[]{:S(2)}) %collective-permute-start.6) | collective-permute-done | bytes 65568 | tf_op jit(solution)/shard_map/ppermute | solution.py:440
  32.8 0.0 collective-permute-done.5.refs_3_
  32.8 0.1 scan8.1.refs_1_
  32.9 2.5 %back_long.1 = (f32[256,1024]{1,0:T(8,128)S(1)}, bf16[256,1024]{1,0:T(8,128)(2,1)S(1)}, bf16[512,1024]{1,0:T(8,128)(2,1)S(1)}, bf16[144,1024]{1,0:T(8,128)(2,1)S(1)}) custom-call(f32[256,1024]{1,0:T(8,128)S(1)} %back_near.1.refs_0_, f32[32,1024]{1,0:T(8,128)S(1)} %scan8.1.refs_1_, f32[16,512]{1,0:T(8,128)S(1)} %copy-done, f32[16,512]{1,0:T(8,128)S(1)} %copy-done.1, ...), custom_call_target="tpu_custom_call" | custom-call | tf_op jit(solution)/shard_map/back_long/pallas_call | solution.py:574
  35.5 4.8 %collective-permute-start.8 = (bf16[144,1024]{1,0:T(8,128)(2,1)S(1)}, bf16[144,1024]{1,0:T(8,128)(2,1)S(1)}, u32[]{:S(2)}, u32[]{:S(2)}) collective-permute-start(bf16[144,1024]{1,0:T(8,128)(2,1)S(1)} %get-tuple-element.101), channel_id=1, source_target_pairs={{8,0},{16,8},{24,16},{32,24},{40,32},{48,40},{56,48},{64,56},{72,6... | collective-permute-start | bytes 884744 | tf_op jit(solution)/shard_map/ppermute | solution.py:446
  40.3 2.5 %fore_long.1 = (bf16[256,1024]{1,0:T(8,128)(2,1)}, bf16[256,1024]{1,0:T(8,128)(2,1)}) custom-call(f32[256,1024]{1,0:T(8,128)S(1)} %fore_near.1.refs_0_, f32[32,1024]{1,0:T(8,128)S(1)} %scan8.1.refs_1_, f32[16,512]{1,0:T(8,128)S(1)} %copy-done, f32[16,512]{1,0:T(8,128)S(1)} %copy-done.1, bf16[256,1024]{1,0:T(8,128)(2,1)S(1)} %get-tuple-element.74.refs_1_.refs_4_, ...), custom_call_target="tpu_custom_call" | custom-call | tf_op jit(solution)/shard_map/fore_long/pallas_call | solution.py:574
  42.7 1.2 %medium_terms.1.refs_10_ = f32[128,512]{1,0:T(8,128)S(1)} custom-call(bf16[256,1024]{1,0:T(8,128)(2,1)S(1)} %get-tuple-element.104.refs_0_, bf16[256,1024]{1,0:T(8,128)(2,1)S(1)} %get-tuple-element.105.refs_1_, bf16[144,1024]{1,0:T(8,128)(2,1)S(1)} %collective-permute-done.refs_6_.refs_2_.refs_8_, ...), custom_call_target="tpu_custom_call" | custom-call | tf_op jit(solution)/shard_map/medium_terms/pallas_call | solution.py:574
  43.9 1.6 %back_rest.1 = (bf16[256,1024]{1,0:T(8,128)(2,1)}, bf16[256,1024]{1,0:T(8,128)(2,1)}, f32[256,1024]{1,0:T(8,128)S(1)}) custom-call(f32[256,1024]{1,0:T(8,128)S(1)} %get-tuple-element.96.refs_0_, bf16[512,1024]{1,0:T(8,128)(2,1)S(1)} %get-tuple-element.97.refs_1_, bf16[256,1024]{1,0:T(8,128)(2,1)S(1)} %get-tuple-element.98.refs_2_, ...), custom_call_target="tpu_custom_call" | custom-call | tf_op jit(solution)/shard_map/back_rest/pallas_call | solution.py:574
  45.6 0.0 collective-permute-done.8.refs_1_
  45.6 4.5 %back_short.1 = (bf16[256,1024]{1,0:T(8,128)(2,1)}, bf16[256,1024]{1,0:T(8,128)(2,1)}, bf16[256,1024]{1,0:T(8,128)(2,1)}, bf16[256,1024]{1,0:T(8,128)(2,1)}, bf16[32,8,384]{2,1,0:T(8,128)(2,1)S(1)}) custom-call(f32[256,1024]{1,0:T(8,128)S(1)} %get-tuple-element.100.refs_0_, bf16[144,1024]{1,0:T(8,128)(2,1)S(1)} %collective-permute-done.8.refs_1_, ...), custom_call_target="tpu_custom_call" | custom-call | tf_op jit(solution)/shard_map/back_short/pallas_call | solution.py:574
  50.1 13.8 %all_to_all.15.refs_0_ = bf16[32,8,384]{2,1,0:T(8,128)(2,1)S(1)} all-to-all(bf16[32,8,384]{2,1,0:T(8,128)(2,1)S(1)} %get-tuple-element.115), channel_id=1, replica_groups=mesh['ctx'=32,'tp'=8] {'ctx'}, dimensions={0} | all-to-all | bytes 393216 | tf_op jit(solution)/shard_map/all_to_all | solution.py:450
  63.9 14.8 %all_to_all.16.refs_0_ = bf16[8,8,256]{2,1,0:T(8,128)(2,1)S(1)} all-to-all(bf16[8,8,256]{2,1,0:T(8,128)(2,1)S(1)} %get-tuple-element.116), channel_id=1, replica_groups=mesh['ctx'=32,'tp'=8] {'tp'}, dimensions={0} | all-to-all | bytes 65536 | tf_op jit(solution)/shard_map/all_to_all | solution.py:450
  78.8 13.3 %all_to_all.17.refs_0_ = bf16[32,8,384]{2,1,0:T(8,128)(2,1)S(1)} all-to-all(bf16[32,8,384]{2,1,0:T(8,128)(2,1)S(1)} %second_sum.1), channel_id=1, replica_groups=mesh['ctx'=32,'tp'=8] {'ctx'}, dimensions={0} | all-to-all | bytes 393216 | tf_op jit(solution)/shard_map/all_to_all | solution.py:450
  92.1 0.7 collect.1
  (2 shorter events, 0.1 us)
Async XLA Ops:
  0.6 6.7 %copy-start.2 = (bf16[128,512]{1,0:T(8,128)(2,1)S(1)}, bf16[128,512]{1,0:T(8,128)(2,1)}, u32[]{:S(2)}) copy-start(bf16[128,512]{1,0:T(8,128)(2,1)} %refs_1_.7) | copy-start | bytes 393220
  2.9 7.2 %copy-start = (f32[16,512]{1,0:T(8,128)S(1)}, f32[16,512]{1,0:T(8,128)}, u32[]{:S(2)}) copy-start(f32[16,512]{1,0:T(8,128)} %refs_2_.9) | copy-start | bytes 98308
  2.9 10.8 %collective-permute-start = (bf16[144,1024]{1,0:T(8,128)(2,1)S(1)}, bf16[144,1024]{1,0:T(8,128)(2,1)S(1)}, u32[]{:S(2)}, u32[]{:S(2)}) collective-permute-start(bf16[144,1024]{1,0:T(8,128)(2,1)S(1)} %get-tuple-element.71), channel_id=1, source_target_pairs={{0,8},{8,16},{16,24},{24,32},{32,40},{40,48},{48,56},{56,64},{64,7... | collective-permute-start | bytes 884744 | tf_op jit(solution)/shard_map/ppermute | solution.py:446
  13.6 7.8 %copy-start.1 = (f32[16,512]{1,0:T(8,128)S(1)}, f32[16,512]{1,0:T(8,128)}, u32[]{:S(2)}) copy-start(f32[16,512]{1,0:T(8,128)} %refs_3_.6) | copy-start | bytes 98308
  16.7 1.3 %collective-permute-start.1 = (bf16[32,1024]{1,0:T(8,128)(2,1)S(1)}, bf16[32,1024]{1,0:T(8,128)(2,1)S(1)}, u32[]{:S(2)}, u32[]{:S(2)}) collective-permute-start(bf16[32,1024]{1,0:T(8,128)(2,1)S(1)} %get-tuple-element.84), channel_id=1, source_target_pairs={{0,8},{8,0},{16,24},{24,16},{32,40},{40,32},{48,56},{56,48},{64,72... | collective-permute-start | bytes 196616 | tf_op jit(solution)/shard_map/ppermute | solution.py:440
  18.1 6.0 %collective-permute-start.4 = (bf16[32,1024]{1,0:T(8,128)(2,1)S(1)}, bf16[32,1024]{1,0:T(8,128)(2,1)S(1)}, u32[]{:S(2)}, u32[]{:S(2)}) collective-permute-start(bf16[32,1024]{1,0:T(8,128)(2,1)S(1)} %get-tuple-element.85), channel_id=1, source_target_pairs={{0,48},{8,56},{16,32},{24,40},{32,16},{40,24},{48,0},{56,8},{64,11... | collective-permute-start | bytes 196616 | tf_op jit(solution)/shard_map/ppermute | solution.py:440
  20.7 4.6 %collective-permute-start.3 = (bf16[32,1024]{1,0:T(8,128)(2,1)S(1)}, bf16[32,1024]{1,0:T(8,128)(2,1)S(1)}, u32[]{:S(2)}, u32[]{:S(2)}) collective-permute-start(bf16[32,1024]{1,0:T(8,128)(2,1)S(1)} %get-tuple-element.85), channel_id=1, source_target_pairs={{0,32},{8,40},{16,48},{24,56},{32,0},{40,8},{48,16},{56,24},{64,96... | collective-permute-start | bytes 196616 | tf_op jit(solution)/shard_map/ppermute | solution.py:440
  21.2 4.1 %collective-permute-start.2 = (bf16[32,1024]{1,0:T(8,128)(2,1)S(1)}, bf16[32,1024]{1,0:T(8,128)(2,1)S(1)}, u32[]{:S(2)}, u32[]{:S(2)}) collective-permute-start(bf16[32,1024]{1,0:T(8,128)(2,1)S(1)} %get-tuple-element.85), channel_id=1, source_target_pairs={{0,16},{8,24},{16,0},{24,8},{32,48},{40,56},{48,32},{56,40},{64,80... | collective-permute-start | bytes 196616 | tf_op jit(solution)/shard_map/ppermute | solution.py:440
  25.5 4.6 %collective-permute-start.7 = (bf16[32,1024]{1,0:T(8,128)(2,1)S(1)}, bf16[32,1024]{1,0:T(8,128)(2,1)S(1)}, u32[]{:S(2)}, u32[]{:S(2)}) collective-permute-start(bf16[32,1024]{1,0:T(8,128)(2,1)S(1)} %get-tuple-element.90), channel_id=1, source_target_pairs={{0,192},{8,200},{16,208},{24,216},{32,224},{40,232},{48,240},{56,2... | collective-permute-start | bytes 196616 | tf_op jit(solution)/shard_map/ppermute | solution.py:440
  28.1 4.7 %collective-permute-start.6 = (bf16[32,1024]{1,0:T(8,128)(2,1)S(1)}, bf16[32,1024]{1,0:T(8,128)(2,1)S(1)}, u32[]{:S(2)}, u32[]{:S(2)}) collective-permute-start(bf16[32,1024]{1,0:T(8,128)(2,1)S(1)} %get-tuple-element.90), channel_id=1, source_target_pairs={{0,128},{8,136},{16,144},{24,152},{32,160},{40,168},{48,176},{56,1... | collective-permute-start | bytes 196616 | tf_op jit(solution)/shard_map/ppermute | solution.py:440
  28.8 4.0 %collective-permute-start.5 = (bf16[32,1024]{1,0:T(8,128)(2,1)S(1)}, bf16[32,1024]{1,0:T(8,128)(2,1)S(1)}, u32[]{:S(2)}, u32[]{:S(2)}) collective-permute-start(bf16[32,1024]{1,0:T(8,128)(2,1)S(1)} %get-tuple-element.90), channel_id=1, source_target_pairs={{0,64},{8,72},{16,80},{24,88},{32,96},{40,104},{48,112},{56,120},{... | collective-permute-start | bytes 196616 | tf_op jit(solution)/shard_map/ppermute | solution.py:440
  35.5 10.1 %collective-permute-start.8 = (bf16[144,1024]{1,0:T(8,128)(2,1)S(1)}, bf16[144,1024]{1,0:T(8,128)(2,1)S(1)}, u32[]{:S(2)}, u32[]{:S(2)}) collective-permute-start(bf16[144,1024]{1,0:T(8,128)(2,1)S(1)} %get-tuple-element.101), channel_id=1, source_target_pairs={{8,0},{16,8},{24,16},{32,24},{40,32},{48,40},{56,48},{64,56},{72,6... | collective-permute-start | bytes 884744 | tf_op jit(solution)/shard_map/ppermute | solution.py:446
